TPU v7x, 32 devices: a whole 2x2x4 slice. The times are simulated.
32 devices in a mesh: dp: 4 (over z), wide: 2 (over x), narrow: 4 (over y, core).
Axes of the slice: x: 2, y: 2, z: 4, core: 2. Of those that a mesh axis runs over, the one named last changes fastest.
Arguments:
- tokens: bfloat16 [32768, 1024], P(('dp', 'narrow'), 'wide'), may hold values from -6 to 6
- memory: bfloat16 [32768, 1024], P(('dp', 'narrow'), 'wide'), may hold values from -6 to 6
- dec_segments: int32 [16, 2048], P(('dp', 'narrow')), may hold values from 0 to 3, never falling along the last dimension, each value on 1 to 1024 neighbouring positions
- mem_segments: int32 [16, 2048], P(('dp', 'narrow')), may hold values from 0 to 3, never falling along the last dimension, each value on 1 to 1024 neighbouring positions
- self_qkv: bfloat16 [3, 1024, 1024], P(None, None, 'wide'), may hold values from -0.1875 to 0.1875
- self_out: bfloat16 [1024, 1024], P('wide'), may hold values from -1.5 to 1.5
- cross_q: bfloat16 [1024, 1024], P(None, 'wide'), may hold values from -0.1875 to 0.1875
- cross_kv: bfloat16 [2, 1024, 1024], P(None, None, 'wide'), may hold values from -0.1875 to 0.1875
- cross_out: bfloat16 [1024, 1024], P('wide'), may hold values from -1.5 to 1.5
- ffn_in: bfloat16 [1024, 4096], P(None, 'wide'), may hold values from -0.1875 to 0.1875
- ffn_out: bfloat16 [4096, 1024], P('wide'), may hold values from -0.09375 to 0.09375
- adapter_down: bfloat16 [1024, 512], P(None, 'narrow'), may hold values from -0.1875 to 0.1875
- adapter_up: bfloat16 [512, 1024], P('narrow'), may hold values from -0.125 to 0.125
- self_prefix: bfloat16 [2, 30, 1024], P(None, None, 'wide'), may hold values from -6 to 6
- cross_prefix: bfloat16 [2, 30, 1024], P(None, None, 'wide'), may hold values from -6 to 6
- gains: float32 [3, 1024], replicated, may hold values from 0.1 to 1.9
- cotangent: bfloat16 [32768, 1024], P(('dp', 'narrow'), 'wide'), may hold values from -6 to 6
Outputs:
- output: bfloat16 [32768, 1024], P(('dp', 'narrow'), 'wide')
- grad_tokens: float32 [32768, 1024], P(('dp', 'narrow'), 'wide')
- grad_memory: float32 [32768, 1024], P(('dp', 'narrow'), 'wide')
- grad_self_prefix: float32 [2, 30, 1024], P(None, None, 'wide')
- grad_cross_prefix: float32 [2, 30, 1024], P(None, None, 'wide')
- grad_adapter_down: float32 [1024, 512], P(None, 'narrow')
- grad_adapter_up: float32 [512, 1024], P('narrow')
Inputs may be any that keep to these rules, and one draw needn't show every extreme that they name: `dec_segments`: within each row, document numbers never fall and every number 0 to 3 occurs. `mem_segments`: within each row, document numbers never fall and every number 0 to 3 occurs.
All inputs are finite; a program needn't handle non-finite values.
Results may differ from a plain program's by a relative error of at most 0.025.
Values may be sent and summed in bfloat16 or wider, within the bound.
A program may use at most 320 MiB of HBM per device.

v0:
```python
from functools import partial

import jax
import jax.numpy as jnp
from jax import lax
from jax.sharding import PartitionSpec as P

HEAD_DIM = 64


def layer_norm(features, norm_gain):
    average = jnp.mean(features, axis=-1, keepdims=True)
    centered = features - average
    variance = jnp.mean(centered * centered, axis=-1, keepdims=True)
    return centered * lax.rsqrt(variance + 1e-05) * norm_gain


def norm_grad(gathered, norm_gain, upstream):
    _, pullback = jax.vjp(partial(layer_norm, norm_gain=norm_gain), gathered.astype(jnp.float32))
    return pullback(upstream)[0]


def gelu_grad(pre_values, upstream):
    _, pullback = jax.vjp(partial(jax.nn.gelu, approximate=False), pre_values)
    return pullback(upstream)[0]


def visible(query_segs, key_seg, block_start, causal):
    allowed = query_segs[:, None] == key_seg[None, :]
    if causal:
        positions = block_start + jnp.arange(query_segs.shape[0], dtype=jnp.int32)
        key_places = jnp.arange(key_seg.shape[0], dtype=jnp.int32)
        allowed = jnp.logical_and(allowed, key_places[None, :] <= positions[:, None])
    return allowed


def head_scores(query_heads, key_heads, prefix_keys, score_scale):
    scores = (
        jnp.einsum("qhd,khd->hqk", query_heads, key_heads, preferred_element_type=jnp.float32)
        * score_scale
    )
    prefix_scores = (
        jnp.einsum("qhd,phd->hqp", query_heads, prefix_keys, preferred_element_type=jnp.float32)
        * score_scale
    )
    return (scores, prefix_scores)


def attend_forward(query, keys, values, query_seg, key_seg, prefix, causal):
    length, columns = query.shape
    key_count = keys.shape[0]
    head_count = columns // HEAD_DIM
    block_rows = min(512, length)
    block_count = length // block_rows
    score_scale = HEAD_DIM ** (-0.5)
    key_heads = keys.reshape(key_count, head_count, HEAD_DIM)
    value_heads = values.reshape(key_count, head_count, HEAD_DIM)
    prefix_keys = prefix[0].reshape(-1, head_count, HEAD_DIM)
    prefix_values = prefix[1].reshape(-1, head_count, HEAD_DIM)

    def one_block(pieces):
        query_rows, query_segs, block_start = pieces
        query_heads = query_rows.reshape(block_rows, head_count, HEAD_DIM)
        scores, prefix_scores = head_scores(query_heads, key_heads, prefix_keys, score_scale)
        scores = jnp.where(visible(query_segs, key_seg, block_start, causal)[None], scores, -1e30)
        largest = jnp.maximum(jnp.max(scores, axis=-1), jnp.max(prefix_scores, axis=-1))
        denominator = jnp.sum(jnp.exp(scores - largest[..., None]), axis=-1) + jnp.sum(
            jnp.exp(prefix_scores - largest[..., None]), axis=-1
        )
        log_total = largest + jnp.log(denominator)
        chances = jnp.exp(scores - log_total[..., None]).astype(jnp.bfloat16)
        prefix_chances = jnp.exp(prefix_scores - log_total[..., None]).astype(jnp.bfloat16)
        attended = jnp.einsum(
            "hqk,khd->qhd", chances, value_heads, preferred_element_type=jnp.float32
        )
        attended = attended + jnp.einsum(
            "hqp,phd->qhd", prefix_chances, prefix_values, preferred_element_type=jnp.float32
        )
        return (attended.reshape(block_rows, columns).astype(jnp.bfloat16), log_total)

    starts = jnp.arange(block_count, dtype=jnp.int32) * block_rows
    blocks, log_totals = lax.map(
        one_block,
        (
            query.reshape(block_count, block_rows, columns),
            query_seg.reshape(block_count, block_rows),
            starts,
        ),
    )
    return (blocks.reshape(length, columns), log_totals)


def attend_backward(query, keys, values, query_seg, key_seg, log_totals, grad_out, prefix, causal):
    length, columns = query.shape
    key_count = keys.shape[0]
    head_count = columns // HEAD_DIM
    block_rows = min(512, length)
    block_count = length // block_rows
    score_scale = HEAD_DIM ** (-0.5)
    key_heads = keys.reshape(key_count, head_count, HEAD_DIM)
    value_heads = values.reshape(key_count, head_count, HEAD_DIM)
    prefix_keys = prefix[0].reshape(-1, head_count, HEAD_DIM)
    prefix_values = prefix[1].reshape(-1, head_count, HEAD_DIM)

    def one_block(totals, pieces):
        grad_keys, grad_values, grad_pkeys, grad_pvalues = totals
        query_rows, query_segs, block_start, log_total, grad_block = pieces
        query_heads = query_rows.reshape(block_rows, head_count, HEAD_DIM)
        grad_heads = grad_block.reshape(block_rows, head_count, HEAD_DIM)
        scores, prefix_scores = head_scores(query_heads, key_heads, prefix_keys, score_scale)
        scores = jnp.where(visible(query_segs, key_seg, block_start, causal)[None], scores, -1e30)
        chances = jnp.exp(scores - log_total[..., None])
        prefix_chances = jnp.exp(prefix_scores - log_total[..., None])
        grad_values = grad_values + jnp.einsum(
            "hqk,qhd->khd",
            chances.astype(jnp.bfloat16),
            grad_heads,
            preferred_element_type=jnp.float32,
        )
        grad_pvalues = grad_pvalues + jnp.einsum(
            "hqp,qhd->phd",
            prefix_chances.astype(jnp.bfloat16),
            grad_heads,
            preferred_element_type=jnp.float32,
        )
        grad_chances = jnp.einsum(
            "qhd,khd->hqk", grad_heads, value_heads, preferred_element_type=jnp.float32
        )
        grad_pchances = jnp.einsum(
            "qhd,phd->hqp", grad_heads, prefix_values, preferred_element_type=jnp.float32
        )
        inner_sum = jnp.sum(chances * grad_chances, axis=-1) + jnp.sum(
            prefix_chances * grad_pchances, axis=-1
        )
        grad_scores = (chances * (grad_chances - inner_sum[..., None])).astype(jnp.bfloat16)
        grad_pscores = (prefix_chances * (grad_pchances - inner_sum[..., None])).astype(
            jnp.bfloat16
        )
        grad_query = jnp.einsum(
            "hqk,khd->qhd", grad_scores, key_heads, preferred_element_type=jnp.float32
        )
        grad_query = (
            grad_query
            + jnp.einsum(
                "hqp,phd->qhd", grad_pscores, prefix_keys, preferred_element_type=jnp.float32
            )
        ) * score_scale
        grad_keys = (
            grad_keys
            + jnp.einsum(
                "hqk,qhd->khd", grad_scores, query_heads, preferred_element_type=jnp.float32
            )
            * score_scale
        )
        grad_pkeys = (
            grad_pkeys
            + jnp.einsum(
                "hqp,qhd->phd", grad_pscores, query_heads, preferred_element_type=jnp.float32
            )
            * score_scale
        )
        return (
            (grad_keys, grad_values, grad_pkeys, grad_pvalues),
            grad_query.reshape(block_rows, columns),
        )

    key_zeros = jnp.zeros((key_count, head_count, HEAD_DIM), jnp.float32)
    prefix_zeros = jnp.zeros(prefix_keys.shape, jnp.float32)
    starts = jnp.arange(block_count, dtype=jnp.int32) * block_rows
    totals, grad_query = lax.scan(
        one_block,
        (key_zeros, key_zeros, prefix_zeros, prefix_zeros),
        (
            query.reshape(block_count, block_rows, columns),
            query_seg.reshape(block_count, block_rows),
            starts,
            log_totals,
            grad_out.reshape(block_count, block_rows, columns),
        ),
    )
    grad_prefix = jnp.stack([totals[2].reshape(-1, columns), totals[3].reshape(-1, columns)])
    return (
        grad_query.reshape(length, columns),
        totals[0].reshape(key_count, columns),
        totals[1].reshape(key_count, columns),
        grad_prefix,
    )


def spread(term):
    return lax.psum_scatter(term, "wide", scatter_dimension=1, tiled=True)


def collect(values):
    return lax.all_gather(values, "wide", axis=1, tiled=True)


def gather_grad(values):
    return lax.all_gather(values, "wide", axis=1, tiled=True)


def adapter_forward(adapter_in, adapter_down, adapter_up):
    down_full, up_full = (adapter_down, adapter_up)
    adapter_rows = lax.all_gather(adapter_in, "narrow", axis=0, tiled=True)
    bottle_pre = jnp.dot(adapter_rows, down_full, preferred_element_type=jnp.float32)
    bottle = jax.nn.gelu(bottle_pre, approximate=False).astype(jnp.bfloat16)
    adapted = lax.psum_scatter(
        jnp.dot(bottle, up_full, preferred_element_type=jnp.float32).astype(jnp.bfloat16),
        "narrow",
        scatter_dimension=0,
        tiled=True,
    ).astype(jnp.float32)
    return (adapted, (adapter_rows, bottle_pre, bottle, down_full, up_full))


def adapter_backward(saved, grad_adapted):
    adapter_rows, bottle_pre, bottle, down_full, up_full = saved
    grad_ad_rows = lax.all_gather(grad_adapted, "narrow", axis=0, tiled=True)
    grad_bottle = jnp.dot(grad_ad_rows, up_full.T, preferred_element_type=jnp.float32)
    grad_bottle_pre = gelu_grad(bottle_pre, grad_bottle).astype(jnp.bfloat16)
    grad_in_rows = lax.psum_scatter(
        jnp.dot(grad_bottle_pre, down_full.T, preferred_element_type=jnp.float32).astype(
            jnp.bfloat16
        ),
        "narrow",
        scatter_dimension=0,
        tiled=True,
    ).astype(jnp.float32)
    local_down = jnp.einsum(
        "rd,rb->db", adapter_rows, grad_bottle_pre, preferred_element_type=jnp.float32
    )
    local_up = jnp.einsum("rb,rd->bd", bottle, grad_ad_rows, preferred_element_type=jnp.float32)
    return (grad_in_rows, local_down, local_up)


def on_device(
    tokens,
    memory,
    dec_segments,
    mem_segments,
    self_qkv,
    self_out,
    cross_q,
    cross_kv,
    cross_out,
    ffn_in,
    ffn_out,
    adapter_down,
    adapter_up,
    self_prefix,
    cross_prefix,
    gains,
    cotangent,
):
    n_wide = lax.axis_size("wide")
    row_count, columns = tokens.shape
    sequences, seq_len = dec_segments.shape
    mem_len = mem_segments.shape[1]
    own_start = lax.axis_index("wide") * columns
    block_size = row_count // n_wide
    block_start = lax.axis_index("wide") * block_size
    gathered_tokens, gathered_memory = (
        lax.all_gather(tokens, "wide", axis=1, tiled=True),
        lax.all_gather(memory, "wide", axis=1, tiled=True),
    )
    projected = jnp.einsum(
        "rd,tdc->trc", gathered_tokens, self_qkv, preferred_element_type=jnp.float32
    ).astype(jnp.bfloat16)
    self_parts = (
        projected[0].reshape(sequences, seq_len, columns),
        projected[1].reshape(sequences, seq_len, columns),
        projected[2].reshape(sequences, seq_len, columns),
    )
    self_heads, self_logs = jax.vmap(partial(attend_forward, prefix=self_prefix, causal=True))(
        self_parts[0], self_parts[1], self_parts[2], dec_segments, dec_segments
    )
    self_heads = self_heads.reshape(row_count, columns)
    attn_own = spread(jnp.dot(self_heads, self_out, preferred_element_type=jnp.float32))
    first_sum = (tokens.astype(jnp.float32) + attn_own).astype(jnp.bfloat16)
    gathered_one = collect(first_sum)
    normed_one = layer_norm(gathered_one.astype(jnp.float32), gains[0])
    resid_one = lax.dynamic_slice_in_dim(normed_one, own_start, columns, 1)
    cross_query = jnp.dot(
        normed_one.astype(jnp.bfloat16), cross_q, preferred_element_type=jnp.float32
    ).astype(jnp.bfloat16)
    cross_keys = jnp.einsum(
        "md,tdc->tmc", gathered_memory, cross_kv, preferred_element_type=jnp.float32
    ).astype(jnp.bfloat16)
    cross_parts = (
        cross_query.reshape(sequences, seq_len, columns),
        cross_keys[0].reshape(sequences, mem_len, columns),
        cross_keys[1].reshape(sequences, mem_len, columns),
    )
    cross_heads, cross_logs = jax.vmap(partial(attend_forward, prefix=cross_prefix, causal=False))(
        cross_parts[0], cross_parts[1], cross_parts[2], dec_segments, mem_segments
    )
    cross_heads = cross_heads.reshape(row_count, columns)
    cross_own = spread(jnp.dot(cross_heads, cross_out, preferred_element_type=jnp.float32))
    second_sum = (resid_one + cross_own).astype(jnp.bfloat16)
    gathered_two = collect(second_sum)
    normed_two = layer_norm(gathered_two.astype(jnp.float32), gains[1])
    normed_low = normed_two.astype(jnp.bfloat16)
    resid_two = lax.dynamic_slice_in_dim(normed_two, own_start, columns, 1)
    adapter_in = lax.dynamic_slice_in_dim(normed_low, block_start, block_size, 0)
    adapted, saved = adapter_forward(adapter_in, adapter_down, adapter_up)
    pre_act = jnp.dot(normed_low, ffn_in, preferred_element_type=jnp.float32)
    hidden = jax.nn.gelu(pre_act, approximate=False).astype(jnp.bfloat16)
    branch = jnp.dot(hidden, ffn_out, preferred_element_type=jnp.float32)
    placed = lax.dynamic_slice_in_dim(branch, block_start, block_size, 0) + 4.0 * adapted
    branch = lax.dynamic_update_slice_in_dim(branch, placed, block_start, 0)
    mixed_own = spread(branch)
    third_sum = (resid_two + mixed_own).astype(jnp.bfloat16)
    gathered_three = collect(third_sum)
    output = lax.dynamic_slice_in_dim(
        layer_norm(gathered_three.astype(jnp.float32), gains[2]), own_start, columns, 1
    ).astype(jnp.bfloat16)
    grad_out = gather_grad(cotangent).astype(jnp.float32)
    grad_three = norm_grad(gathered_three, gains[2], grad_out)
    grad_branch = grad_three.astype(jnp.bfloat16)
    grad_hidden = jnp.dot(grad_branch, ffn_out.T, preferred_element_type=jnp.float32)
    grad_pre = gelu_grad(pre_act, grad_hidden).astype(jnp.bfloat16)
    grad_normed = jnp.dot(grad_pre, ffn_in.T, preferred_element_type=jnp.float32)
    grad_adapted = (
        lax.dynamic_slice_in_dim(grad_branch, block_start, block_size, 0).astype(jnp.float32) * 4.0
    ).astype(jnp.bfloat16)
    grad_in_rows, local_down, local_up = adapter_backward(saved, grad_adapted)
    placed_grad = lax.dynamic_slice_in_dim(grad_normed, block_start, block_size, 0) + grad_in_rows
    grad_normed = lax.dynamic_update_slice_in_dim(grad_normed, placed_grad, block_start, 0)
    grad_two_own = lax.dynamic_slice_in_dim(grad_three, own_start, columns, 1) + spread(grad_normed)
    grad_two = gather_grad(grad_two_own.astype(jnp.bfloat16)).astype(jnp.float32)
    grad_down, grad_up = lax.psum((local_down, local_up), ("dp", "wide"))
    grad_second = norm_grad(gathered_two, gains[1], grad_two)
    grad_cross = jnp.dot(
        grad_second.astype(jnp.bfloat16), cross_out.T, preferred_element_type=jnp.float32
    ).astype(jnp.bfloat16)
    cross_back = jax.vmap(partial(attend_backward, prefix=cross_prefix, causal=False))(
        cross_parts[0],
        cross_parts[1],
        cross_parts[2],
        dec_segments,
        mem_segments,
        cross_logs,
        grad_cross.reshape(sequences, seq_len, columns),
    )
    grad_cquery = cross_back[0].reshape(row_count, columns).astype(jnp.bfloat16)
    grad_ckv = jnp.stack(
        [cross_back[1].reshape(-1, columns), cross_back[2].reshape(-1, columns)]
    ).astype(jnp.bfloat16)
    grad_one_part = jnp.dot(grad_cquery, cross_q.T, preferred_element_type=jnp.float32)
    grad_mem_part = jnp.einsum(
        "tmc,tdc->md", grad_ckv, cross_kv, preferred_element_type=jnp.float32
    )
    spread_one, grad_memory = (
        lax.psum_scatter(
            grad_one_part.astype(jnp.bfloat16), "wide", scatter_dimension=1, tiled=True
        ).astype(jnp.float32),
        lax.psum_scatter(
            grad_mem_part.astype(jnp.bfloat16), "wide", scatter_dimension=1, tiled=True
        ).astype(jnp.float32),
    )
    grad_one_own = lax.dynamic_slice_in_dim(grad_second, own_start, columns, 1) + spread_one
    grad_one = lax.all_gather(grad_one_own.astype(jnp.bfloat16), "wide", axis=1, tiled=True).astype(
        jnp.float32
    )
    grad_first = norm_grad(gathered_one, gains[0], grad_one)
    grad_self = jnp.dot(
        grad_first.astype(jnp.bfloat16), self_out.T, preferred_element_type=jnp.float32
    ).astype(jnp.bfloat16)
    self_back = jax.vmap(partial(attend_backward, prefix=self_prefix, causal=True))(
        self_parts[0],
        self_parts[1],
        self_parts[2],
        dec_segments,
        dec_segments,
        self_logs,
        grad_self.reshape(sequences, seq_len, columns),
    )
    grad_projected = jnp.stack(
        [
            self_back[0].reshape(row_count, columns),
            self_back[1].reshape(row_count, columns),
            self_back[2].reshape(row_count, columns),
        ]
    ).astype(jnp.bfloat16)
    grad_input_part = jnp.einsum(
        "trc,tdc->rd", grad_projected, self_qkv, preferred_element_type=jnp.float32
    )
    grad_tokens = lax.dynamic_slice_in_dim(grad_first, own_start, columns, 1) + spread(
        grad_input_part
    )
    grad_self_prefix, grad_cross_prefix = (
        lax.psum(jnp.sum(self_back[3], axis=0).astype(jnp.bfloat16), ("dp", "narrow")).astype(
            jnp.float32
        ),
        lax.psum(jnp.sum(cross_back[3], axis=0).astype(jnp.bfloat16), ("dp", "narrow")).astype(
            jnp.float32
        ),
    )
    return (
        output,
        grad_tokens,
        grad_memory,
        grad_self_prefix,
        grad_cross_prefix,
        grad_down,
        grad_up,
    )


def solution(mesh):
    return jax.shard_map(
        on_device,
        mesh=mesh,
        in_specs=(
            P(("dp", "narrow"), "wide"),
            P(("dp", "narrow"), "wide"),
            P(("dp", "narrow"), None),
            P(("dp", "narrow"), None),
            P(None, None, "wide"),
            P("wide", None),
            P(None, "wide"),
            P(None, None, "wide"),
            P("wide", None),
            P(None, "wide"),
            P("wide", None),
            P(None, "narrow"),
            P("narrow", None),
            P(None, None, "wide"),
            P(None, None, "wide"),
            P(),
            P(("dp", "narrow"), "wide"),
        ),
        out_specs=(
            P(("dp", "narrow"), "wide"),
            P(("dp", "narrow"), "wide"),
            P(("dp", "narrow"), "wide"),
            P(None, None, "wide"),
            P(None, None, "wide"),
            P(None, "narrow"),
            P("narrow", None),
        ),
        check_vma=False,
    )
```

profile of v0, /device:TPU:0, one launch (start us, length us, event | category | flops | bytes accessed | tf_op | source)
XLA Modules:
  0.0 3143.3 jit_solution(6404103960606428820)
XLA Ops:
  10.1 59.0 %all-gather.11.cloned.1.call-done = bf16[2048,1024]{1,0:T(8,128)(2,1)} async-done(((bf16[2048,512]{1,0:T(8,128)(2,1)}), bf16[2048,1024]{1,0:T(8,128)(2,1)}) %all-gather.11.cloned.1.call-update) | async-done | bytes 4194320 | tf_op jit(solution)/shard_map/all_gather | solution.py:263
  85.2 230.8 %while.62 = (s32[]{:T(128)}, bf16[4,1,512,512]{3,2,0,1:T(8,128)(2,1)}, f32[4,1,8,512]{3,2,1,0:T(8,128)}, s32[4,1,512]{2,1,0:T(1,128)}, s32[1,2048]{1,0:T(1,128)}...) while((s32[]{:T(128)}, ...), condition=%wide.region_5.6_spmd, body=%wide.region_0.5_spmd.sunk | while | flops 2275619328 | bytes 130268352 | solution.py:82
  122.7 16.4 fusion.325
  180.3 16.4 fusion.325
  237.9 16.4 fusion.325
  295.5 16.4 fusion.325
  324.4 98.6 %reduce-scatter.10.cloned.1.call-done = f32[2048,512]{1,0:T(8,128)} async-done(((f32[2048,1024]{1,0:T(8,128)}), f32[2048,512]{1,0:T(8,128)}) %reduce-scatter.10.cloned.1.call-update) | async-done | bytes 4194320 | tf_op jit(solution)/shard_map/reduce_scatter | solution.py:191
  429.1 52.3 %all-gather.15.cloned.1.call-done = bf16[2048,1024]{1,0:T(8,128)(2,1)} async-done(((bf16[2048,512]{1,0:T(8,128)(2,1)}), bf16[2048,1024]{1,0:T(8,128)(2,1)}) %all-gather.15.cloned.1.call-update) | async-done | bytes 4194320 | tf_op jit(solution)/shard_map/all_gather | solution.py:264
  491.1 49.1 %all-gather.13.cloned.1.call-done = bf16[2048,1024]{1,0:T(8,128)(2,1)} async-done(((bf16[2048,512]{1,0:T(8,128)(2,1)}), bf16[2048,1024]{1,0:T(8,128)(2,1)}) %all-gather.13.cloned.1.call-update) | async-done | bytes 4194320 | tf_op jit(solution)/shard_map/all_gather | solution.py:195
  555.9 220.8 %while.63 = (s32[]{:T(128)}, bf16[4,1,512,512]{3,2,0,1:T(8,128)(2,1)}, f32[4,1,8,512]{3,2,1,0:T(8,128)}, s32[4,1,512]{2,1,0:T(1,128)}, s32[1,2048]{1,0:T(1,128)}...) while((s32[]{:T(128)}, ...), condition=%wide.region_14.15_spmd, body=%wide.region_9.14_spmd.sunk | while | flops 2273521664 | bytes 130264232 | solution.py:82
  590.8 16.4 fusion.333
  646.0 16.4 fusion.333
  701.1 16.4 fusion.333
  756.3 16.4 fusion.333
  790.5 93.2 %reduce-scatter.12.cloned.1.call-done = f32[2048,512]{1,0:T(8,128)} async-done(((f32[2048,1024]{1,0:T(8,128)}), f32[2048,512]{1,0:T(8,128)}) %reduce-scatter.12.cloned.1.call-update) | async-done | bytes 4194320 | tf_op jit(solution)/shard_map/reduce_scatter | solution.py:191
  889.3 56.9 %all-gather.17.cloned.1.call-done = bf16[2048,1024]{1,0:T(8,128)(2,1)} async-done(((bf16[2048,512]{1,0:T(8,128)(2,1)}), bf16[2048,1024]{1,0:T(8,128)(2,1)}) %all-gather.17.cloned.1.call-update) | async-done | bytes 4194320 | tf_op jit(solution)/shard_map/all_gather | solution.py:195
  959.2 58.4 %all-gather.19.cloned.1.call-done = bf16[4096,1024]{1,0:T(8,128)(2,1)} async-done(((bf16[1024,1024]{1,0:T(8,128)(2,1)}), bf16[4096,1024]{1,0:T(8,128)(2,1)}) %all-gather.19.cloned.1.call-update) | async-done | bytes 8388624 | tf_op jit(solution)/shard_map/all_gather | solution.py:204
  1034.0 46.9 %fusion.86 = (f32[2048,2048]{1,0:T(8,128)}, f32[2048,2048]{1,0:T(8,128)}) fusion(bf16[2048,1024]{1,0:T(8,128)(2,1)} %copy-done.32, bf16[1024,2048]{1,0:T(8,128)(2,1)} %param.34), kind=kOutput, calls=%fused_computation.121 | convolution fusion | flops 8849981440 | bytes 41943040 | tf_op jit(solution)/shard_map/dot_general | solution.py:306
  1080.9 18.6 fusion.106
  1111.9 99.3 %reduce-scatter.16.cloned.1.call-done = f32[2048,512]{1,0:T(8,128)} async-done(((f32[2048,1024]{1,0:T(8,128)}), f32[2048,512]{1,0:T(8,128)}) %reduce-scatter.16.cloned.1.call-update) | async-done | bytes 4194320 | tf_op jit(solution)/shard_map/reduce_scatter | solution.py:191
  1217.9 55.7 %all-gather.21.cloned.1.call-done = bf16[2048,1024]{1,0:T(8,128)(2,1)} async-done(((bf16[2048,512]{1,0:T(8,128)(2,1)}), bf16[2048,1024]{1,0:T(8,128)(2,1)}) %all-gather.21.cloned.1.call-update) | async-done | bytes 4194320 | tf_op jit(solution)/shard_map/all_gather | solution.py:195
  1276.5 55.5 %all-gather.23.cloned.1.call-done = bf16[2048,1024]{1,0:T(8,128)(2,1)} async-done(((bf16[2048,512]{1,0:T(8,128)(2,1)}), bf16[2048,1024]{1,0:T(8,128)(2,1)}) %all-gather.23.cloned.1.call-update) | async-done | bytes 4194320 | tf_op jit(solution)/shard_map/all_gather | solution.py:199
  1352.0 58.4 %all-gather.25.cloned.1.call-done = bf16[4096,1024]{1,0:T(8,128)(2,1)} async-done(((bf16[1024,1024]{1,0:T(8,128)(2,1)}), bf16[4096,1024]{1,0:T(8,128)(2,1)}) %all-gather.25.cloned.1.call-update) | async-done | bytes 8388624 | tf_op jit(solution)/shard_map/all_gather | solution.py:218
  1424.5 28.9 fusion.108
  1453.4 42.7 %reduce-scatter.18.cloned.1.call-done = bf16[1024,1024]{1,0:T(8,128)(2,1)} async-done(((bf16[4096,1024]{1,0:T(8,128)(2,1)}), bf16[1024,1024]{1,0:T(8,128)(2,1)}) %reduce-scatter.18.cloned.1.call-update) | async-done | bytes 2097168 | tf_op jit(solution)/shard_map/reduce_scatter | solution.py:221
  1502.2 99.3 %reduce-scatter.20.cloned.1.call-done = f32[2048,512]{1,0:T(8,128)} async-done(((f32[2048,1024]{1,0:T(8,128)}), f32[2048,512]{1,0:T(8,128)}) %reduce-scatter.20.cloned.1.call-update) | async-done | bytes 4194320 | tf_op jit(solution)/shard_map/reduce_scatter | solution.py:191
  1607.1 56.8 %all-gather.27.cloned.1.call-done = bf16[2048,1024]{1,0:T(8,128)(2,1)} async-done(((bf16[2048,512]{1,0:T(8,128)(2,1)}), bf16[2048,1024]{1,0:T(8,128)(2,1)}) %all-gather.27.cloned.1.call-update) | async-done | bytes 4194320 | tf_op jit(solution)/shard_map/all_gather | solution.py:199
  1680.0 509.6 %while.64 = (s32[]{:T(128)}, f32[1,2048,8,64]{1,3,2,0:T(8,128)}, f32[1,2048,8,64]{1,3,2,0:T(8,128)}, f32[1,30,8,64]{3,1,2,0:T(8,128)}, f32[1,30,8,64]{3,1,2,0:T(...) while((s32[]{:T(128)}, f32[1,2048,8,64]{1,3,2,0:T(8,128)}, ...), condition=%wide.region_31.32_spmd.clone, body=%wide.region_28.31_spmd.clone.sunk | while | flops 5530983424 | bytes 310731712 | solution.py:170
  1684.4 17.5 fusion.353
  1705.7 25.7 multiply_reduce_fusion.10
  1732.8 27.5 multiply_convert_fusion.12
  1809.8 17.5 fusion.353
  1831.2 25.7 multiply_reduce_fusion.10
  1858.3 27.5 multiply_convert_fusion.12
  1914.7 17.0 bitcast_add_fusion.9
  1937.7 17.5 fusion.353
  1959.0 25.7 multiply_reduce_fusion.10
  1986.1 27.5 multiply_convert_fusion.12
  2042.5 17.0 bitcast_add_fusion.9
  2065.5 17.5 fusion.353
  2086.9 25.7 multiply_reduce_fusion.10
  2113.9 27.5 multiply_convert_fusion.12
  2170.4 17.0 bitcast_add_fusion.9
  2195.9 54.4 %reduce-scatter.22.cloned.1.call-done = bf16[2048,512]{1,0:T(8,128)(2,1)} async-done(((bf16[2048,1024]{1,0:T(8,128)(2,1)}), bf16[2048,512]{1,0:T(8,128)(2,1)}) %reduce-scatter.22.cloned.1.call-update) | async-done | bytes 2097168 | tf_op jit(solution)/shard_map/reduce_scatter | solution.py:354
  2282.4 29.7 all-gather.29.cloned.1.call-done
  2328.3 508.5 %while.65 = (s32[]{:T(128)}, f32[1,2048,8,64]{1,3,2,0:T(8,128)}, f32[1,2048,8,64]{1,3,2,0:T(8,128)}, f32[1,30,8,64]{3,1,2,0:T(8,128)}, f32[1,30,8,64]{3,1,2,0:T(...) while((s32[]{:T(128)}, f32[1,2048,8,64]{1,3,2,0:T(8,128)}, ...), condition=%wide.region_38.39_spmd.clone, body=%wide.region_35.38_spmd.clone.sunk | while | flops 5533081088 | bytes 313881600 | solution.py:170
  2338.1 17.9 fusion.377
  2357.8 25.7 multiply_reduce_fusion.12
  2384.9 27.5 multiply_convert_fusion.14
  2463.6 17.5 fusion.377
  2482.9 25.7 multiply_reduce_fusion.12
  2509.9 27.5 multiply_convert_fusion.14
  2562.6 17.0 bitcast_add_fusion.11
  2591.0 17.5 fusion.377
  2610.4 25.7 multiply_reduce_fusion.12
  2637.4 27.5 multiply_convert_fusion.14
  2690.0 17.0 bitcast_add_fusion.11
  2718.5 17.5 fusion.377
  2737.8 25.7 multiply_reduce_fusion.12
  2764.9 27.5 multiply_convert_fusion.14
  2817.5 17.0 bitcast_add_fusion.11
  2891.5 55.0 %all-reduce.7.cloned.1.call-done = (bf16[2,30,512]{2,1,0:T(8,128)(2,1)}, bf16[2,30,512]{2,1,0:T(8,128)(2,1)}) async-done(((bf16[2,30,512]{2,1,0:T(8,128)(2,1)}, bf16[2,30,512]{2,1,0:T(8,128)(2,1)}), (bf16[2,30,512]{2,1,0:T(8,128)(2,1)}, bf16[2,30,512]{2,1,0:T(8,128)(2,1)})) %all-reduce.7.cloned.1.call-update) | async-done | bytes 122896 | tf_op jit(solution)/shard_map/psum | solution.py:392
  2949.6 100.1 %reduce-scatter.24.cloned.1.call-done = f32[2048,512]{1,0:T(8,128)} async-done(((f32[2048,1024]{1,0:T(8,128)}), f32[2048,512]{1,0:T(8,128)}) %reduce-scatter.24.cloned.1.call-update) | async-done | bytes 4194320 | tf_op jit(solution)/shard_map/reduce_scatter | solution.py:191
  3056.1 76.5 %all-reduce.5.cloned.1.call-done = (f32[1024,128]{1,0:T(8,128)}, f32[128,1024]{1,0:T(8,128)}) async-done(((f32[1024,128]{1,0:T(8,128)}, f32[128,1024]{1,0:T(8,128)}), (f32[1024,128]{1,0:T(8,128)}, f32[128,1024]{1,0:T(8,128)})) %all-reduce.5.cloned.1.call-update) | async-done | bytes 1048592 | tf_op jit(solution)/shard_map/psum | solution.py:331
  (706 shorter events, 980.8 us)
Async XLA Ops:
  7.2 61.9 %copy-start = (bf16[3,1024,512]{2,1,0:T(8,128)(2,1)S(1)}, bf16[3,1024,512]{2,1,0:T(8,128)(2,1)}, u32[]{:S(2)}) copy-start(bf16[3,1024,512]{2,1,0:T(8,128)(2,1)} %param.29) | copy-start | bytes 9437188
  7.2 61.9 %all-gather.11.cloned.1.call-start = ((), (), s32[]{:S(2)}) async-start(), calls=%async_computation.9 | async-start | bytes 6291456 | tf_op jit(solution)/shard_map/all_gather | solution.py:263
  7.9 415.1 %reduce-scatter.10.cloned.1.call-start = ((), (), s32[]{:S(2)}) async-start(), calls=%async_computation.10 | async-start | bytes 12582912 | tf_op jit(solution)/shard_map/reduce_scatter | solution.py:191
  323.6 157.8 %all-gather.15.cloned.1.call-start = ((), (), s32[]{:S(2)}) async-start(), calls=%async_computation.12 | async-start | bytes 6291456 | tf_op jit(solution)/shard_map/all_gather | solution.py:264
  324.3 103.6 %copy-start.58 = (bf16[2,30,512]{2,0,1:T(2,128)(2,1)S(1)}, bf16[2,30,512]{2,0,1:T(2,128)(2,1)}, u32[]{:S(2)}) copy-start(bf16[2,30,512]{2,0,1:T(2,128)(2,1)} %param.39) | copy-start | bytes 184324
  324.4 104.1 %copy-start.79 = (f32[3,1024]{1,0:T(4,128)S(1)}, f32[3,1024]{1,0:T(4,128)}, u32[]{:S(2)}) copy-start(f32[3,1024]{1,0:T(4,128)} %param.40) | copy-start | bytes 36868
  324.4 215.9 %all-gather.13.cloned.1.call-start = ((), (), s32[]{:S(2)}) async-start(), calls=%async_computation.11 | async-start | bytes 6291456 | tf_op jit(solution)/shard_map/all_gather | solution.py:195
  427.9 455.8 %reduce-scatter.12.cloned.1.call-start = ((), (), s32[]{:S(2)}) async-start(), calls=%async_computation.13 | async-start | bytes 12582912 | tf_op jit(solution)/shard_map/reduce_scatter | solution.py:191
  429.1 117.0 %copy-start.68 = (f32[1,1024]{1,0:T(1,128)}, f32[1,1024]{1,0:T(1,128)S(1)}, u32[]{:S(2)}) copy-start(f32[1,1024]{1,0:T(1,128)S(1)} %get-tuple-element.656) | copy-start | bytes 12292
  784.4 161.8 %all-gather.17.cloned.1.call-start = ((), (), s32[]{:S(2)}) async-start(), calls=%async_computation.14 | async-start | bytes 6291456 | tf_op jit(solution)/shard_map/all_gather | solution.py:195
  889.3 128.3 %all-gather.19.cloned.1.call-start = ((), (), s32[]{:S(2)}) async-start(), calls=%async_computation.15 | async-start | bytes 10485760 | tf_op jit(solution)/shard_map/all_gather | solution.py:204
  889.3 62.3 %copy-start.71 = (f32[1,1024]{1,0:T(1,128)S(1)}, f32[1,1024]{1,0:T(1,128)}, u32[]{:S(2)}) copy-start(f32[1,1024]{1,0:T(1,128)} %get-tuple-element.657) | copy-start | bytes 12292
  955.6 62.0 %copy-start.54 = (bf16[1024,128]{1,0:T(8,128)(2,1)S(1)}, bf16[1024,128]{1,0:T(8,128)(2,1)}, u32[]{:S(2)}) copy-start(bf16[1024,128]{1,0:T(8,128)(2,1)} %param.36) | copy-start | bytes 786436
  959.1 146.7 %reduce-scatter.14.cloned.1.call-start = ((), (), s32[]{:S(2)}) async-start(), calls=%async_computation.16 | async-start | bytes 10485760 | tf_op jit(solution)/shard_map/reduce_scatter | solution.py:207
  1033.9 177.3 %reduce-scatter.16.cloned.1.call-start = ((), (), s32[]{:S(2)}) async-start(), calls=%async_computation.17 | async-start | bytes 12582912 | tf_op jit(solution)/shard_map/reduce_scatter | solution.py:191
  1111.9 161.8 %all-gather.21.cloned.1.call-start = ((), (), s32[]{:S(2)}) async-start(), calls=%async_computation.18 | async-start | bytes 6291456 | tf_op jit(solution)/shard_map/all_gather | solution.py:195
  1216.7 115.3 %copy-start.73 = (f32[1,1024]{1,0:T(1,128)S(1)}, f32[1,1024]{1,0:T(1,128)}, u32[]{:S(2)}) copy-start(f32[1,1024]{1,0:T(1,128)} %get-tuple-element.655) | copy-start | bytes 12292
  1216.8 115.2 %all-gather.23.cloned.1.call-start = ((), (), s32[]{:S(2)}) async-start(), calls=%async_computation.19 | async-start | bytes 6291456 | tf_op jit(solution)/shard_map/all_gather | solution.py:199
  1217.5 192.9 %all-gather.25.cloned.1.call-start = ((), (), s32[]{:S(2)}) async-start(), calls=%async_computation.20 | async-start | bytes 10485760 | tf_op jit(solution)/shard_map/all_gather | solution.py:218
  1348.0 62.4 %copy-start.57 = (bf16[128,1024]{1,0:T(8,128)(2,1)S(1)}, bf16[128,1024]{1,0:T(8,128)(2,1)}, u32[]{:S(2)}) copy-start(bf16[128,1024]{1,0:T(8,128)(2,1)} %param.37) | copy-start | bytes 786436
  1351.9 144.2 %reduce-scatter.18.cloned.1.call-start = ((), (), s32[]{:S(2)}) async-start(), calls=%async_computation.21 | async-start | bytes 10485760 | tf_op jit(solution)/shard_map/reduce_scatter | solution.py:221
  1424.3 177.2 %reduce-scatter.20.cloned.1.call-start = ((), (), s32[]{:S(2)}) async-start(), calls=%async_computation.22 | async-start | bytes 12582912 | tf_op jit(solution)/shard_map/reduce_scatter | solution.py:191
  1502.1 161.8 %all-gather.27.cloned.1.call-start = ((), (), s32[]{:S(2)}) async-start(), calls=%async_computation.23 | async-start | bytes 6291456 | tf_op jit(solution)/shard_map/all_gather | solution.py:199
  1601.4 62.5 %copy-start.50 = (f32[2048]{0:T(1024)S(1)}, f32[2048]{0:T(1024)}, u32[]{:S(2)}) copy-start(f32[2048]{0:T(1024)} %copy-done.49) | copy-start | bytes 24580
  1601.4 62.5 %copy-start.72 = (f32[1,1024]{1,0:T(1,128)S(1)}, f32[1,1024]{1,0:T(1,128)}, u32[]{:S(2)}) copy-start(f32[1,1024]{1,0:T(1,128)} %get-tuple-element.657) | copy-start | bytes 12292
  1607.0 643.3 %reduce-scatter.22.cloned.1.call-start = ((), (), s32[]{:S(2)}) async-start(), calls=%async_computation.24 | async-start | bytes 6291456 | tf_op jit(solution)/shard_map/reduce_scatter | solution.py:354
  1607.1 61.4 %copy-start.78 = (f32[2048]{0:T(1024)S(1)}, f32[2048]{0:T(1024)}, u32[]{:S(2)}) copy-start(f32[2048]{0:T(1024)} %copy-done.77) | copy-start | bytes 24580
  1607.1 61.4 %copy-start.64 = (f32[2048]{0:T(1024)S(1)}, f32[2048]{0:T(1024)}, u32[]{:S(2)}) copy-start(f32[2048]{0:T(1024)} %copy-done.63) | copy-start | bytes 24580
  1684.4 21.4 copy-start.4
  1702.9 28.7 copy-start.9
  1705.7 25.7 copy-start.7
  1809.8 21.4 copy-start.4
  1828.4 28.7 copy-start.9
  1831.2 25.7 copy-start.7
  1937.7 21.4 copy-start.4
  1956.2 28.8 copy-start.9
  1959.0 25.7 copy-start.7
  2065.5 21.4 copy-start.4
  2084.1 28.8 copy-start.9
  2086.9 25.7 copy-start.7
  2195.9 59.5 %copy-start.46 = (f32[1,30,8,64]{3,1,2,0:T(8,128)S(1)}, f32[1,30,8,64]{3,1,2,0:T(8,128)}, u32[]{:S(2)}) copy-start(f32[1,30,8,64]{3,1,2,0:T(8,128)} %get-tuple-element.297) | copy-start | bytes 184324
  2195.9 60.2 %copy-start.41 = (f32[1,30,8,64]{3,1,2,0:T(8,128)S(1)}, f32[1,30,8,64]{3,1,2,0:T(8,128)}, u32[]{:S(2)}) copy-start(f32[1,30,8,64]{3,1,2,0:T(8,128)} %get-tuple-element.298) | copy-start | bytes 184324
  2195.9 116.3 %all-gather.29.cloned.1.call-start = ((), (), s32[]{:S(2)}) async-start(), calls=%async_computation.25 | async-start | bytes 6291456 | tf_op jit(solution)/shard_map/all_gather | solution.py:362
  2255.2 632.0 %reduce-scatter.26.cloned.1.call-start = ((), (), s32[]{:S(2)}) async-start(), calls=%async_computation.27 | async-start | bytes 6291456 | tf_op jit(solution)/shard_map/reduce_scatter | solution.py:357
  2282.3 29.8 copy-start.53
  2282.4 29.8 copy-start.70
  2282.4 34.4 %copy-start.76 = (f32[2048]{0:T(1024)S(1)}, f32[2048]{0:T(1024)}, u32[]{:S(2)}) copy-start(f32[2048]{0:T(1024)} %copy-done.75) | copy-start | bytes 24580
  2282.4 34.4 %copy-start.67 = (f32[2048]{0:T(1024)S(1)}, f32[2048]{0:T(1024)}, u32[]{:S(2)}) copy-start(f32[2048]{0:T(1024)} %copy-done.65) | copy-start | bytes 24580
  2282.4 664.1 %all-reduce.7.cloned.1.call-start = ((), (), s32[]{:S(2)}) async-start(), calls=%async_computation.29 | async-start | bytes 262144 | tf_op jit(solution)/shard_map/psum | solution.py:392
  2338.1 19.7 copy-start.2
  2338.1 19.7 copy-start.13
  2357.0 26.8 copy-start.11
  2357.8 25.7 copy-start.8
  2482.1 26.7 copy-start.11
  2482.9 25.7 copy-start.8
  2591.0 19.3 copy-start.2
  2591.0 19.3 copy-start.13
  2609.6 26.7 copy-start.11
  2610.4 25.7 copy-start.8
  2718.5 19.3 copy-start.13
  2737.1 26.7 copy-start.11
  2737.8 25.7 copy-start.8
  2859.2 190.4 %reduce-scatter.24.cloned.1.call-start = ((), (), s32[]{:S(2)}) async-start(), calls=%async_computation.26 | async-start | bytes 12582912 | tf_op jit(solution)/shard_map/reduce_scatter | solution.py:191
  2870.1 262.5 %all-reduce.5.cloned.1.call-start = ((), (), s32[]{:S(2)}) async-start(), calls=%async_computation.28 | async-start | bytes 2097152 | tf_op jit(solution)/shard_map/psum | solution.py:331
  (109 other events, 754.3 us)
Sparse Core Ops, SparseCore 0:
  9.6 59.4 all-gather.10
  323.7 99.2 reduce-scatter.9
  424.6 56.7 all-gather.14
  483.5 56.7 all-gather.12
  784.5 99.2 reduce-scatter.11
  889.4 56.7 all-gather.16
  959.2 58.2 all-gather.18
  1034.1 71.7 reduce-scatter.13
  1112.0 99.1 reduce-scatter.15
  1216.9 56.7 all-gather.20
  1275.2 56.7 all-gather.22
  1352.0 58.2 all-gather.24
  1424.4 71.7 reduce-scatter.17
  1502.2 99.1 reduce-scatter.19
  1607.1 56.7 all-gather.26
  2196.0 54.2 reduce-scatter.21
  2255.4 56.7 all-gather.28
  2314.4 54.3 reduce-scatter.25
  2859.3 87.0 all-reduce.6
  2948.6 100.9 reduce-scatter.23
  3054.2 78.3 all-reduce.4
where the time goes:
time: 3150 us; the launch traced here: 3140 us
  waiting for transfers between devices  1260 us (40%)
  matrix products  1140 us (36%)
  other arithmetic  524 us (17%)
  local copies, waits for them, and re-layouts  201 us (6%)
    reduce_scatter x5, waiting for transfers between devices, spread(): return lax.psum_scatter(term, 'wide', scatter_dimension=1, tiled=True)  490 us
    dot_general x16, matrix products, head_scores(): jnp.einsum('qhd,khd->hqk', query_heads, key_heads, preferred_element_type...  317 us
    convert_element_type x8, other arithmetic, one_block(): (chances * (grad_chances - inner_sum[..., None])).astype(jnp.bfloat16)  220 us
    all_gather x3, waiting for transfers between devices, collect(): return lax.all_gather(values, 'wide', axis=1, tiled=True)  162 us
    dot_general x8, matrix products, one_block(): jnp.einsum('qhd,khd->hqk', grad_heads, value_heads, preferred_element_typ...  140 us
    dot_general x8, matrix products, one_block(): jnp.einsum('hqk,qhd->khd', chances.astype(jnp.bfloat16), grad_heads, pref...  133 us
    dot_general x8, matrix products, one_block(): jnp.einsum('hqk,khd->qhd', chances, value_heads, preferred_element_type=j...  131 us
    reduce_sum x8, other arithmetic, one_block(): jnp.sum(jnp.exp(scores - largest[..., None]), axis=-1)  120 us
  transfers between devices with their start and end apart: 21, of which 20 were waited for; matrix products, arithmetic and copies ran while one was open for 23% of the time, Pallas kernels for 0%

commit v1 on v0

v1 whole, which is shorter than its diff:
```python
import functools
import math
from functools import partial

import jax
import jax.numpy as jnp
from jax import lax
from jax.experimental import pallas as pl
from jax.experimental.pallas import tpu as pltpu
from jax.sharding import Mesh
from jax.sharding import PartitionSpec as P

HEAD_DIM = 64
DOCS = 4
NEG = -1e30
BQ = 256
BK = 256
PP = 32
BT = 256
HEADS_FWD = 8
HEADS_BWD = 4
SWAP = [(0, 1), (1, 0)]
MIB = 2**20


def mm(a, b):
    return jnp.dot(a, b, preferred_element_type=jnp.float32)


def mm_nt(a, b):
    return lax.dot_general(a, b, (((1,), (1,)), ((), ())), preferred_element_type=jnp.float32)


def mm_tn(a, b):
    return lax.dot_general(a, b, (((0,), (0,)), ((), ())), preferred_element_type=jnp.float32)


def pair_rows(t):
    zero = jnp.zeros((HEAD_DIM, t.shape[1]), t.dtype)
    return [
        jnp.concatenate([t[:HEAD_DIM], zero], axis=0),
        jnp.concatenate([zero, t[HEAD_DIM:]], axis=0),
    ]


def part_offsets(n_parts, part_len):
    if n_parts == 1:
        return [0]
    core = lax.axis_index("c")
    return [pl.multiple_of(core * part_len, part_len), pl.multiple_of((1 - core) * part_len, part_len)]


def fwd_kernel(causal, n_parts, lo_ref, hi_ref, *refs):
    q_parts, k_parts, v_parts = refs[:n_parts], refs[n_parts:2 * n_parts], refs[2 * n_parts:3 * n_parts]
    ek_ref, eq_ref, pre_ref, ep_ref = refs[3 * n_parts:3 * n_parts + 4]
    o_parts = refs[3 * n_parts + 4:4 * n_parts + 4]
    ot_ref, lt_ref, qt, vt, ke = refs[4 * n_parts + 4:]
    seq = qt.shape[1]
    q_len, m_len = q_parts[0].shape[0], k_parts[0].shape[0]
    width = q_parts[0].shape[1]
    n_pairs = width // 128
    heads_here = width // HEAD_DIM
    n_q = seq // BQ

    for q_ref, at in zip(q_parts, part_offsets(n_parts, q_len)):
        qt[:, pl.ds(at, q_len)] = (q_ref[...] * jnp.bfloat16(0.125)).T
    for k_ref, v_ref, at in zip(k_parts, v_parts, part_offsets(n_parts, m_len)):
        vt[:, pl.ds(at, m_len)] = v_ref[...].T
        for p in range(n_pairs):
            ke[p, pl.ds(at, m_len), :128] = k_ref[:, p * 128:(p + 1) * 128]
    for p in range(n_pairs):
        ke[p, :, 128:] = ek_ref[...]
    vpt = pre_ref[1].T
    ones = jnp.ones((16, BK), jnp.bfloat16)

    def q_step(i, _):
        qs = pl.ds(pl.multiple_of(i * BQ, BQ), BQ)
        eq = eq_ref[:, qs]
        heads = []
        for p in range(n_pairs):
            heads += [jnp.concatenate([r, eq], axis=0) for r in pair_rows(qt[p * 128:(p + 1) * 128, qs])]

        def block(j, carry, diag):
            ks = pl.ds(pl.multiple_of(j * BK, BK), BK)
            out = []
            scores = [mm(ke[h // 2, ks, :], heads[h]) for h in range(heads_here)]
            for h in range(heads_here):
                m, acc = carry[h]
                s = scores[h]
                if diag:
                    kk = lax.broadcasted_iota(jnp.int32, (BK, BQ), 0)
                    qq = lax.broadcasted_iota(jnp.int32, (BK, BQ), 1)
                    s = jnp.where(kk <= qq, s, NEG)
                m_new = jnp.maximum(m, jnp.max(s, axis=0, keepdims=True))
                p = jnp.exp(s - m_new).astype(jnp.bfloat16)
                vb = jnp.concatenate([vt[h * HEAD_DIM:(h + 1) * HEAD_DIM, ks], ones], axis=0)
                acc = acc * jnp.exp(m - m_new) + mm(vb, p)
                out.append((m_new, acc))
            return tuple(out)

        carry = []
        for h in range(heads_here):
            kp = jnp.concatenate([pre_ref[0, :, (h // 2) * 128:(h // 2 + 1) * 128], ep_ref[...]], axis=1)
            s = mm(kp, heads[h])
            m = jnp.max(s, axis=0, keepdims=True)
            p = jnp.exp(s - m).astype(jnp.bfloat16)
            vb = jnp.concatenate([vpt[h * HEAD_DIM:(h + 1) * HEAD_DIM], ones[:, :PP]], axis=0)
            carry.append((m, mm(vb, p)))
        carry = tuple(carry)
        if causal:
            carry = block(i, carry, True)
        carry = lax.fori_loop(lo_ref[i], hi_ref[i], lambda j, c: block(j, c, False), carry)
        outs = []
        for h in range(heads_here):
            m, acc = carry[h]
            total = acc[HEAD_DIM:HEAD_DIM + 1]
            lt_ref[h // 2, h % 2:h % 2 + 1, qs] = m + jnp.log(total)
            outs.append(acc[:HEAD_DIM] / total)
        ot = jnp.concatenate(outs, axis=0)
        ot_ref[:, qs] = ot.astype(jnp.bfloat16)
        o = ot.T.astype(jnp.bfloat16)
        store_part(o_parts, i, o)
        return 0

    lax.fori_loop(0, n_q, q_step, 0)


def store_part(parts, i, value):
    per_part = parts[0].shape[0] // BQ
    at = pl.ds(pl.multiple_of((i % per_part) * BQ, BQ), BQ)
    if len(parts) == 1:
        parts[0][at, :] = value
        return
    own = i // per_part == lax.axis_index("c")

    @pl.when(own)
    def _():
        parts[0][at, :] = value

    @pl.when(jnp.logical_not(own))
    def _():
        parts[1][at, :] = value


def attend_fwd(qs, ks, vs, cols, masks, prefix, lo, hi, causal):
    ek, eq, ep = masks
    n = len(qs)
    q_len, m_len = qs[0][0].shape[0], ks[0][0].shape[0]
    seq, mem = q_len * n, m_len * n
    wd = min(HEAD_DIM * HEADS_FWD, cols)
    steps = cols // wd
    in_specs, operands = [], []
    for group, length in ((qs, q_len), (ks, m_len), (vs, m_len)):
        for array, at in group:
            in_specs.append(pl.BlockSpec((length, wd), partial(lambda at, p, *_: (0, at * steps + p), at)))
            operands.append(array)
    in_specs += [
        pl.BlockSpec((mem, 128), lambda p, *_: (0, 0)),
        pl.BlockSpec((128, seq), lambda p, *_: (0, 0)),
        pl.BlockSpec((2, PP, wd), lambda p, *_: (0, 0, p)),
        pl.BlockSpec((PP, 128), lambda p, *_: (0, 0)),
    ]
    grid_spec = pltpu.PrefetchScalarGridSpec(
        num_scalar_prefetch=2,
        grid=(steps,),
        in_specs=in_specs,
        out_specs=[pl.BlockSpec((q_len, wd), lambda p, *_: (0, p))] * n
        + [
            pl.BlockSpec((wd, seq), lambda p, *_: (p, 0)),
            pl.BlockSpec((wd // 128, 2, seq), lambda p, *_: (p, 0, 0)),
        ],
        scratch_shapes=[
            pltpu.VMEM((wd, seq), jnp.bfloat16),
            pltpu.VMEM((wd, mem), jnp.bfloat16),
            pltpu.VMEM((wd // 128, mem, 256), jnp.bfloat16),
        ],
    )
    result = pl.pallas_call(
        functools.partial(fwd_kernel, causal, n),
        grid_spec=grid_spec,
        out_shape=[jax.ShapeDtypeStruct((q_len, cols), jnp.bfloat16)] * n
        + [
            jax.ShapeDtypeStruct((cols, seq), jnp.bfloat16),
            jax.ShapeDtypeStruct((cols // 128, 2, seq), jnp.float32),
        ],
        compiler_params=pltpu.CompilerParams(vmem_limit_bytes=56 * MIB),
        cost_estimate=pl.CostEstimate(
            flops=8 * seq * mem * cols, bytes_accessed=12 * MIB, transcendentals=seq * mem * cols // 256
        ),
        name="attend_fwd_self" if causal else "attend_fwd_cross",
    )(lo, hi, *operands, ek, eq, prefix, ep)
    return result[:n], result[n], result[n + 1]


def bwd_kernel(causal, n_parts, lo_ref, hi_ref, *refs):
    q_parts, k_parts, v_parts, g_parts = (refs[t * n_parts:(t + 1) * n_parts] for t in range(4))
    ot_ref, lt_ref, ek_ref, eq_ref, pre_ref, ep_ref = refs[4 * n_parts:4 * n_parts + 6]
    dq_parts = refs[4 * n_parts + 6:5 * n_parts + 6]
    dkv_parts = refs[5 * n_parts + 6:6 * n_parts + 6]
    dp_ref, qt, gt, kt, ke, vv, qm, gm, dk, dv, delta = refs[6 * n_parts + 6:]
    seq = qt.shape[1]
    q_len, m_len = q_parts[0].shape[0], k_parts[0].shape[0]
    width = q_parts[0].shape[1]
    n_pairs = width // 128
    heads_here = width // HEAD_DIM
    n_q = seq // BQ
    lane = lax.broadcasted_iota(jnp.int32, (1, width), 1)
    first = lane % 128 < HEAD_DIM
    zero = jnp.zeros((), jnp.bfloat16)

    for q_ref, g_ref, at in zip(q_parts, g_parts, part_offsets(n_parts, q_len)):
        here = pl.ds(at, q_len)
        q_all = q_ref[...] * jnp.bfloat16(0.125)
        g_all = g_ref[...]
        qt[:, here] = q_all.T
        g_turned = g_all.T
        gt[:, here] = g_turned
        qm[0, here, :] = jnp.where(first, q_all, zero)
        qm[1, here, :] = jnp.where(first, zero, q_all)
        gm[0, here, :] = jnp.where(first, g_all, zero)
        gm[1, here, :] = jnp.where(first, zero, g_all)
        prod = g_turned.astype(jnp.float32) * ot_ref[:, here].astype(jnp.float32)
        for h in range(heads_here):
            delta[h:h + 1, here] = jnp.sum(prod[h * HEAD_DIM:(h + 1) * HEAD_DIM], axis=0, keepdims=True)
    for k_ref, v_ref, at in zip(k_parts, v_parts, part_offsets(n_parts, m_len)):
        here = pl.ds(at, m_len)
        kt[:, here] = k_ref[...].T
        vv[here, :] = v_ref[...]
        for p in range(n_pairs):
            ke[p, here, :128] = k_ref[:, p * 128:(p + 1) * 128]
    for p in range(n_pairs):
        ke[p, :, 128:] = ek_ref[...]
    dk[...] = jnp.zeros_like(dk)
    dv[...] = jnp.zeros_like(dv)
    dp_ref[...] = jnp.zeros_like(dp_ref)
    kpt = pre_ref[0].T

    def q_step(i, _):
        qs = pl.ds(pl.multiple_of(i * BQ, BQ), BQ)
        eq = eq_ref[:, qs]
        q_heads, g_heads = [], []
        for p in range(n_pairs):
            q_heads += [jnp.concatenate([r, eq], axis=0) for r in pair_rows(qt[p * 128:(p + 1) * 128, qs])]
            g_heads += pair_rows(gt[p * 128:(p + 1) * 128, qs])
        lts = [lt_ref[h // 2, h % 2:h % 2 + 1, qs] for h in range(heads_here)]
        dls = [delta[h:h + 1, qs] for h in range(heads_here)]

        def grads(s, dp, h, diag):
            if diag:
                kk = lax.broadcasted_iota(jnp.int32, s.shape, 0)
                qq = lax.broadcasted_iota(jnp.int32, s.shape, 1)
                s = jnp.where(kk <= qq, s, NEG)
            p = jnp.exp(s - lts[h])
            ds = (p * (dp - dls[h])).astype(jnp.bfloat16)
            return p.astype(jnp.bfloat16), ds

        def block(j, carry, diag):
            ks = pl.ds(pl.multiple_of(j * BK, BK), BK)
            out, both = [], []
            for h in range(heads_here):
                c = (h // 2) * 128
                both.append((mm(ke[h // 2, ks, :], q_heads[h]), mm(vv[ks, c:c + 128], g_heads[h])))
            for pr in range(n_pairs):
                c = pr * 128
                dkb = dk[ks, c:c + 128]
                dvb = dv[ks, c:c + 128]
                for h in (2 * pr, 2 * pr + 1):
                    p, ds = grads(*both[h], h, diag)
                    dvb += mm(p, gm[h % 2, qs, c:c + 128])
                    dkb += mm(ds, qm[h % 2, qs, c:c + 128])
                    out.append(carry[h] + mm(kt[h * HEAD_DIM:(h + 1) * HEAD_DIM, ks], ds))
                dk[ks, c:c + 128] = dkb
                dv[ks, c:c + 128] = dvb
            return tuple(out)

        carry = []
        for h in range(heads_here):
            c = (h // 2) * 128
            kp = jnp.concatenate([pre_ref[0, :, c:c + 128], ep_ref[...]], axis=1)
            p, ds = grads(mm(kp, q_heads[h]), mm(pre_ref[1, :, c:c + 128], g_heads[h]), h, False)
            dp_ref[0, :, c:c + 128] += mm(ds, qm[h % 2, qs, c:c + 128])
            dp_ref[1, :, c:c + 128] += mm(p, gm[h % 2, qs, c:c + 128])
            carry.append(mm(kpt[h * HEAD_DIM:(h + 1) * HEAD_DIM], ds))
        carry = tuple(carry)
        if causal:
            carry = block(i, carry, True)
        carry = lax.fori_loop(lo_ref[i], hi_ref[i], lambda j, c: block(j, c, False), carry)
        dq = jnp.concatenate(carry, axis=0) * 0.125
        store_part(dq_parts, i, dq.T.astype(jnp.bfloat16))
        return 0

    lax.fori_loop(0, n_q, q_step, 0)
    for dkv_ref, at in zip(dkv_parts, part_offsets(n_parts, m_len)):
        here = pl.ds(at, m_len)
        dkv_ref[0] = dk[here, :].astype(jnp.bfloat16)
        dkv_ref[1] = dv[here, :].astype(jnp.bfloat16)


def attend_bwd(qs, ks, vs, gs, cols, ot, lt, masks, prefix, lo, hi, causal):
    ek, eq, ep = masks
    n = len(qs)
    q_len, m_len = qs[0][0].shape[0], ks[0][0].shape[0]
    seq, mem = q_len * n, m_len * n
    wd = min(HEAD_DIM * HEADS_BWD, cols)
    steps = cols // wd
    in_specs, operands = [], []
    for group, length in ((qs, q_len), (ks, m_len), (vs, m_len), (gs, q_len)):
        for array, at in group:
            in_specs.append(pl.BlockSpec((length, wd), partial(lambda at, p, *_: (0, at * steps + p), at)))
            operands.append(array)
    in_specs += [
        pl.BlockSpec((wd, seq), lambda p, *_: (p, 0)),
        pl.BlockSpec((wd // 128, 2, seq), lambda p, *_: (p, 0, 0)),
        pl.BlockSpec((mem, 128), lambda p, *_: (0, 0)),
        pl.BlockSpec((128, seq), lambda p, *_: (0, 0)),
        pl.BlockSpec((2, PP, wd), lambda p, *_: (0, 0, p)),
        pl.BlockSpec((PP, 128), lambda p, *_: (0, 0)),
    ]
    grid_spec = pltpu.PrefetchScalarGridSpec(
        num_scalar_prefetch=2,
        grid=(steps,),
        in_specs=in_specs,
        out_specs=[pl.BlockSpec((q_len, wd), lambda p, *_: (0, p))] * n
        + [pl.BlockSpec((2, m_len, wd), lambda p, *_: (0, 0, p))] * n
        + [pl.BlockSpec((2, PP, wd), lambda p, *_: (0, 0, p))],
        scratch_shapes=[
            pltpu.VMEM((wd, seq), jnp.bfloat16),
            pltpu.VMEM((wd, seq), jnp.bfloat16),
            pltpu.VMEM((wd, mem), jnp.bfloat16),
            pltpu.VMEM((wd // 128, mem, 256), jnp.bfloat16),
            pltpu.VMEM((mem, wd), jnp.bfloat16),
            pltpu.VMEM((2, seq, wd), jnp.bfloat16),
            pltpu.VMEM((2, seq, wd), jnp.bfloat16),
            pltpu.VMEM((mem, wd), jnp.float32),
            pltpu.VMEM((mem, wd), jnp.float32),
            pltpu.VMEM((8, seq), jnp.float32),
        ],
    )
    result = pl.pallas_call(
        functools.partial(bwd_kernel, causal, n),
        grid_spec=grid_spec,
        out_shape=[jax.ShapeDtypeStruct((q_len, cols), jnp.bfloat16)] * n
        + [jax.ShapeDtypeStruct((2, m_len, cols), jnp.bfloat16)] * n
        + [jax.ShapeDtypeStruct((2, PP, cols), jnp.float32)],
        compiler_params=pltpu.CompilerParams(vmem_limit_bytes=56 * MIB),
        cost_estimate=pl.CostEstimate(
            flops=12 * seq * mem * cols, bytes_accessed=20 * MIB, transcendentals=seq * mem * cols // 256
        ),
        name="attend_bwd_self" if causal else "attend_bwd_cross",
    )(lo, hi, *operands, ot, lt, ek, eq, prefix, ep)
    return result[:n], result[n:2 * n], result[2 * n]


def ranges(dec_seg, mem_seg, causal):
    seq = dec_seg.shape[0]
    blocks = dec_seg.reshape(seq // BQ, BQ)
    low, high = blocks[:, 0], blocks[:, -1]
    lo = jnp.sum((mem_seg[None, :] < low[:, None]).astype(jnp.int32), axis=1) // BK
    if causal:
        hi = jnp.arange(seq // BQ, dtype=jnp.int32)
    else:
        hi = (jnp.sum((mem_seg[None, :] <= high[:, None]).astype(jnp.int32), axis=1) + BK - 1) // BK
    return lo, hi


def mask_columns(dec_seg, mem_seg, prefix_count):
    lane = jnp.arange(128, dtype=jnp.int32)
    row = lane[:, None]
    ek = (mem_seg[:, None] == lane[None, :]).astype(jnp.bfloat16)
    differ = jnp.logical_and(row < DOCS, row != dec_seg[None, :])
    eq = jnp.where(jnp.logical_or(differ, row == DOCS), NEG, 0.0).astype(jnp.bfloat16)
    padding = jnp.arange(PP, dtype=jnp.int32)[:, None] >= prefix_count
    ep = jnp.logical_and(padding, lane[None, :] == DOCS).astype(jnp.bfloat16)
    return ek, eq, ep


def normalize(v):
    centered = v - jnp.mean(v, axis=-1, keepdims=True)
    r = lax.rsqrt(jnp.mean(centered * centered, axis=-1, keepdims=True) + 1e-05)
    return centered * r, r


def norm_back(n, r, gain, upstream):
    u = upstream * gain
    return r * (u - jnp.mean(u, axis=-1, keepdims=True) - n * jnp.mean(u * n, axis=-1, keepdims=True))


def gelu_parts(v):
    chance = 0.5 * (1.0 + lax.erf(v * math.sqrt(0.5)))
    slope = chance + v * (jnp.exp(-0.5 * v * v) * (1.0 / math.sqrt(2.0 * math.pi)))
    return v * chance, slope


def low(v):
    return v.astype(jnp.bfloat16)


def place_halves(own, other, held, sems, at):
    x = lax.axis_index("x")
    return [
        pltpu.make_async_copy(own, held.at[x], sems.at[at]),
        pltpu.make_async_copy(other, held.at[1 - x], sems.at[at + 1]),
    ]


def on_first(copies, act):
    @pl.when(pl.program_id(0) == 0)
    def _():
        for copy in copies:
            getattr(copy, act)()


def after_self_kernel(own_ref, par_ref, tok_ref, gains_ref, so_own, so_oth, cq_own, cq_oth,
                      first_ref, q_own_ref, q_par_ref, so, cq, sems):
    core = lax.axis_index("c")
    so_copies = place_halves(so_own, so_oth, so, sems, 0)
    cq_copies = place_halves(cq_own, cq_oth, cq, sems, 2)
    on_first(so_copies + cq_copies, "start")
    on_first(so_copies, "wait")
    total = tok_ref[...].astype(jnp.float32) + (mm(own_ref[...], so[core]) + mm(par_ref[...], so[1 - core]))
    first = low(total)
    first_ref[...] = first
    n, _ = normalize(first.astype(jnp.float32))
    normed = low(n * gains_ref[0:1, :])
    on_first(cq_copies, "wait")
    q_own_ref[...] = low(mm(normed, cq[core]))
    q_par_ref[...] = low(mm(normed, cq[1 - core]))


def rows_spec(width):
    return pl.BlockSpec((BT, width), lambda i: (i, 0))


ANY = pl.BlockSpec(memory_space=pl.ANY)


def after_self(own, par, tokens, gains, so_own, so_oth, cq_own, cq_oth):
    rows, d = tokens.shape
    half = d // 2
    return pl.pallas_call(
        after_self_kernel,
        grid=(rows // BT,),
        in_specs=[rows_spec(half), rows_spec(half), rows_spec(d), pl.BlockSpec((3, d), lambda i: (0, 0)), ANY, ANY, ANY, ANY],
        out_specs=[rows_spec(d), rows_spec(half), rows_spec(half)],
        out_shape=[
            jax.ShapeDtypeStruct((rows, d), jnp.bfloat16),
            jax.ShapeDtypeStruct((rows, half), jnp.bfloat16),
            jax.ShapeDtypeStruct((rows, half), jnp.bfloat16),
        ],
        scratch_shapes=[
            pltpu.VMEM((2, half, d), jnp.bfloat16),
            pltpu.VMEM((2, d, half), jnp.bfloat16),
            pltpu.SemaphoreType.DMA((4,)),
        ],
        compiler_params=pltpu.CompilerParams(vmem_limit_bytes=40 * MIB),
        cost_estimate=pl.CostEstimate(flops=4 * rows * d * d, bytes_accessed=12 * MIB, transcendentals=0),
        name="after_self",
    )(own, par, tokens, gains, so_own, so_oth, cq_own, cq_oth)


CHUNK = 512


def ffn_kernel(own_ref, par_ref, first_ref, cot_ref, gains_ref, down_ref, up_ref,
               co_own, co_oth, in_own, in_oth, out_own, out_oth,
               keep_ref, send_ref, gsec_ref, g_own_ref, g_par_ref, adapt_ref,
               co, w_in, w_out, slopes, acc, full, sems):
    core = lax.axis_index("c")
    x = lax.axis_index("x")
    half = keep_ref.shape[1]
    hidden_half = w_in.shape[2]
    chunks = 2 * hidden_half // CHUNK
    co_copies = place_halves(co_own, co_oth, co, sems, 0)
    in_copies = place_halves(in_own, in_oth, w_in, sems, 2)
    out_copies = place_halves(out_own, out_oth, w_out, sems, 4)
    on_first(co_copies + in_copies + out_copies, "start")

    @pl.when(pl.program_id(0) == 0)
    def _():
        adapt_ref[...] = jnp.zeros_like(adapt_ref)

    n_one, _ = normalize(first_ref[...].astype(jnp.float32))
    on_first(co_copies, "wait")
    cross = mm(own_ref[...], co[core]) + mm(par_ref[...], co[1 - core])
    second = low(n_one * gains_ref[0:1, :] + cross)
    n_two, r_two = normalize(second.astype(jnp.float32))
    normed_two = n_two * gains_ref[1:2, :]
    normed_low = low(normed_two)
    bottle_pre = mm(normed_low, down_ref[...])
    bottle, bottle_slope = gelu_parts(bottle_pre)
    bottle = low(bottle)
    acc[...] = normed_two + 4.0 * mm(bottle, up_ref[...])
    on_first(in_copies, "wait")
    on_first(out_copies, "wait")

    def up_step(t, _):
        which = t // (hidden_half // CHUNK)
        at = pl.ds(pl.multiple_of((t % (hidden_half // CHUNK)) * CHUNK, CHUNK), CHUNK)
        pre = mm(normed_low, w_in[which, :, at])
        hidden, slope = gelu_parts(pre)
        slopes[t] = slope
        acc[...] += mm(low(hidden), w_out[which, at, :])
        return 0

    lax.fori_loop(0, chunks, up_step, 0, unroll=2)
    third = low(acc[...])
    n_three, r_three = normalize(third.astype(jnp.float32))
    gain_three = gains_ref[2:3, :]
    full[...] = low(n_three * gain_three)
    keep_ref[...] = full[:, pl.ds(pl.multiple_of(x * half, half), half)]
    send_ref[...] = full[:, pl.ds(pl.multiple_of((1 - x) * half, half), half)]

    grad_three = norm_back(n_three, r_three, gain_three, cot_ref[...].astype(jnp.float32))
    branch = low(grad_three)
    adapted = low(4.0 * branch.astype(jnp.float32))
    bottle_grad = low(mm_nt(adapted, up_ref[...]) * bottle_slope)
    adapt_ref[0] += mm_tn(bottle_grad, normed_low)
    adapt_ref[1] += mm_tn(bottle, adapted)
    acc[...] = grad_three + mm_nt(bottle_grad, down_ref[...])

    def down_step(t, _):
        which = t // (hidden_half // CHUNK)
        at = pl.ds(pl.multiple_of((t % (hidden_half // CHUNK)) * CHUNK, CHUNK), CHUNK)
        grad_pre = low(mm_nt(branch, w_out[which, at, :]) * slopes[t])
        acc[...] += mm_nt(grad_pre, w_in[which, :, at])
        return 0

    lax.fori_loop(0, chunks, down_step, 0, unroll=2)
    grad_two = low(acc[...]).astype(jnp.float32)
    grad_second = norm_back(n_two, r_two, gains_ref[1:2, :], grad_two)
    gsec_ref[...] = grad_second
    second_low = low(grad_second)
    g_own_ref[...] = low(mm_nt(second_low, co[core]))
    g_par_ref[...] = low(mm_nt(second_low, co[1 - core]))


def ffn_both_ways(own, par, first, cot, gains, down, up, co_own, co_oth, in_own, in_oth, out_own, out_oth):
    rows, d = first.shape
    half = d // 2
    hidden_half = in_own.shape[1]
    bottleneck = down.shape[1]
    whole = lambda shape: pl.BlockSpec(shape, lambda i: (0,) * len(shape))
    flops = 2 * rows * d * (8 * hidden_half + 6 * bottleneck + 2 * d)
    return pl.pallas_call(
        ffn_kernel,
        grid=(rows // BT,),
        in_specs=[
            rows_spec(half), rows_spec(half), rows_spec(d), rows_spec(d),
            whole((3, d)), whole((d, bottleneck)), whole((bottleneck, d)),
            ANY, ANY, ANY, ANY, ANY, ANY,
        ],
        out_specs=[
            rows_spec(half), rows_spec(half), rows_spec(d), rows_spec(half), rows_spec(half),
            whole((2, bottleneck, d)),
        ],
        out_shape=[
            jax.ShapeDtypeStruct((rows, half), jnp.bfloat16),
            jax.ShapeDtypeStruct((rows, half), jnp.bfloat16),
            jax.ShapeDtypeStruct((rows, d), jnp.float32),
            jax.ShapeDtypeStruct((rows, half), jnp.bfloat16),
            jax.ShapeDtypeStruct((rows, half), jnp.bfloat16),
            jax.ShapeDtypeStruct((2, bottleneck, d), jnp.float32),
        ],
        scratch_shapes=[
            pltpu.VMEM((2, half, d), jnp.bfloat16),
            pltpu.VMEM((2, d, hidden_half), jnp.bfloat16),
            pltpu.VMEM((2, hidden_half, d), jnp.bfloat16),
            pltpu.VMEM((2 * hidden_half // CHUNK, BT, CHUNK), jnp.float32),
            pltpu.VMEM((BT, d), jnp.float32),
            pltpu.VMEM((BT, d), jnp.bfloat16),
            pltpu.SemaphoreType.DMA((6,)),
        ],
        compiler_params=pltpu.CompilerParams(vmem_limit_bytes=58 * MIB),
        cost_estimate=pl.CostEstimate(flops=flops, bytes_accessed=48 * MIB, transcendentals=0),
        name="ffn_both_ways",
    )(own, par, first, cot, gains, down, up, co_own, co_oth, in_own, in_oth, out_own, out_oth)


def before_self_kernel(gsec_ref, own_ref, par_ref, first_ref, gains_ref, so_own, so_oth, cq_own, cq_oth,
                       gfirst_ref, g_own_ref, g_par_ref, so, cq, sems):
    core = lax.axis_index("c")
    so_copies = place_halves(so_own, so_oth, so, sems, 0)
    cq_copies = place_halves(cq_own, cq_oth, cq, sems, 2)
    on_first(cq_copies + so_copies, "start")
    on_first(cq_copies, "wait")
    grad_one = low(gsec_ref[...] + (mm_nt(own_ref[...], cq[core]) + mm_nt(par_ref[...], cq[1 - core])))
    n, r = normalize(first_ref[...].astype(jnp.float32))
    grad_first = norm_back(n, r, gains_ref[0:1, :], grad_one.astype(jnp.float32))
    gfirst_ref[...] = grad_first
    first_low = low(grad_first)
    on_first(so_copies, "wait")
    g_own_ref[...] = low(mm_nt(first_low, so[core]))
    g_par_ref[...] = low(mm_nt(first_low, so[1 - core]))


def before_self(gsec, own, par, first, gains, so_own, so_oth, cq_own, cq_oth):
    rows, d = first.shape
    half = d // 2
    return pl.pallas_call(
        before_self_kernel,
        grid=(rows // BT,),
        in_specs=[
            rows_spec(d), rows_spec(half), rows_spec(half), rows_spec(d), pl.BlockSpec((3, d), lambda i: (0, 0)),
            ANY, ANY, ANY, ANY,
        ],
        out_specs=[rows_spec(d), rows_spec(half), rows_spec(half)],
        out_shape=[
            jax.ShapeDtypeStruct((rows, d), jnp.float32),
            jax.ShapeDtypeStruct((rows, half), jnp.bfloat16),
            jax.ShapeDtypeStruct((rows, half), jnp.bfloat16),
        ],
        scratch_shapes=[
            pltpu.VMEM((2, half, d), jnp.bfloat16),
            pltpu.VMEM((2, d, half), jnp.bfloat16),
            pltpu.SemaphoreType.DMA((4,)),
        ],
        compiler_params=pltpu.CompilerParams(vmem_limit_bytes=40 * MIB),
        cost_estimate=pl.CostEstimate(flops=4 * rows * d * d, bytes_accessed=16 * MIB, transcendentals=0),
        name="before_self",
    )(gsec, own, par, first, gains, so_own, so_oth, cq_own, cq_oth)


def swap(value, axis):
    return lax.ppermute(value, axis, SWAP)


def after(value, *others):
    return lax.optimization_barrier((value, *others))[0]


def other_half(weight):
    group = ("zl", "y", "c")
    count = math.prod(lax.axis_size(name) for name in group)
    piece = weight.shape[0] // count
    mine = lax.dynamic_slice_in_dim(weight, lax.axis_index(group) * piece, piece, 0)
    return swap(mine, "x")


def gather_half(piece):
    return lax.all_gather(piece, ("zl", "y", "c"), axis=0, tiled=True)


def bring_in(rows, agree):
    half = rows.shape[0] // 2
    core = lax.axis_index("c")
    keep = lax.dynamic_slice_in_dim(rows, core * half, half, 0)
    got = swap(lax.dynamic_slice_in_dim(rows, (1 - core) * half, half, 0), "c")
    return jnp.where(agree, keep, got), jnp.where(agree, got, keep)


def in_order(first_here, mine, others, axis):
    left = jnp.where(first_here, mine, others)
    right = jnp.where(first_here, others, mine)
    return jnp.concatenate([left, right], axis=axis)


def send_out(keep, send, agree):
    got = swap(send, "x")
    mine = jnp.where(agree, keep, got)
    passed = swap(jnp.where(agree, got, keep), "c")
    return in_order(lax.axis_index("c") == 0, mine, passed, 0)


def feature_halves(value):
    half = value.shape[1] // 2
    x = lax.axis_index("x")
    return lax.dynamic_slice_in_dim(value, x * half, half, 1), lax.dynamic_slice_in_dim(value, (1 - x) * half, half, 1)


def sum_over(value, axes):
    for name in axes:
        if lax.axis_size(name) == 2:
            value = value + swap(value, name)
        elif lax.axis_size(name) > 2:
            value = lax.psum(value, name)
    return value


def paired_device(
    tokens, memory, dec_segments, mem_segments, self_qkv, self_out, cross_q, cross_kv, cross_out, ffn_in, ffn_out,
    adapter_down, adapter_up, self_prefix, cross_prefix, gains, cotangent,
):
    x, core = lax.axis_index("x"), lax.axis_index("c")
    agree = x == core
    columns = tokens.shape[1]
    prefix_count = self_prefix.shape[1]

    qkv_flat = self_qkv.reshape(-1, columns)
    qkv_piece = other_half(qkv_flat)
    tok_mine, tok_send = bring_in(tokens, agree)
    mem_mine, mem_send = bring_in(memory, agree)
    cot_mine, cot_send = bring_in(cotangent, agree)
    segs = jnp.concatenate([dec_segments, mem_segments], axis=0)
    segs = jnp.where(agree, segs, swap(segs, "c"))
    dec_seg, mem_seg = segs[0], segs[1]
    prefixes = jnp.concatenate([self_prefix, cross_prefix], axis=0)
    prefixes = jnp.where(agree, prefixes, swap(prefixes, "x"))
    prefixes = jnp.pad(prefixes, ((0, 0), (0, PP - prefix_count), (0, 0)))
    self_pre, cross_pre = prefixes[:2], prefixes[2:]

    tok_got = swap(tok_send, "x")
    rows_own = in_order(x == 0, tok_mine, tok_got, 1)
    rows_par = swap(rows_own, "c")
    qkv_other = gather_half(qkv_piece)

    gate = tok_got
    mem_got = swap(after(mem_send, gate), "x")
    ckv_flat = cross_kv.reshape(-1, columns)
    ckv_other = gather_half(other_half(after(ckv_flat, gate)))
    so_other = gather_half(other_half(after(self_out, gate)))
    cq_other = gather_half(other_half(after(cross_q, gate)))
    co_other = gather_half(other_half(after(cross_out, gate)))

    self_masks = mask_columns(dec_seg, dec_seg, prefix_count)
    self_lo, self_hi = ranges(dec_seg, dec_seg, True)
    cross_masks = mask_columns(dec_seg, mem_seg, prefix_count)
    cross_lo, cross_hi = ranges(dec_seg, mem_seg, False)

    qkv_here = jnp.where(agree, qkv_flat, qkv_other).reshape(self_qkv.shape)
    qkv_there = jnp.where(agree, qkv_other, qkv_flat).reshape(self_qkv.shape)

    def project(rows, weights):
        return [low(mm(rows, weights[t])) for t in range(weights.shape[0])]

    own = project(rows_own, qkv_here)
    par = project(rows_par, qkv_here)
    self_q, self_k, self_v = ([(own[t], 0), (par[t], 0)] for t in range(3))
    self_o, self_ot, self_lt = attend_fwd(
        self_q, self_k, self_v, columns, self_masks, self_pre, self_lo, self_hi, True
    )
    heads_got = swap(self_o[1], "c")

    gate = (mem_got, heads_got)
    in_other = gather_half(other_half(after(ffn_in, *gate)))
    out_other = gather_half(other_half(after(ffn_out, *gate)))
    cot_got = swap(after(cot_send, *gate), "x")
    down_full = lax.all_gather(adapter_down.T, ("y", "c"), axis=0, tiled=True).T
    up_full = lax.all_gather(adapter_up, ("y", "c"), axis=0, tiled=True)

    mem_own = in_order(x == 0, mem_mine, mem_got, 1)
    mem_par = swap(mem_own, "c")
    ckv_here = jnp.where(agree, ckv_flat, ckv_other).reshape(cross_kv.shape)
    ckv_there = jnp.where(agree, ckv_other, ckv_flat).reshape(cross_kv.shape)
    first_sum, cq_own, cq_send = after_self(
        self_o[0], heads_got, rows_own, gains, self_out, so_other, cross_q, cq_other
    )
    cq_par = swap(cq_send, "c")
    own = project(mem_own, ckv_here)
    par = project(mem_par, ckv_here)
    cross_qp = [(cq_own, 0), (cq_par, 0)]
    cross_k, cross_v = ([(own[t], 0), (par[t], 0)] for t in range(2))
    cross_o, cross_ot, cross_lt = attend_fwd(
        cross_qp, cross_k, cross_v, columns, cross_masks, cross_pre, cross_lo, cross_hi, False
    )
    cross_got = swap(cross_o[1], "c")
    cot_own = in_order(x == 0, cot_mine, cot_got, 1)
    out_keep, out_send, grad_second, g_own, g_send, grad_adapt = ffn_both_ways(
        cross_o[0], cross_got, first_sum, cot_own, gains, down_full, up_full,
        cross_out, co_other, ffn_in, in_other, ffn_out, out_other,
    )
    g_par = swap(g_send, "c")
    output = send_out(out_keep, out_send, agree)

    n_y = lax.axis_size("y")
    block = grad_adapt.shape[1] // (2 * n_y)
    blocks = grad_adapt.reshape(2, n_y, 2, block, -1)
    part = lax.dynamic_index_in_dim(blocks, core, 2, False) + swap(
        lax.dynamic_index_in_dim(blocks, 1 - core, 2, False), "c"
    )
    if n_y == 2:
        y = lax.axis_index("y")
        part = lax.dynamic_index_in_dim(part, y, 1, False) + swap(
            low(lax.dynamic_index_in_dim(part, 1 - y, 1, False)), "y"
        ).astype(jnp.float32)
    else:
        part = lax.psum_scatter(part, "y", scatter_dimension=1, tiled=False)
    for name in ("zl", "zh", "x"):
        if lax.axis_size(name) == 2:
            part = low(part)
            part = part.astype(jnp.float32) + swap(part, name).astype(jnp.float32)
        elif lax.axis_size(name) > 2:
            part = lax.psum(part, name)
    grad_down, grad_up = part[0].T, part[1]

    cdq, cdkv, cross_dp = attend_bwd(
        cross_qp, cross_k, cross_v, [(g_own, 0), (g_par, 0)], columns, cross_ot, cross_lt,
        cross_masks, cross_pre, cross_lo, cross_hi, False,
    )
    cdq_got = swap(cdq[1], "c")
    cdkv_got = swap(cdkv[1], "c")
    grad_first, g_own, g_send = before_self(
        grad_second, cdq[0], cdq_got, first_sum, gains, self_out, so_other, cross_q, cq_other
    )
    g_par = swap(g_send, "c")

    def back(own, got, here, there):
        total = None
        for t in range(here.shape[0]):
            for rows, weight in ((own[t], here[t]), (got[t], there[t])):
                term = mm_nt(rows, weight)
                total = term if total is None else total + term
        return total

    grad_mem = low(back(cdkv[0], cdkv_got, ckv_here, ckv_there))
    mem_keep, mem_out = feature_halves(grad_mem)
    grad_memory = send_out(mem_keep, mem_out, agree).astype(jnp.float32)

    sdq, sdkv, self_dp = attend_bwd(
        self_q, self_k, self_v, [(g_own, 0), (g_par, 0)], columns, self_ot, self_lt,
        self_masks, self_pre, self_lo, self_hi, True,
    )
    sdq_got = swap(sdq[1], "c")
    sdkv_got = swap(sdkv[1], "c")
    grad_rows = low(
        grad_first
        + back(
            [sdq[0], sdkv[0][0], sdkv[0][1]], [sdq_got, sdkv_got[0], sdkv_got[1]], qkv_here, qkv_there
        )
    )
    tok_keep, tok_out = feature_halves(grad_rows)
    grad_tokens = send_out(tok_keep, tok_out, agree).astype(jnp.float32)

    def prefix_total(value):
        value = sum_over(value, ("zl", "y", "zh", "x"))
        return jnp.where(agree, value, swap(value, "c"))[:, :prefix_count]

    return (
        output, grad_tokens, grad_memory, prefix_total(self_dp), prefix_total(cross_dp), grad_down, grad_up,
    )


def norm_grad(gathered, gain, upstream):
    n, r = normalize(gathered.astype(jnp.float32))
    return norm_back(n, r, gain, upstream)


def wide_device(
    tokens, memory, dec_segments, mem_segments, self_qkv, self_out, cross_q, cross_kv, cross_out, ffn_in, ffn_out,
    adapter_down, adapter_up, self_prefix, cross_prefix, gains, cotangent,
):
    n_wide = lax.axis_size("wide")
    row_count, columns = tokens.shape
    own_start = lax.axis_index("wide") * columns
    block_size = row_count // n_wide
    block_start = lax.axis_index("wide") * block_size
    prefix_count = self_prefix.shape[1]
    dec_seg, mem_seg = dec_segments[0], mem_segments[0]

    def collect(values):
        return lax.all_gather(values, "wide", axis=1, tiled=True)

    def spread(term):
        return lax.psum_scatter(term, "wide", scatter_dimension=1, tiled=True)

    def own_columns(values):
        return lax.dynamic_slice_in_dim(values, own_start, columns, 1)

    def padded(prefix):
        return jnp.pad(prefix, ((0, 0), (0, PP - prefix_count), (0, 0)))

    self_masks = mask_columns(dec_seg, dec_seg, prefix_count)
    self_lo, self_hi = ranges(dec_seg, dec_seg, True)
    cross_masks = mask_columns(dec_seg, mem_seg, prefix_count)
    cross_lo, cross_hi = ranges(dec_seg, mem_seg, False)
    self_pre, cross_pre = padded(self_prefix), padded(cross_prefix)

    all_tokens, all_memory = collect(tokens), collect(memory)
    self_q, self_k, self_v = ([(low(mm(all_tokens, self_qkv[t])), 0)] for t in range(3))
    (self_heads,), self_ot, self_lt = attend_fwd(
        self_q, self_k, self_v, columns, self_masks, self_pre, self_lo, self_hi, True
    )
    first_sum = low(tokens.astype(jnp.float32) + spread(mm(self_heads, self_out)))
    gathered_one = collect(first_sum)
    normed_one = normalize(gathered_one.astype(jnp.float32))[0] * gains[0]
    cross_qp = [(low(mm(low(normed_one), cross_q)), 0)]
    cross_k, cross_v = ([(low(mm(all_memory, cross_kv[t])), 0)] for t in range(2))
    (cross_heads,), cross_ot, cross_lt = attend_fwd(
        cross_qp, cross_k, cross_v, columns, cross_masks, cross_pre, cross_lo, cross_hi, False
    )
    second_sum = low(own_columns(normed_one) + spread(mm(cross_heads, cross_out)))
    gathered_two = collect(second_sum)
    normed_two = normalize(gathered_two.astype(jnp.float32))[0] * gains[1]
    normed_low = low(normed_two)
    adapter_in = lax.dynamic_slice_in_dim(normed_low, block_start, block_size, 0)
    adapter_rows = lax.all_gather(adapter_in, "narrow", axis=0, tiled=True)
    bottle, bottle_slope = gelu_parts(mm(adapter_rows, adapter_down))
    bottle = low(bottle)
    adapted = lax.psum_scatter(low(mm(bottle, adapter_up)), "narrow", scatter_dimension=0, tiled=True)
    hidden, slope = gelu_parts(mm(normed_low, ffn_in))
    branch = mm(low(hidden), ffn_out)
    placed = lax.dynamic_slice_in_dim(branch, block_start, block_size, 0) + 4.0 * adapted.astype(jnp.float32)
    branch = lax.dynamic_update_slice_in_dim(branch, placed, block_start, 0)
    third_sum = low(own_columns(normed_two) + spread(branch))
    gathered_three = collect(third_sum)
    output = low(own_columns(normalize(gathered_three.astype(jnp.float32))[0] * gains[2]))
    grad_three = norm_grad(gathered_three, gains[2], collect(cotangent).astype(jnp.float32))
    grad_branch = low(grad_three)
    grad_pre = low(mm_nt(grad_branch, ffn_out) * slope)
    grad_normed = mm_nt(grad_pre, ffn_in)
    grad_adapted = low(4.0 * lax.dynamic_slice_in_dim(grad_branch, block_start, block_size, 0).astype(jnp.float32))
    grad_adapted = lax.all_gather(grad_adapted, "narrow", axis=0, tiled=True)
    bottle_grad = low(mm_nt(grad_adapted, adapter_up) * bottle_slope)
    grad_in = lax.psum_scatter(low(mm_nt(bottle_grad, adapter_down)), "narrow", scatter_dimension=0, tiled=True)
    placed = lax.dynamic_slice_in_dim(grad_normed, block_start, block_size, 0) + grad_in.astype(jnp.float32)
    grad_normed = lax.dynamic_update_slice_in_dim(grad_normed, placed, block_start, 0)
    grad_down, grad_up = lax.psum(
        (mm_tn(adapter_rows, bottle_grad), mm_tn(bottle, grad_adapted)), ("dp", "wide")
    )
    grad_two = collect(low(own_columns(grad_three) + spread(grad_normed))).astype(jnp.float32)
    grad_second = norm_grad(gathered_two, gains[1], grad_two)
    grad_cross = low(mm_nt(low(grad_second), cross_out))
    (cdq,), (cdkv,), cross_dp = attend_bwd(
        cross_qp, cross_k, cross_v, [(grad_cross, 0)], columns, cross_ot, cross_lt,
        cross_masks, cross_pre, cross_lo, cross_hi, False,
    )
    spread_one = spread(low(mm_nt(cdq, cross_q))).astype(jnp.float32)
    grad_memory = spread(low(mm_nt(cdkv[0], cross_kv[0]) + mm_nt(cdkv[1], cross_kv[1]))).astype(jnp.float32)
    grad_one = collect(low(own_columns(grad_second) + spread_one)).astype(jnp.float32)
    grad_first = norm_grad(gathered_one, gains[0], grad_one)
    grad_self = low(mm_nt(low(grad_first), self_out))
    (sdq,), (sdkv,), self_dp = attend_bwd(
        self_q, self_k, self_v, [(grad_self, 0)], columns, self_ot, self_lt,
        self_masks, self_pre, self_lo, self_hi, True,
    )
    grad_input = mm_nt(sdq, self_qkv[0]) + mm_nt(sdkv[0], self_qkv[1]) + mm_nt(sdkv[1], self_qkv[2])
    grad_tokens = own_columns(grad_first) + spread(grad_input)
    totals = lax.psum((low(self_dp), low(cross_dp)), ("dp", "narrow"))
    grad_self_prefix, grad_cross_prefix = (t.astype(jnp.float32)[:, :prefix_count] for t in totals)
    return (output, grad_tokens, grad_memory, grad_self_prefix, grad_cross_prefix, grad_down, grad_up)


def solution(mesh):
    dp, wide, narrow = (mesh.shape[name] for name in ("dp", "wide", "narrow"))
    if wide == 2 and narrow % 2 == 0:
        zl = 2 if dp % 2 == 0 else 1
        parts = Mesh(mesh.devices.reshape(dp // zl, zl, wide, narrow // 2, 2), ("zh", "zl", "x", "y", "c"))
        device, used = paired_device, parts
        rows, split, thin = ("zh", "zl", "y", "c"), "x", ("y", "c")
    else:
        device, used = wide_device, mesh
        rows, split, thin = ("dp", "narrow"), "wide", "narrow"
    return jax.shard_map(
        device,
        mesh=used,
        in_specs=(
            P(rows, split),
            P(rows, split),
            P(rows, None),
            P(rows, None),
            P(None, None, split),
            P(split, None),
            P(None, split),
            P(None, None, split),
            P(split, None),
            P(None, split),
            P(split, None),
            P(None, thin),
            P(thin, None),
            P(None, None, split),
            P(None, None, split),
            P(),
            P(rows, split),
        ),
        out_specs=(
            P(rows, split),
            P(rows, split),
            P(rows, split),
            P(None, None, split),
            P(None, None, split),
            P(None, thin),
            P(thin, None),
        ),
        check_vma=False,
    )
```

time: 3150 us -> 683 us (0.22)
  waiting for transfers between devices: 1260 us -> 132 us
  matrix products: 1140 us -> 63.7 us
  other arithmetic: 524 us -> 56.8 us
  Pallas kernels: 0 us -> 298 us
  local copies, waits for them, and re-layouts: 201 us -> 44.5 us
  starting transfers between devices: 1.45 us -> 68.3 us
    dot_general x131 -> x20, matrix products: 1140 us -> 63.7 us  [the longest x10 33.1 us: mm_nt(): lax.dot_general(a, b, (((1,), (1,)), ((), ())), preferred_element_type=jn...]
    reduce_scatter x9 -> x0, waiting for transfers between devices: 594 us -> none  [the longest x5 490 us: spread(): return lax.psum_scatter(term, 'wide', scatter_dimension=1, tiled=True)]
    all_gather x10 -> x9, waiting for transfers between devices: 532 us -> 0.03 us  [the longest x7 0.03 us: gather_half(): return lax.all_gather(piece, ('zl', 'y', 'c'), axis=0, tiled=True)]
    pallas_call x0 -> x7, Pallas kernels: none -> 298 us  [the longest x2 115 us: attend_bwd(): pl.pallas_call(functools.partial(bwd_kernel, causal, n), grid_spec=grid_s...]
    convert_element_type x26 -> x10, other arithmetic: 275 us -> 18.4 us  [the longest x4 9.12 us: low(): return v.astype(jnp.bfloat16)]
    reduce_sum x27 -> x1, other arithmetic: 156 us -> 0.23 us  [ranges(): jnp.sum((mem_seg[None, :] <= high[:, None]).astype(jnp.int32), axis=1) + BK]
    psum x2 -> x0, waiting for transfers between devices: 131 us -> none  [the longest x1 76.5 us: on_device(): grad_down, grad_up = lax.psum((local_down, local_up), ('dp', 'wide'))]
    ppermute x0 -> x47, waiting for transfers between devices: none -> 131 us  [swap(): return lax.ppermute(value, axis, SWAP)]
  transfers between devices with their start and end apart: 21 -> 56, of which waited for: 20 -> 18; matrix products, arithmetic and copies ran while one was open for 23% -> 21% of each run, Pallas kernels for 0% -> 32%
where the time goes in v1:
time: 683 us; the launch traced here: 679 us
  Pallas kernels  298 us (44%)
  waiting for transfers between devices  132 us (19%)
  starting transfers between devices  68.3 us (10%)
  matrix products  63.7 us (9%)
  other arithmetic  56.8 us (8%)
  local copies, waits for them, and re-layouts  44.5 us (7%)
  between operations  15 us (2%)
    ppermute x47, waiting for transfers between devices, swap(): return lax.ppermute(value, axis, SWAP)  131 us
    pallas_call x2, Pallas kernels, attend_bwd(): pl.pallas_call(functools.partial(bwd_kernel, causal, n), grid_spec=grid_s...  115 us
    pallas_call x2, Pallas kernels, attend_fwd(): pl.pallas_call(functools.partial(fwd_kernel, causal, n), grid_spec=grid_s...  85.6 us
    pallas_call x1, Pallas kernels, ffn_both_ways(): pl.pallas_call(ffn_kernel, grid=(rows // BT,), in_specs=[rows_spec(half),...  81 us
    ppermute x47, starting transfers between devices, swap(): return lax.ppermute(value, axis, SWAP)  67.5 us
    dot_general x10, matrix products, mm_nt(): lax.dot_general(a, b, (((1,), (1,)), ((), ())), preferred_element_type=jn...  33.1 us
    dot_general x10, matrix products, mm(): return jnp.dot(a, b, preferred_element_type=jnp.float32)  30.6 us
    unnamed x138, local copies, waits for them, and re-layouts  23.2 us
  transfers between devices with their start and end apart: 56, of which 18 were waited for; matrix products, arithmetic and copies ran while one was open for 21% of the time, Pallas kernels for 32%

profile of v1, /device:TPU:0, one launch (start us, length us, event | category | flops | bytes accessed | tf_op | source)
XLA Modules:
  0.0 678.5 jit_solution(18268292506698712770)
XLA Ops:
  8.4 3.0 collective-permute-start.3
  11.4 9.1 %collective-permute-done.3 = bf16[384,512]{1,0:T(8,128)(2,1)S(1)} collective-permute-done((bf16[384,512]{1,0:T(8,128)(2,1)S(1)}, bf16[384,512]{1,0:T(8,128)(2,1)S(1)}, u32[]{:S(2)}, u32[]{:S(2)}) %collective-permute-start.3) | collective-permute-done | bytes 393248 | tf_op jit(solution)/shard_map/ppermute | solution.py:624
  21.3 2.3 constant_dynamic-slice_fusion.13
  23.6 3.0 collective-permute-done.1
  26.6 2.5 broadcast_select_fusion.20
  29.6 25.0 %collective-permute-done.2 = bf16[1024,512]{1,0:T(8,128)(2,1)} collective-permute-done((bf16[1024,512]{1,0:T(8,128)(2,1)}, bf16[1024,512]{1,0:T(8,128)(2,1)}, u32[]{:S(2)}, u32[]{:S(2)}) %collective-permute-start.2) | collective-permute-done | bytes 1048608 | tf_op jit(solution)/shard_map/ppermute | solution.py:624
  56.7 6.6 collective-permute-done.12
  64.1 1.8 collective-permute-start.7
  65.9 3.2 collective-permute-done.7
  70.8 1.8 collective-permute-start.8
  72.6 3.2 collective-permute-done.8
  80.8 2.3 constant_dynamic-slice_fusion.9
  92.7 2.5 broadcast_select_fusion.18
  96.0 2.2 collective-permute-done.17
  99.1 5.3 broadcast_select_fusion
  104.4 2.2 convolution_convert_fusion.5.refs_4_
  106.6 2.3 convolution_convert_fusion.7.refs_2_
  108.9 2.2 convolution_convert_fusion.9.refs_0_
  111.1 3.8 convolution_convert_fusion.4.refs_5_
  114.9 3.8 convolution_convert_fusion.6.refs_3_
  118.8 3.8 convolution_convert_fusion.8.refs_1_
  123.2 40.6 %attend_fwd_self.1 = (bf16[1024,512]{1,0:T(8,128)(2,1)}, bf16[1024,512]{1,0:T(8,128)(2,1)}, bf16[512,2048]{1,0:T(8,128)(2,1)}, f32[4,2,2048]{2,1,0:T(2,128)}) custom-call(s32[8]{0:T(128)} %and_select_fusion.lo_ref, s32[8]{0:T(128)} %iota.40.hi_ref, bf16[1024,512]{1,0:T(8,128)(2,1)} %convolution_convert_fusion.9.refs_0_, ...), custom_call_target="tpu_custom_call" | custom-call | flops 17179869184 | bytes 12582912 | tf_op jit(solution)/shard_map/attend_fwd_self/pallas_call | solution.py:178
  163.8 2.9 collective-permute-done.6.par_ref
  168.7 2.3 collective-permute-start.18
  171.1 12.3 %collective-permute-done.18 = bf16[128,2048]{1,0:T(8,128)(2,1)} collective-permute-done((bf16[128,2048]{1,0:T(8,128)(2,1)S(1)}, bf16[128,2048]{1,0:T(8,128)(2,1)}, u32[]{:S(2)}, u32[]{:S(2)}) %collective-permute-start.18) | collective-permute-done | bytes 524320 | tf_op jit(solution)/shard_map/ppermute | solution.py:624
  184.8 1.8 collective-permute-start.19
  186.6 11.8 %collective-permute-done.19 = bf16[256,1024]{1,0:T(8,128)(2,1)} collective-permute-done((bf16[256,1024]{1,0:T(8,128)(2,1)S(1)}, bf16[256,1024]{1,0:T(8,128)(2,1)}, u32[]{:S(2)}, u32[]{:S(2)}) %collective-permute-start.19) | collective-permute-done | bytes 524320 | tf_op jit(solution)/shard_map/ppermute | solution.py:624
  208.7 4.1 broadcast_select_fusion.2
  214.0 2.2 convolution_convert_fusion.1.refs_4_
  222.4 7.2 %after_self.1 = (bf16[1024,1024]{1,0:T(8,128)(2,1)S(1)}, bf16[1024,512]{1,0:T(8,128)(2,1)S(1)}, bf16[1024,512]{1,0:T(8,128)(2,1)S(1)}) custom-call(bf16[1024,512]{1,0:T(8,128)(2,1)S(1)} %copy-done.16, bf16[1024,512]{1,0:T(8,128)(2,1)S(1)} %copy-done.8, bf16[1024,1024]{1,0:T(8,128)(2,1)S(1)} %pad_maximum_fusion.tok_ref, f32[3,1024]{1,0:T(4,128)S(1)} %copy-done.9, ...), custom_call_target="tpu_custom_call" | custom-call | flops 4294967296 | bytes 12582912 | tf_op jit(solution)/shard_map/after_self/pallas_call | solution.py:440
  229.8 2.3 convolution_convert_fusion.3.refs_2_
  232.1 3.9 convolution_convert_fusion.refs_5_
  236.0 4.0 convolution_convert_fusion.2.refs_3_
  242.4 45.0 %attend_fwd_cross.1 = (bf16[1024,512]{1,0:T(8,128)(2,1)}, bf16[1024,512]{1,0:T(8,128)(2,1)}, bf16[512,2048]{1,0:T(8,128)(2,1)}, f32[4,2,2048]{2,1,0:T(2,128)}) custom-call(s32[8]{0:T(128)} %get-tuple-element.128.lo_ref, s32[8]{0:T(128)} %get-tuple-element.127.hi_ref, bf16[1024,512]{1,0:T(8,128)(2,1)} %copy-done.15, bf16[1024,512]{1,0:T(8,128)(2,1)} %copy-done.59, ...), custom_call_target="tpu_custom_call" | custom-call | flops 17179869184 | bytes 12582912 | tf_op jit(solution)/shard_map/attend_fwd_cross/pallas_call | solution.py:178
  291.3 81.0 %ffn_both_ways.1 = (bf16[1024,512]{1,0:T(8,128)(2,1)}, bf16[1024,512]{1,0:T(8,128)(2,1)}, f32[1024,1024]{1,0:T(8,128)}, bf16[1024,512]{1,0:T(8,128)(2,1)}, bf16[...) custom-call(bf16[1024,512]{1,0:T(8,128)(2,1)} %get-tuple-element.53.own_ref, bf16[1024,512]{1,0:T(8,128)(2,1)} %copy-done.62, ...), custom_call_target="tpu_custom_call" | custom-call | flops 45097156608 | bytes 50331648 | tf_op jit(solution)/shard_map/ffn_both_ways/pallas_call | solution.py:544
  372.5 2.5 constant_dynamic-slice_fusion.1
  376.9 4.7 collective-permute-start.20
  381.6 59.7 %attend_bwd_cross.1 = (bf16[1024,512]{1,0:T(8,128)(2,1)}, bf16[1024,512]{1,0:T(8,128)(2,1)}, bf16[2,1024,512]{2,1,0:T(8,128)(2,1)}, bf16[2,1024,512]{2,1,0:T(8,128)(2,1)}, f32[2,32,512]{2,1,0:T(8,128)}) custom-call(s32[8]{0:T(128)} %get-tuple-element.128.lo_ref, s32[8]{0:T(128)} %get-tuple-element.127.hi_ref, bf16[1024,512]{1,0:T(8,128)(2,1)} %copy-done.15, ...), custom_call_target="tpu_custom_call" | custom-call | flops 25769803776 | bytes 20971520 | tf_op jit(solution)/shard_map/attend_bwd_cross/pallas_call | solution.py:339
  441.3 13.4 %collective-permute-start.37 = (f32[2,32,512]{2,1,0:T(8,128)}, f32[2,32,512]{2,1,0:T(8,128)S(1)}, u32[]{:S(2)}, u32[]{:S(2)}) collective-permute-start(f32[2,32,512]{2,1,0:T(8,128)} %get-tuple-element.81), channel_id=1, source_target_pairs={{0,8},{8,0},{1,9},{9,1},{2,10},{10,2},{3,11},{11,3},{4,12},{12,4},... | collective-permute-start | bytes 393224 | tf_op jit(solution)/shard_map/ppermute | solution.py:624
  455.2 3.2 collective-permute-done.37
  459.4 4.9 fusion.13
  464.4 15.1 %collective-permute-start.39 = (f32[2,32,512]{2,1,0:T(8,128)S(1)}, f32[2,32,512]{2,1,0:T(8,128)S(1)}, u32[]{:S(2)}, u32[]{:S(2)}) collective-permute-start(f32[2,32,512]{2,1,0:T(8,128)S(1)} %add.166), channel_id=1, source_target_pairs={{0,16},{16,0},{1,17},{17,1},{2,18},{18,2},{3,19},{19,3},{4,20},{20... | collective-permute-start | bytes 393224 | tf_op jit(solution)/shard_map/ppermute | solution.py:624
  480.9 4.6 collective-permute-done.39
  485.6 2.1 bitcast_add_fusion
  489.7 3.3 fusion.15
  493.2 9.3 %before_self.1 = (f32[1024,1024]{1,0:T(8,128)}, bf16[1024,512]{1,0:T(8,128)(2,1)S(1)}, bf16[1024,512]{1,0:T(8,128)(2,1)S(1)}) custom-call(f32[1024,1024]{1,0:T(8,128)} %get-tuple-element.62.gsec_ref, bf16[1024,512]{1,0:T(8,128)(2,1)S(1)} %copy-done.13, bf16[1024,512]{1,0:T(8,128)(2,1)S(1)} %collective-permute-done.23.par_ref, ...), custom_call_target="tpu_custom_call" | custom-call | flops 4294967296 | bytes 16777216 | tf_op jit(solution)/shard_map/before_self/pallas_call | solution.py:599
  506.3 10.9 %collective-permute-done.44 = bf16[2,128,1024]{2,1,0:T(8,128)(2,1)S(1)} collective-permute-done((bf16[2,128,1024]{2,1,0:T(8,128)(2,1)S(1)}, bf16[2,128,1024]{2,1,0:T(8,128)(2,1)S(1)}, u32[]{:S(2)}, u32[]{:S(2)}) %collective-permute-start.44) | collective-permute-done | bytes 524320 | tf_op jit(solution)/shard_map/ppermute | solution.py:624
  518.2 2.3 collective-permute-start.45
  520.5 4.5 fusion.4
  526.0 55.5 %attend_bwd_self.1 = (bf16[1024,512]{1,0:T(8,128)(2,1)}, bf16[1024,512]{1,0:T(8,128)(2,1)}, bf16[2,1024,512]{2,1,0:T(8,128)(2,1)}, bf16[2,1024,512]{2,1,0:T(8,128)(2,1)}, f32[2,32,512]{2,1,0:T(8,128)}) custom-call(s32[8]{0:T(128)} %and_select_fusion.lo_ref, s32[8]{0:T(128)} %iota.44.hi_ref, bf16[1024,512]{1,0:T(8,128)(2,1)} %convolution_convert_fusion.9.refs_0_, ...), custom_call_target="tpu_custom_call" | custom-call | flops 25769803776 | bytes 20971520 | tf_op jit(solution)/shard_map/attend_bwd_self/pallas_call | solution.py:339
  581.6 6.4 add_convert_fusion
  589.1 5.0 collective-permute-start.30
  596.9 2.7 collective-permute-done.32
  601.1 3.6 collective-permute-done.33
  605.4 3.3 fusion.10
  608.7 3.4 fusion.8
  612.1 3.3 fusion.6
  615.4 6.6 add_convert_fusion.1
  629.3 21.8 %collective-permute-done.35 = f32[2,32,512]{2,1,0:T(8,128)S(1)} collective-permute-done((f32[2,32,512]{2,1,0:T(8,128)S(1)}, f32[2,32,512]{2,1,0:T(8,128)S(1)}, u32[]{:S(2)}, u32[]{:S(2)}) %collective-permute-start.35) | collective-permute-done | bytes 131104 | tf_op jit(solution)/shard_map/ppermute | solution.py:624
  655.3 4.3 collective-permute-done.46
  660.8 2.0 copy.41
  664.7 2.6 maximum_convert_fusion.1
  667.3 1.8 broadcast_select_fusion.25
  669.1 2.6 maximum_convert_fusion
  (293 shorter events, 84.6 us)
Async XLA Ops:
  7.2 19.5 %copy-start.19 = (bf16[2048,512]{1,0:T(8,128)(2,1)S(1)}, bf16[2048,512]{1,0:T(8,128)(2,1)}, u32[]{:S(2)}) copy-start(bf16[2048,512]{1,0:T(8,128)(2,1)} %param.17) | copy-start | bytes 6291460
  7.2 91.9 %all-gather.10.cloned.1.call-start = ((), (), s32[]{:S(2)}) async-start(), calls=%async_computation | async-start | bytes 3538944 | tf_op jit(solution)/shard_map/all_gather | solution.py:640
  8.4 12.1 %collective-permute-start.3 = (bf16[384,512]{1,0:T(8,128)(2,1)S(1)}, bf16[384,512]{1,0:T(8,128)(2,1)S(1)}, u32[]{:S(2)}, u32[]{:S(2)}) collective-permute-start(bf16[384,512]{1,0:T(8,128)(2,1)S(1)} %constant_dynamic-slice_fusion.12), channel_id=1, source_target_pairs={{0,4},{4,0},{1,5},{5,1},{2,6},{6,2},{3,7},{7,3},{8,12},{12,8},{9,1... | collective-permute-start | bytes 1179656 | tf_op jit(solution)/shard_map/ppermute | solution.py:624
  21.3 187.4 %all-gather.16.cloned.1.call-start = ((), (), s32[]{:S(2)}) async-start(), calls=%async_computation.3 | async-start | bytes 2359296 | tf_op jit(solution)/shard_map/all_gather | solution.py:640
  23.6 40.5 %copy-start = (bf16[512,1024]{1,0:T(8,128)(2,1)S(1)}, bf16[512,1024]{1,0:T(8,128)(2,1)}, u32[]{:S(2)}) copy-start(bf16[512,1024]{1,0:T(8,128)(2,1)} %so_own.3) | copy-start | bytes 3145732
  23.6 3.0 collective-permute-start.1
  23.6 53.5 %copy-start.57 = (s32[1,2048]{1,0:T(1,128)S(1)}, s32[1,2048]{1,0:T(1,128)}, u32[]{:S(2)}) copy-start(s32[1,2048]{1,0:T(1,128)} %param.20) | copy-start | bytes 24580
  23.6 53.5 %copy-start.58 = (s32[1,2048]{1,0:T(1,128)S(1)}, s32[1,2048]{1,0:T(1,128)}, u32[]{:S(2)}) copy-start(s32[1,2048]{1,0:T(1,128)} %param.19) | copy-start | bytes 24580
  29.1 25.5 %collective-permute-start.2 = (bf16[1024,512]{1,0:T(8,128)(2,1)}, bf16[1024,512]{1,0:T(8,128)(2,1)}, u32[]{:S(2)}, u32[]{:S(2)}) collective-permute-start(bf16[1024,512]{1,0:T(8,128)(2,1)} %broadcast_select_fusion.20), channel_id=1, source_target_pairs={{0,4},{4,0},{1,5},{5,1},{2,6},{6,2},{3,7},{7,3},{8,12},{12,8},{9,1... | collective-permute-start | bytes 3145736 | tf_op jit(solution)/shard_map/ppermute | solution.py:624
  55.6 7.7 %collective-permute-start.12 = (bf16[256,512]{1,0:T(8,128)(2,1)S(1)}, bf16[256,512]{1,0:T(8,128)(2,1)S(1)}, u32[]{:S(2)}, u32[]{:S(2)}) collective-permute-start(bf16[256,512]{1,0:T(8,128)(2,1)S(1)} %constant_dynamic-slice_fusion.8), channel_id=1, source_target_pairs={{0,4},{4,0},{1,5},{5,1},{2,6},{6,2},{3,7},{7,3},{8,12},{12,8},{9,1... | collective-permute-start | bytes 786440 | tf_op jit(solution)/shard_map/ppermute | solution.py:624
  64.0 152.2 %all-gather.12.cloned.1.call-start = ((), (), s32[]{:S(2)}) async-start(), calls=%async_computation.1 | async-start | bytes 1179648 | tf_op jit(solution)/shard_map/all_gather | solution.py:640
  64.1 5.0 collective-permute-start.7
  69.8 146.4 %all-gather.14.cloned.1.call-start = ((), (), s32[]{:S(2)}) async-start(), calls=%async_computation.2 | async-start | bytes 1179648 | tf_op jit(solution)/shard_map/all_gather | solution.py:640
  70.8 5.0 collective-permute-start.8
  76.5 213.1 %all-gather.20.cloned.1.call-start = ((), (), s32[]{:S(2)}) async-start(), calls=%async_computation.5 | async-start | bytes 1310720 | tf_op jit(solution)/shard_map/all_gather | solution.py:738
  77.1 212.5 %all-gather.18.cloned.1.call-start = ((), (), s32[]{:S(2)}) async-start(), calls=%async_computation.4 | async-start | bytes 1310720 | tf_op jit(solution)/shard_map/all_gather | solution.py:737
  77.2 6.9 %collective-permute-start = (s32[2,2048]{1,0:T(2,128)S(1)}, s32[2,2048]{1,0:T(2,128)S(1)}, u32[]{:S(2)}, u32[]{:S(2)}) collective-permute-start(s32[2,2048]{1,0:T(2,128)S(1)} %pad_add_fusion), channel_id=1, source_target_pairs={{0,1},{1,0},{2,3},{3,2},{4,5},{5,4},{6,7},{7,6},{8,9},{9,8},{10,11... | collective-permute-start | bytes 49160 | tf_op jit(solution)/shard_map/ppermute | solution.py:624
  79.0 8.4 %collective-permute-start.5 = (bf16[4,30,512]{2,1,0:T(8,128)(2,1)S(1)}, bf16[4,30,512]{2,1,0:T(8,128)(2,1)S(1)}, u32[]{:S(2)}, u32[]{:S(2)}) collective-permute-start(bf16[4,30,512]{2,1,0:T(8,128)(2,1)S(1)} %copy_dynamic-update-slice_fusion), channel_id=1, source_target_pairs={{0,4},{4,0},{1,5},{5,1},{2,6},{6,2},{3,7},{7,3},{8,12},{12,8},{9,1... | collective-permute-start | bytes 368648 | tf_op jit(solution)/shard_map/ppermute | solution.py:624
  83.0 9.7 %collective-permute-start.10 = (bf16[1024,512]{1,0:T(8,128)(2,1)}, bf16[1024,512]{1,0:T(8,128)(2,1)}, u32[]{:S(2)}, u32[]{:S(2)}) collective-permute-start(bf16[1024,512]{1,0:T(8,128)(2,1)} %constant_dynamic-slice_fusion.9), channel_id=1, source_target_pairs={{0,1},{1,0},{2,3},{3,2},{4,5},{5,4},{6,7},{7,6},{8,9},{9,8},{10,11... | collective-permute-start | bytes 3145736 | tf_op jit(solution)/shard_map/ppermute | solution.py:624
  83.3 206.3 %all-gather.22.cloned.1.call-start = ((), (), s32[]{:S(2)}) async-start(), calls=%async_computation.6 | async-start | bytes 1179648 | tf_op jit(solution)/shard_map/all_gather | solution.py:640
  91.1 20.0 %collective-permute-start.4 = (bf16[1024,1024]{1,0:T(8,128)(2,1)S(1)}, bf16[1024,1024]{1,0:T(8,128)(2,1)}, u32[]{:S(2)}, u32[]{:S(2)}) collective-permute-start(bf16[1024,1024]{1,0:T(8,128)(2,1)S(1)} %pad_maximum_fusion.tok_ref), channel_id=1, source_target_pairs={{0,1},{1,0},{2,3},{3,2},{4,5},{5,4},{6,7},{7,6},{8,9},{9,8},{10,11... | collective-permute-start | bytes 6291464 | tf_op jit(solution)/shard_map/ppermute | solution.py:624
  92.6 5.6 collective-permute-start.17
  95.2 68.5 %collective-permute-start.11 = (bf16[1024,512]{1,0:T(8,128)(2,1)}, bf16[1024,512]{1,0:T(8,128)(2,1)}, u32[]{:S(2)}, u32[]{:S(2)}) collective-permute-start(bf16[1024,512]{1,0:T(8,128)(2,1)} %broadcast_select_fusion.18), channel_id=1, source_target_pairs={{0,4},{4,0},{1,5},{5,1},{2,6},{6,2},{3,7},{7,3},{8,12},{12,8},{9,1... | collective-permute-start | bytes 3145736 | tf_op jit(solution)/shard_map/ppermute | solution.py:624
  98.8 191.4 %all-gather.24.cloned.1.call-start = ((), (), s32[]{:S(2)}) async-start(), calls=%async_computation.7 | async-start | bytes 4718592 | tf_op jit(solution)/shard_map/all_gather | solution.py:640
  163.8 2.9 collective-permute-start.6
  168.7 14.7 %collective-permute-start.18 = (bf16[128,2048]{1,0:T(8,128)(2,1)S(1)}, bf16[128,2048]{1,0:T(8,128)(2,1)}, u32[]{:S(2)}, u32[]{:S(2)}) collective-permute-start(bf16[128,2048]{1,0:T(8,128)(2,1)S(1)} %constant_dynamic-slice_fusion.5), channel_id=1, source_target_pairs={{0,4},{4,0},{1,5},{5,1},{2,6},{6,2},{3,7},{7,3},{8,12},{12,8},{9,1... | collective-permute-start | bytes 1572872 | tf_op jit(solution)/shard_map/ppermute | solution.py:624
  183.4 106.9 %all-gather.26.cloned.1.call-start = ((), (), s32[]{:S(2)}) async-start(), calls=%async_computation.8 | async-start | bytes 4718592 | tf_op jit(solution)/shard_map/all_gather | solution.py:640
  184.8 13.6 %collective-permute-start.19 = (bf16[256,1024]{1,0:T(8,128)(2,1)S(1)}, bf16[256,1024]{1,0:T(8,128)(2,1)}, u32[]{:S(2)}, u32[]{:S(2)}) collective-permute-start(bf16[256,1024]{1,0:T(8,128)(2,1)S(1)} %constant_dynamic-slice_fusion.4), channel_id=1, source_target_pairs={{0,4},{4,0},{1,5},{5,1},{2,6},{6,2},{3,7},{7,3},{8,12},{12,8},{9,1... | collective-permute-start | bytes 1572872 | tf_op jit(solution)/shard_map/ppermute | solution.py:624
  199.9 6.5 collective-permute-start.15
  205.0 27.1 %collective-permute-start.13 = (bf16[1024,1024]{1,0:T(8,128)(2,1)}, bf16[1024,1024]{1,0:T(8,128)(2,1)}, u32[]{:S(2)}, u32[]{:S(2)}) collective-permute-start(bf16[1024,1024]{1,0:T(8,128)(2,1)} %pad_maximum_fusion.1), channel_id=1, source_target_pairs={{0,1},{1,0},{2,3},{3,2},{4,5},{5,4},{6,7},{7,6},{8,9},{9,8},{10,11... | collective-permute-start | bytes 6291464 | tf_op jit(solution)/shard_map/ppermute | solution.py:624
  229.7 11.8 %collective-permute-start.9 = (bf16[1024,512]{1,0:T(8,128)(2,1)S(1)}, bf16[1024,512]{1,0:T(8,128)(2,1)S(1)}, u32[]{:S(2)}, u32[]{:S(2)}) collective-permute-start(bf16[1024,512]{1,0:T(8,128)(2,1)S(1)} %get-tuple-element.50), channel_id=1, source_target_pairs={{0,1},{1,0},{2,3},{3,2},{4,5},{5,4},{6,7},{7,6},{8,9},{9,8},{10,11... | collective-permute-start | bytes 3145736 | tf_op jit(solution)/shard_map/ppermute | solution.py:624
  240.0 47.5 %collective-permute-start.16 = (bf16[1024,512]{1,0:T(8,128)(2,1)S(1)}, bf16[1024,512]{1,0:T(8,128)(2,1)S(1)}, u32[]{:S(2)}, u32[]{:S(2)}) collective-permute-start(bf16[1024,512]{1,0:T(8,128)(2,1)S(1)} %copy-done.50), channel_id=1, source_target_pairs={{0,4},{4,0},{1,5},{5,1},{2,6},{6,2},{3,7},{7,3},{8,12},{12,8},{9,1... | collective-permute-start | bytes 3145736 | tf_op jit(solution)/shard_map/ppermute | solution.py:624
  242.4 45.1 %copy-start.23 = (bf16[2048,512]{1,0:T(8,128)(2,1)S(1)}, bf16[2048,512]{1,0:T(8,128)(2,1)}, u32[]{:S(2)}) copy-start(bf16[2048,512]{1,0:T(8,128)(2,1)} %param.33) | copy-start | bytes 6291460
  242.4 45.1 %copy-start.31 = (bf16[1024,512]{1,0:T(8,128)(2,1)S(1)}, bf16[1024,512]{1,0:T(8,128)(2,1)}, u32[]{:S(2)}) copy-start(bf16[1024,512]{1,0:T(8,128)(2,1)} %copy-done.30) | copy-start | bytes 3145732
  287.4 2.9 collective-permute-start.14
  372.3 9.3 %collective-permute-start.22 = (bf16[1024,512]{1,0:T(8,128)(2,1)}, bf16[1024,512]{1,0:T(8,128)(2,1)}, u32[]{:S(2)}, u32[]{:S(2)}) collective-permute-start(bf16[1024,512]{1,0:T(8,128)(2,1)} %get-tuple-element.64), channel_id=1, source_target_pairs={{0,1},{1,0},{2,3},{3,2},{4,5},{5,4},{6,7},{7,6},{8,9},{9,8},{10,11... | collective-permute-start | bytes 3145736 | tf_op jit(solution)/shard_map/ppermute | solution.py:624
  376.5 109.0 %collective-permute-start.42 = (f32[2,2,128,1024]{3,2,0,1:T(8,128)}, f32[2,2,128,1024]{3,2,0,1:T(8,128)}, u32[]{:S(2)}, u32[]{:S(2)}) collective-permute-start(f32[2,2,128,1024]{3,2,0,1:T(8,128)} %bitcast.60), channel_id=1, source_target_pairs={{0,1},{1,0},{2,3},{3,2},{4,5},{5,4},{6,7},{7,6},{8,9},{9,8},{10,11... | collective-permute-start | bytes 6291464 | tf_op jit(solution)/shard_map/ppermute | solution.py:624
  376.9 102.5 %collective-permute-start.20 = (bf16[1024,512]{1,0:T(8,128)(2,1)}, bf16[1024,512]{1,0:T(8,128)(2,1)}, u32[]{:S(2)}, u32[]{:S(2)}) collective-permute-start(bf16[1024,512]{1,0:T(8,128)(2,1)} %get-tuple-element.61), channel_id=1, source_target_pairs={{0,4},{4,0},{1,5},{5,1},{2,6},{6,2},{3,7},{7,3},{8,12},{12,8},{9,1... | collective-permute-start | bytes 3145736 | tf_op jit(solution)/shard_map/ppermute | solution.py:624
  441.3 17.1 %collective-permute-start.37 = (f32[2,32,512]{2,1,0:T(8,128)}, f32[2,32,512]{2,1,0:T(8,128)S(1)}, u32[]{:S(2)}, u32[]{:S(2)}) collective-permute-start(f32[2,32,512]{2,1,0:T(8,128)} %get-tuple-element.81), channel_id=1, source_target_pairs={{0,8},{8,0},{1,9},{9,1},{2,10},{10,2},{3,11},{11,3},{4,12},{12,4},... | collective-permute-start | bytes 393224 | tf_op jit(solution)/shard_map/ppermute | solution.py:624
  454.6 38.5 %collective-permute-start.23 = (bf16[1024,512]{1,0:T(8,128)(2,1)}, bf16[1024,512]{1,0:T(8,128)(2,1)S(1)}, u32[]{:S(2)}, u32[]{:S(2)}) collective-permute-start(bf16[1024,512]{1,0:T(8,128)(2,1)} %get-tuple-element.68), channel_id=1, source_target_pairs={{0,1},{1,0},{2,3},{3,2},{4,5},{5,4},{6,7},{7,6},{8,9},{9,8},{10,11... | collective-permute-start | bytes 3145736 | tf_op jit(solution)/shard_map/ppermute | solution.py:624
  454.6 65.8 %collective-permute-start.29 = (bf16[2,1024,512]{2,1,0:T(8,128)(2,1)}, bf16[2,1024,512]{2,1,0:T(8,128)(2,1)}, u32[]{:S(2)}, u32[]{:S(2)}) collective-permute-start(bf16[2,1024,512]{2,1,0:T(8,128)(2,1)} %get-tuple-element.79), channel_id=1, source_target_pairs={{0,1},{1,0},{2,3},{3,2},{4,5},{5,4},{6,7},{7,6},{8,9},{9,8},{10,11... | collective-permute-start | bytes 6291464 | tf_op jit(solution)/shard_map/ppermute | solution.py:624
  459.3 5.0 collective-permute-start.38
  459.4 20.1 %copy-start.26 = (bf16[1024,512]{1,0:T(8,128)(2,1)S(1)}, bf16[1024,512]{1,0:T(8,128)(2,1)}, u32[]{:S(2)}) copy-start(bf16[1024,512]{1,0:T(8,128)(2,1)} %get-tuple-element.60) | copy-start | bytes 3145732
  464.4 21.1 %collective-permute-start.39 = (f32[2,32,512]{2,1,0:T(8,128)S(1)}, f32[2,32,512]{2,1,0:T(8,128)S(1)}, u32[]{:S(2)}, u32[]{:S(2)}) collective-permute-start(f32[2,32,512]{2,1,0:T(8,128)S(1)} %add.166), channel_id=1, source_target_pairs={{0,16},{16,0},{1,17},{17,1},{2,18},{18,2},{3,19},{19,3},{4,20},{20... | collective-permute-start | bytes 393224 | tf_op jit(solution)/shard_map/ppermute | solution.py:624
  480.8 24.0 %collective-permute-start.21 = (bf16[1024,512]{1,0:T(8,128)(2,1)S(1)}, bf16[1024,512]{1,0:T(8,128)(2,1)S(1)}, u32[]{:S(2)}, u32[]{:S(2)}) collective-permute-start(bf16[1024,512]{1,0:T(8,128)(2,1)S(1)} %broadcast_select_fusion.14), channel_id=1, source_target_pairs={{0,1},{1,0},{2,3},{3,2},{4,5},{5,4},{6,7},{7,6},{8,9},{9,8},{10,11... | collective-permute-start | bytes 3145736 | tf_op jit(solution)/shard_map/ppermute | solution.py:624
  485.5 7.6 %collective-permute-start.40 = (f32[2,32,512]{2,1,0:T(8,128)S(1)}, f32[2,32,512]{2,1,0:T(8,128)S(1)}, u32[]{:S(2)}, u32[]{:S(2)}) collective-permute-start(f32[2,32,512]{2,1,0:T(8,128)S(1)} %add.167), channel_id=1, source_target_pairs={{0,4},{4,0},{1,5},{5,1},{2,6},{6,2},{3,7},{7,3},{8,12},{12,8},{9,1... | collective-permute-start | bytes 393224 | tf_op jit(solution)/shard_map/ppermute | solution.py:624
  487.9 15.2 %collective-permute-start.43 = (bf16[2,128,1024]{2,1,0:T(8,128)(2,1)S(1)}, bf16[2,128,1024]{2,1,0:T(8,128)(2,1)S(1)}, u32[]{:S(2)}, u32[]{:S(2)}) collective-permute-start(bf16[2,128,1024]{2,1,0:T(8,128)(2,1)S(1)} %fusion.45), channel_id=1, source_target_pairs={{0,2},{2,0},{1,3},{3,1},{4,6},{6,4},{5,7},{7,5},{8,10},{10,8},{9,1... | collective-permute-start | bytes 1572872 | tf_op jit(solution)/shard_map/ppermute | solution.py:624
  493.1 10.9 %collective-permute-start.41 = (f32[2,32,512]{2,1,0:T(8,128)S(1)}, f32[2,32,512]{2,1,0:T(8,128)S(1)}, u32[]{:S(2)}, u32[]{:S(2)}) collective-permute-start(f32[2,32,512]{2,1,0:T(8,128)S(1)} %add.168), channel_id=1, source_target_pairs={{0,1},{1,0},{2,3},{3,2},{4,5},{5,4},{6,7},{7,6},{8,9},{9,8},{10,11... | collective-permute-start | bytes 393224 | tf_op jit(solution)/shard_map/ppermute | solution.py:624
  502.5 22.5 %collective-permute-start.24 = (bf16[1024,512]{1,0:T(8,128)(2,1)S(1)}, bf16[1024,512]{1,0:T(8,128)(2,1)S(1)}, u32[]{:S(2)}, u32[]{:S(2)}) collective-permute-start(bf16[1024,512]{1,0:T(8,128)(2,1)S(1)} %get-tuple-element.71), channel_id=1, source_target_pairs={{0,1},{1,0},{2,3},{3,2},{4,5},{5,4},{6,7},{7,6},{8,9},{9,8},{10,11... | collective-permute-start | bytes 3145736 | tf_op jit(solution)/shard_map/ppermute | solution.py:624
  503.2 13.9 %collective-permute-start.44 = (bf16[2,128,1024]{2,1,0:T(8,128)(2,1)S(1)}, bf16[2,128,1024]{2,1,0:T(8,128)(2,1)S(1)}, u32[]{:S(2)}, u32[]{:S(2)}) collective-permute-start(bf16[2,128,1024]{2,1,0:T(8,128)(2,1)S(1)} %fusion.12), channel_id=1, source_target_pairs={{0,8},{8,0},{1,9},{9,1},{2,10},{10,2},{3,11},{11,3},{4,12},{12,4},... | collective-permute-start | bytes 1572872 | tf_op jit(solution)/shard_map/ppermute | solution.py:624
  518.2 108.1 %collective-permute-start.45 = (bf16[2,128,1024]{2,1,0:T(8,128)(2,1)}, bf16[2,128,1024]{2,1,0:T(8,128)(2,1)}, u32[]{:S(2)}, u32[]{:S(2)}) collective-permute-start(bf16[2,128,1024]{2,1,0:T(8,128)(2,1)} %add_convert_fusion.3), channel_id=1, source_target_pairs={{0,16},{16,0},{1,17},{17,1},{2,18},{18,2},{3,19},{19,3},{4,20},{20... | collective-permute-start | bytes 1572872 | tf_op jit(solution)/shard_map/ppermute | solution.py:624
  581.5 27.3 %collective-permute-start.26 = (bf16[2,1024,512]{2,1,0:T(8,128)(2,1)}, bf16[2,1024,512]{2,1,0:T(8,128)(2,1)S(1)}, u32[]{:S(2)}, u32[]{:S(2)}) collective-permute-start(bf16[2,1024,512]{2,1,0:T(8,128)(2,1)} %get-tuple-element.77), channel_id=1, source_target_pairs={{0,1},{1,0},{2,3},{3,2},{4,5},{5,4},{6,7},{7,6},{8,9},{9,8},{10,11... | collective-permute-start | bytes 6291464 | tf_op jit(solution)/shard_map/ppermute | solution.py:624
  589.1 62.1 %collective-permute-start.30 = (bf16[1024,512]{1,0:T(8,128)(2,1)}, bf16[1024,512]{1,0:T(8,128)(2,1)S(1)}, u32[]{:S(2)}, u32[]{:S(2)}) collective-permute-start(bf16[1024,512]{1,0:T(8,128)(2,1)} %constant_dynamic-slice_fusion.2), channel_id=1, source_target_pairs={{0,4},{4,0},{1,5},{5,1},{2,6},{6,2},{3,7},{7,3},{8,12},{12,8},{9,1... | collective-permute-start | bytes 3145736 | tf_op jit(solution)/shard_map/ppermute | solution.py:624
  594.1 5.6 collective-permute-start.32
  594.1 11.4 %collective-permute-start.25 = (bf16[1024,512]{1,0:T(8,128)(2,1)S(1)}, bf16[1024,512]{1,0:T(8,128)(2,1)S(1)}, u32[]{:S(2)}, u32[]{:S(2)}) collective-permute-start(bf16[1024,512]{1,0:T(8,128)(2,1)S(1)} %copy-done.61), channel_id=1, source_target_pairs={{0,1},{1,0},{2,3},{3,2},{4,5},{5,4},{6,7},{7,6},{8,9},{9,8},{10,11... | collective-permute-start | bytes 3145736 | tf_op jit(solution)/shard_map/ppermute | solution.py:624
  599.7 5.0 collective-permute-start.33
  604.7 21.0 %collective-permute-start.34 = (f32[2,32,512]{2,1,0:T(8,128)S(1)}, f32[2,32,512]{2,1,0:T(8,128)S(1)}, u32[]{:S(2)}, u32[]{:S(2)}) collective-permute-start(f32[2,32,512]{2,1,0:T(8,128)S(1)} %add.162), channel_id=1, source_target_pairs={{0,16},{16,0},{1,17},{17,1},{2,18},{18,2},{3,19},{19,3},{4,20},{20... | collective-permute-start | bytes 393224 | tf_op jit(solution)/shard_map/ppermute | solution.py:624
  622.0 31.9 %copy-start.17 = (bf16[1024,1024]{1,0:T(8,128)(2,1)}, bf16[1024,1024]{1,0:T(8,128)(2,1)S(1)}, u32[]{:S(2)}) copy-start(bf16[1024,1024]{1,0:T(8,128)(2,1)S(1)} %add_convert_fusion.1) | copy-start | bytes 6291460
  622.1 31.7 %collective-permute-start.27 = (bf16[1024,512]{1,0:T(8,128)(2,1)S(1)}, bf16[1024,512]{1,0:T(8,128)(2,1)S(1)}, u32[]{:S(2)}, u32[]{:S(2)}) collective-permute-start(bf16[1024,512]{1,0:T(8,128)(2,1)S(1)} %constant_dynamic-slice_fusion.3), channel_id=1, source_target_pairs={{0,4},{4,0},{1,5},{5,1},{2,6},{6,2},{3,7},{7,3},{8,12},{12,8},{9,1... | collective-permute-start | bytes 3145736 | tf_op jit(solution)/shard_map/ppermute | solution.py:624
  625.8 25.3 %collective-permute-start.35 = (f32[2,32,512]{2,1,0:T(8,128)S(1)}, f32[2,32,512]{2,1,0:T(8,128)S(1)}, u32[]{:S(2)}, u32[]{:S(2)}) collective-permute-start(f32[2,32,512]{2,1,0:T(8,128)S(1)} %add.163), channel_id=1, source_target_pairs={{0,4},{4,0},{1,5},{5,1},{2,6},{6,2},{3,7},{7,3},{8,12},{12,8},{9,1... | collective-permute-start | bytes 393224 | tf_op jit(solution)/shard_map/ppermute | solution.py:624
  627.7 31.9 %collective-permute-start.46 = (bf16[2,128,1024]{2,1,0:T(8,128)(2,1)S(1)}, bf16[2,128,1024]{2,1,0:T(8,128)(2,1)S(1)}, u32[]{:S(2)}, u32[]{:S(2)}) collective-permute-start(bf16[2,128,1024]{2,1,0:T(8,128)(2,1)S(1)} %add_convert_fusion.2), channel_id=1, source_target_pairs={{0,4},{4,0},{1,5},{5,1},{2,6},{6,2},{3,7},{7,3},{8,12},{12,8},{9,1... | collective-permute-start | bytes 1572872 | tf_op jit(solution)/shard_map/ppermute | solution.py:624
  651.1 1.9 collective-permute-start.36
  652.6 10.2 %collective-permute-start.31 = (bf16[1024,512]{1,0:T(8,128)(2,1)}, bf16[1024,512]{1,0:T(8,128)(2,1)}, u32[]{:S(2)}, u32[]{:S(2)}) collective-permute-start(bf16[1024,512]{1,0:T(8,128)(2,1)} %broadcast_select_fusion.10), channel_id=1, source_target_pairs={{0,1},{1,0},{2,3},{3,2},{4,5},{5,4},{6,7},{7,6},{8,9},{9,8},{10,11... | collective-permute-start | bytes 3145736 | tf_op jit(solution)/shard_map/ppermute | solution.py:624
  655.2 12.0 %collective-permute-start.28 = (bf16[1024,512]{1,0:T(8,128)(2,1)}, bf16[1024,512]{1,0:T(8,128)(2,1)}, u32[]{:S(2)}, u32[]{:S(2)}) collective-permute-start(bf16[1024,512]{1,0:T(8,128)(2,1)} %broadcast_select_fusion.12), channel_id=1, source_target_pairs={{0,1},{1,0},{2,3},{3,2},{4,5},{5,4},{6,7},{7,6},{8,9},{9,8},{10,11... | collective-permute-start | bytes 3145736 | tf_op jit(solution)/shard_map/ppermute | solution.py:624
  (58 other events, 230.7 us)
Sparse Core Ops, SparseCore 0:
  21.4 26.2 all-gather.9
  64.2 23.0 all-gather.15
  88.8 19.5 all-gather.11
  109.9 19.2 all-gather.13
  130.6 17.0 all-gather.19
  149.1 17.6 all-gather.17
  168.3 18.6 all-gather.21
  188.6 29.3 all-gather.23
  219.6 29.2 all-gather.25

commit v2 on v1

--- a/solution.py
+++ b/solution.py
@@ -183,7 +183,7 @@
             jax.ShapeDtypeStruct((cols, seq), jnp.bfloat16),
             jax.ShapeDtypeStruct((cols // 128, 2, seq), jnp.float32),
         ],
-        compiler_params=pltpu.CompilerParams(vmem_limit_bytes=56 * MIB),
+        compiler_params=pltpu.CompilerParams(vmem_limit_bytes=58 * MIB),
         cost_estimate=pl.CostEstimate(
             flops=8 * seq * mem * cols, bytes_accessed=12 * MIB, transcendentals=seq * mem * cols // 256
         ),
@@ -342,7 +342,7 @@
         out_shape=[jax.ShapeDtypeStruct((q_len, cols), jnp.bfloat16)] * n
         + [jax.ShapeDtypeStruct((2, m_len, cols), jnp.bfloat16)] * n
         + [jax.ShapeDtypeStruct((2, PP, cols), jnp.float32)],
-        compiler_params=pltpu.CompilerParams(vmem_limit_bytes=56 * MIB),
+        compiler_params=pltpu.CompilerParams(vmem_limit_bytes=58 * MIB),
         cost_estimate=pl.CostEstimate(
             flops=12 * seq * mem * cols, bytes_accessed=20 * MIB, transcendentals=seq * mem * cols // 256
         ),
@@ -452,7 +452,7 @@
             pltpu.VMEM((2, d, half), jnp.bfloat16),
             pltpu.SemaphoreType.DMA((4,)),
         ],
-        compiler_params=pltpu.CompilerParams(vmem_limit_bytes=40 * MIB),
+        compiler_params=pltpu.CompilerParams(vmem_limit_bytes=58 * MIB),
         cost_estimate=pl.CostEstimate(flops=4 * rows * d * d, bytes_accessed=12 * MIB, transcendentals=0),
         name="after_self",
     )(own, par, tokens, gains, so_own, so_oth, cq_own, cq_oth)
@@ -461,18 +461,29 @@
 CHUNK = 512
 
 
-def ffn_kernel(own_ref, par_ref, first_ref, cot_ref, gains_ref, down_ref, up_ref,
-               co_own, co_oth, in_own, in_oth, out_own, out_oth,
+def ffn_kernel(own_ref, par_ref, first_ref, cot_mine_ref, cot_got_ref, gains_ref, down_ref, up_ref,
+               co_own, co_oth, in_own, out_own, ffn_other,
                keep_ref, send_ref, gsec_ref, g_own_ref, g_par_ref, adapt_ref,
                co, w_in, w_out, slopes, acc, full, sems):
     core = lax.axis_index("c")
     x = lax.axis_index("x")
     half = keep_ref.shape[1]
-    hidden_half = w_in.shape[2]
+    hidden_half = w_in.shape[3]
+    d = full.shape[1]
     chunks = 2 * hidden_half // CHUNK
     co_copies = place_halves(co_own, co_oth, co, sems, 0)
-    in_copies = place_halves(in_own, in_oth, w_in, sems, 2)
-    out_copies = place_halves(out_own, out_oth, w_out, sems, 4)
+    in_copies = [pltpu.make_async_copy(in_own, w_in.at[x], sems.at[2])]
+    out_copies = [pltpu.make_async_copy(out_own, w_out.at[x], sems.at[3])]
+    at = 0
+    for held, copies in ((w_in, in_copies), (w_out, out_copies)):
+        tall, wide = held.shape[2:]
+        for j in range(wide // half):
+            copies.append(
+                pltpu.make_async_copy(
+                    ffn_other.at[:, pl.ds(at, tall)], held.at[1 - x, :, :, pl.ds(j * half, half)], sems.at[4 + len(copies) + 4 * (held is w_out)]
+                )
+            )
+            at += tall
     on_first(co_copies + in_copies + out_copies, "start")
 
     @pl.when(pl.program_id(0) == 0)
@@ -493,13 +504,18 @@
     on_first(in_copies, "wait")
     on_first(out_copies, "wait")
 
+    tall_out = w_out.shape[2]
+
+    def tall_at(t):
+        return (t % (hidden_half // CHUNK)) * (CHUNK // tall_out)
+
     def up_step(t, _):
         which = t // (hidden_half // CHUNK)
         at = pl.ds(pl.multiple_of((t % (hidden_half // CHUNK)) * CHUNK, CHUNK), CHUNK)
-        pre = mm(normed_low, w_in[which, :, at])
+        pre = mm(normed_low, w_in[which, :, :, at].reshape(d, CHUNK))
         hidden, slope = gelu_parts(pre)
         slopes[t] = slope
-        acc[...] += mm(low(hidden), w_out[which, at, :])
+        acc[...] += mm(low(hidden), w_out[which, pl.ds(tall_at(t), CHUNK // tall_out)].reshape(CHUNK, d))
         return 0
 
     lax.fori_loop(0, chunks, up_step, 0, unroll=2)
@@ -510,7 +526,9 @@
     keep_ref[...] = full[:, pl.ds(pl.multiple_of(x * half, half), half)]
     send_ref[...] = full[:, pl.ds(pl.multiple_of((1 - x) * half, half), half)]
 
-    grad_three = norm_back(n_three, r_three, gain_three, cot_ref[...].astype(jnp.float32))
+    full[:, pl.ds(pl.multiple_of(x * half, half), half)] = cot_mine_ref[...]
+    full[:, pl.ds(pl.multiple_of((1 - x) * half, half), half)] = cot_got_ref[...]
+    grad_three = norm_back(n_three, r_three, gain_three, full[...].astype(jnp.float32))
     branch = low(grad_three)
     adapted = low(4.0 * branch.astype(jnp.float32))
     bottle_grad = low(mm_nt(adapted, up_ref[...]) * bottle_slope)
@@ -521,8 +539,8 @@
     def down_step(t, _):
         which = t // (hidden_half // CHUNK)
         at = pl.ds(pl.multiple_of((t % (hidden_half // CHUNK)) * CHUNK, CHUNK), CHUNK)
-        grad_pre = low(mm_nt(branch, w_out[which, at, :]) * slopes[t])
-        acc[...] += mm_nt(grad_pre, w_in[which, :, at])
+        grad_pre = low(mm_nt(branch, w_out[which, pl.ds(tall_at(t), CHUNK // tall_out)].reshape(CHUNK, d)) * slopes[t])
+        acc[...] += mm_nt(grad_pre, w_in[which, :, :, at].reshape(d, CHUNK))
         return 0
 
     lax.fori_loop(0, chunks, down_step, 0, unroll=2)
@@ -534,10 +552,12 @@
     g_par_ref[...] = low(mm_nt(second_low, co[1 - core]))
 
 
-def ffn_both_ways(own, par, first, cot, gains, down, up, co_own, co_oth, in_own, in_oth, out_own, out_oth):
+def ffn_both_ways(own, par, first, cot_mine, cot_got, gains, down, up, co_own, co_oth, in_own, out_own, ffn_other):
     rows, d = first.shape
     half = d // 2
     hidden_half = in_own.shape[1]
+    in_own = in_own.reshape(8, d // 8, hidden_half)
+    out_own = out_own.reshape(8, hidden_half // 8, d)
     bottleneck = down.shape[1]
     whole = lambda shape: pl.BlockSpec(shape, lambda i: (0,) * len(shape))
     flops = 2 * rows * d * (8 * hidden_half + 6 * bottleneck + 2 * d)
@@ -545,9 +565,9 @@
         ffn_kernel,
         grid=(rows // BT,),
         in_specs=[
-            rows_spec(half), rows_spec(half), rows_spec(d), rows_spec(d),
+            rows_spec(half), rows_spec(half), rows_spec(d), rows_spec(half), rows_spec(half),
             whole((3, d)), whole((d, bottleneck)), whole((bottleneck, d)),
-            ANY, ANY, ANY, ANY, ANY, ANY,
+            ANY, ANY, ANY, ANY, ANY,
         ],
         out_specs=[
             rows_spec(half), rows_spec(half), rows_spec(d), rows_spec(half), rows_spec(half),
@@ -563,17 +583,17 @@
         ],
         scratch_shapes=[
             pltpu.VMEM((2, half, d), jnp.bfloat16),
-            pltpu.VMEM((2, d, hidden_half), jnp.bfloat16),
-            pltpu.VMEM((2, hidden_half, d), jnp.bfloat16),
+            pltpu.VMEM((2, *in_own.shape), jnp.bfloat16),
+            pltpu.VMEM((2, *out_own.shape), jnp.bfloat16),
             pltpu.VMEM((2 * hidden_half // CHUNK, BT, CHUNK), jnp.float32),
             pltpu.VMEM((BT, d), jnp.float32),
             pltpu.VMEM((BT, d), jnp.bfloat16),
-            pltpu.SemaphoreType.DMA((6,)),
+            pltpu.SemaphoreType.DMA((16,)),
         ],
         compiler_params=pltpu.CompilerParams(vmem_limit_bytes=58 * MIB),
         cost_estimate=pl.CostEstimate(flops=flops, bytes_accessed=48 * MIB, transcendentals=0),
         name="ffn_both_ways",
-    )(own, par, first, cot, gains, down, up, co_own, co_oth, in_own, in_oth, out_own, out_oth)
+    )(own, par, first, cot_mine, cot_got, gains, down, up, co_own, co_oth, in_own, out_own, ffn_other)
 
 
 def before_self_kernel(gsec_ref, own_ref, par_ref, first_ref, gains_ref, so_own, so_oth, cq_own, cq_oth,
@@ -614,12 +634,502 @@
             pltpu.VMEM((2, d, half), jnp.bfloat16),
             pltpu.SemaphoreType.DMA((4,)),
         ],
-        compiler_params=pltpu.CompilerParams(vmem_limit_bytes=40 * MIB),
+        compiler_params=pltpu.CompilerParams(vmem_limit_bytes=58 * MIB),
         cost_estimate=pl.CostEstimate(flops=4 * rows * d * d, bytes_accessed=16 * MIB, transcendentals=0),
         name="before_self",
     )(gsec, own, par, first, gains, so_own, so_oth, cq_own, cq_oth)
 
 
+MESH_ID = pl.DeviceIdType.MESH
+PARTS_IN = 4
+
+
+def greet(targets):
+    barrier = pltpu.get_barrier_semaphore()
+    for target in targets:
+        pl.semaphore_signal(barrier, inc=1, device_id=target, device_id_type=MESH_ID)
+    pl.semaphore_wait(barrier, len(targets))
+
+
+def remote(src, dst, send, recv, target):
+    return pltpu.make_async_remote_copy(
+        src_ref=src, dst_ref=dst, send_sem=send, recv_sem=recv, device_id=target, device_id_type=MESH_ID
+    )
+
+
+def eighth_index():
+    return (lax.axis_index("zl") * 2 + lax.axis_index("y")) * 2 + lax.axis_index("c")
+
+
+def piece_copies(wholes, pieces, send, recv, at):
+    index = eighth_index()
+    copies = []
+    for n, (whole, piece) in enumerate(zip(wholes, pieces)):
+        rows = piece.shape[0]
+        source = whole.at[pl.ds(pl.multiple_of(index * rows, rows), rows)]
+        copies.append(remote(source, piece, send.at[at + n], recv.at[at + n], {"x": 1 - lax.axis_index("x")}))
+    return copies
+
+
+def piece_shapes(weights):
+    return [jax.ShapeDtypeStruct((w.shape[0] // 8, w.shape[1]), w.dtype) for w in weights]
+
+
+def bring_kernel(tok, mem, cot, qkv, prefix, segs, w_in, w_out, *refs):
+    wholes, pieces = refs[:2], refs[11:13]
+    rows_own, rows_par, mem_mine, packed, cot_mine, cot_send, qkv_oth, prefix_got, segs_got = refs[2:11]
+    stage, send, recv, load = refs[13:]
+    x, y, zl, core = (lax.axis_index(name) for name in ("x", "y", "zl", "c"))
+    half = rows_own.shape[0]
+    cols = tok.shape[1]
+    chunk = half // PARTS_IN
+    piece = qkv.shape[0] // 8
+    stays = x == core
+    partner = {"c": 1 - core}
+    across = {"x": 1 - x}
+
+    def token_half(which):
+        return pl.ds(pl.multiple_of(which * half, half), half)
+
+    loads = [
+        pltpu.make_async_copy(source.at[token_half(which)], stage.at[n], load.at[n])
+        for n, (source, which) in enumerate(((tok, core), (tok, 1 - core), (mem, core), (cot, core)))
+    ]
+    at = 0
+    for whole in (w_in, w_out):
+        tall, wide = whole.shape[0] // 8, whole.shape[1]
+        source = pl.ds(pl.multiple_of(eighth_index() * tall, tall), tall)
+        for j in range(wide // cols):
+            n = len(loads)
+            loads.append(
+                pltpu.make_async_copy(
+                    whole.at[source, pl.ds(j * cols, cols)], stage.at[4, pl.ds(at, tall)], load.at[n]
+                )
+            )
+            at += tall
+    pack = pltpu.make_async_copy(stage.at[4], packed.at[pl.ds(half, half)], load.at[len(loads)])
+    mem_send = packed.at[pl.ds(0, half)]
+    for copy in loads:
+        copy.start()
+    greet([across, {"x": 1 - x, "c": 1 - core}, {"y": 1 - y}, {"zl": 1 - zl}, partner])
+
+    def features(which):
+        return pl.ds(pl.multiple_of(which * cols, cols), cols)
+
+    def part(k):
+        return pl.ds(k * chunk, chunk)
+
+    def eighth(a, b, c):
+        return pl.ds(pl.multiple_of(((a * 2 + b) * 2 + c) * piece, piece), piece)
+
+    def weight(at, slot, target, source=None):
+        return remote((qkv_oth if source is None else source).at[at], qkv_oth.at[at], send.at[slot], recv.at[slot], target)
+
+    mine = eighth(zl, y, core)
+    w_x = weight(mine, 0, across, qkv)
+    w_x.start()
+    at_small = 14 + 3 * PARTS_IN
+    small = [
+        remote(prefix, prefix_got, send.at[at_small], recv.at[at_small], across),
+        remote(segs, segs_got, send.at[at_small + 1], recv.at[at_small + 1], partner),
+    ]
+    for copy in small:
+        copy.start()
+    others = small + piece_copies(wholes, pieces, send, recv, at_small + 2)
+
+    at_own, at_par = 8, 8 + PARTS_IN
+    at_here = 8 + 2 * PARTS_IN
+
+    def token_sends():
+        copies = []
+        for t in range(2):
+            for k in range(PARTS_IN):
+                slot = at_own + k
+                copies.append(
+                    remote(
+                        tok.at[pl.ds(t * half + k * chunk, chunk)],
+                        rows_own.at[part(k), features(x)],
+                        send.at[slot + t * PARTS_IN],
+                        recv.at[slot],
+                        {"x": 1 - x, "c": t},
+                    )
+                )
+        return copies
+
+    def here_copies():
+        own = tok.at[token_half(core)]
+        other = tok.at[token_half(1 - core)]
+        return [
+            remote(other, rows_own.at[:, features(x)], send.at[at_here], recv.at[at_here], partner),
+            remote(own, rows_par.at[:, features(x)], send.at[at_here + 1], recv.at[at_here + 1], partner),
+        ]
+
+    def row_copy(source, to, slot):
+        return remote(source.at[token_half(1 - core)], to, send.at[slot], recv.at[slot], partner)
+
+    @pl.when(jnp.logical_not(stays))
+    def _():
+        for copy in token_sends():
+            copy.start()
+        row_copy(mem, mem_send, at_here + 3).start()
+        row_copy(cot, cot_send, at_here + 5).start()
+        for n, to, slot in ((2, mem_send, at_here + 3), (3, cot_send, at_here + 5)):
+            loads[n].wait()
+            pltpu.make_async_copy(stage.at[n], to, recv.at[slot]).start()
+        loads[0].wait()
+        loads[1].wait()
+
+    @pl.when(stays)
+    def _():
+        for copy in here_copies():
+            copy.start()
+        row_copy(mem, mem_mine, at_here + 2).start()
+        row_copy(cot, cot_mine, at_here + 4).start()
+        for n, to, slot in (
+            (0, rows_own.at[:, features(x)], at_here),
+            (1, rows_par.at[:, features(x)], at_here + 1),
+            (2, mem_mine, at_here + 2),
+            (3, cot_mine, at_here + 4),
+        ):
+            loads[n].wait()
+            pltpu.make_async_copy(stage.at[n], to, recv.at[slot]).start()
+
+    for copy in others[2:]:
+        copy.start()
+
+    for copy in loads[4:]:
+        copy.wait()
+    pack.start()
+
+    w_x.wait_recv()
+    w_y = weight(mine, 1, {"y": 1 - y})
+    w_z = weight(mine, 2, {"zl": 1 - zl})
+    w_c = weight(mine, 4, partner)
+    for copy in (w_y, w_z, w_c):
+        copy.start()
+
+    forwards = []
+
+    def forward(k):
+        here = rows_own.at[part(k), features(1 - x)]
+        remote(here, here, send.at[at_own + k], recv.at[at_own + k], across).wait_recv()
+        copy = remote(here, rows_par.at[part(k), features(1 - x)], send.at[at_here + 6 + k], recv.at[at_par + k], partner)
+        copy.start()
+        forwards.append(copy)
+
+    forward(0)
+    w_y.wait_recv()
+    from_y = eighth(zl, 1 - y, core)
+    w_yz = weight(from_y, 3, {"zl": 1 - zl})
+    w_yc = weight(from_y, 5, partner)
+    w_yz.start()
+    w_yc.start()
+    forward(1)
+    w_z.wait_recv()
+    w_zc = weight(eighth(1 - zl, y, core), 6, partner)
+    w_zc.start()
+    for k in range(2, PARTS_IN):
+        forward(k)
+    w_yz.wait_recv()
+    w_yzc = weight(eighth(1 - zl, 1 - y, core), 7, partner)
+    w_yzc.start()
+
+    for copy in (w_c, w_yc, w_zc, w_yzc, *others):
+        copy.wait_recv()
+    for k, copy in enumerate(forwards):
+        copy.wait_recv()
+    for to, slot in (
+        (rows_own.at[:, features(x)], at_here),
+        (rows_par.at[:, features(x)], at_here + 1),
+        (mem_mine, at_here + 2),
+        (mem_send, at_here + 3),
+        (cot_mine, at_here + 4),
+        (cot_send, at_here + 5),
+    ):
+        remote(to, to, send.at[slot], recv.at[slot], partner).wait_recv()
+
+    pack.wait()
+
+    for copy in (w_x, w_y, w_z, w_c, w_yz, w_yc, w_zc, w_yzc, *forwards, *others):
+        copy.wait_send()
+
+    @pl.when(jnp.logical_not(stays))
+    def _():
+        for copy in token_sends():
+            copy.wait_send()
+        row_copy(mem, mem_send, at_here + 3).wait_send()
+        row_copy(cot, cot_send, at_here + 5).wait_send()
+
+    @pl.when(stays)
+    def _():
+        for copy in here_copies():
+            copy.wait_send()
+        row_copy(mem, mem_mine, at_here + 2).wait_send()
+        row_copy(cot, cot_mine, at_here + 4).wait_send()
+
+
+def bring_rows(tokens, memory, cotangent, qkv_flat, prefixes, segs, ffn_in, ffn_out, weights):
+    rows, cols = tokens.shape
+    half = rows // 2
+    wide_rows = jax.ShapeDtypeStruct((half, 2 * cols), jnp.bfloat16)
+    thin_rows = jax.ShapeDtypeStruct((half, cols), jnp.bfloat16)
+    slots = 16 + 3 * PARTS_IN + len(weights)
+    return pl.pallas_call(
+        bring_kernel,
+        in_specs=[ANY] * 10,
+        out_specs=[ANY] * 11,
+        out_shape=[wide_rows, wide_rows, thin_rows, jax.ShapeDtypeStruct((rows, cols), jnp.bfloat16), thin_rows, thin_rows,
+                   jax.ShapeDtypeStruct(qkv_flat.shape, jnp.bfloat16),
+                   jax.ShapeDtypeStruct(prefixes.shape, prefixes.dtype),
+                   jax.ShapeDtypeStruct(segs.shape, segs.dtype)] + piece_shapes(weights),
+        scratch_shapes=[
+            pltpu.VMEM((5, half, cols), jnp.bfloat16),
+            pltpu.SemaphoreType.DMA((slots,)),
+            pltpu.SemaphoreType.DMA((slots,)),
+            pltpu.SemaphoreType.DMA((16,)),
+        ],
+        compiler_params=pltpu.CompilerParams(collective_id=0, has_side_effects=True, vmem_limit_bytes=58 * MIB),
+        cost_estimate=pl.CostEstimate(flops=0, bytes_accessed=64 * MIB, transcendentals=0),
+        name="bring_rows",
+    )(tokens, memory, cotangent, qkv_flat, prefixes, segs, ffn_in, ffn_out, *weights)
+
+
+def project_kernel(n_weights, n_pieces, n_passed, *refs):
+    own, par = refs[:n_pieces], refs[n_pieces:2 * n_pieces]
+    refs = refs[2 * n_pieces:]
+    w_own, w_oth, wholes = refs[0], refs[1], refs[2:2 + n_passed]
+    out_own, out_par, passed = refs[2 + n_passed], refs[3 + n_passed], refs[4 + n_passed:4 + 2 * n_passed]
+    held, sems = refs[4 + 2 * n_passed:6 + 2 * n_passed]
+    x, core = lax.axis_index("x"), lax.axis_index("c")
+    d = held.shape[0] // n_weights
+    cols = held.shape[1]
+
+    def copies(source):
+        return [
+            pltpu.make_async_copy(source.at[pl.ds(t * d, d)], held.at[pl.ds(t * d, d)], sems.at[t])
+            for t in range(n_weights)
+        ]
+
+    first = pl.program_id(0) == 0
+
+    @pl.when(jnp.logical_and(first, x == core))
+    def _():
+        for copy in copies(w_own):
+            copy.start()
+
+    @pl.when(jnp.logical_and(first, x != core))
+    def _():
+        for copy in copies(w_oth):
+            copy.start()
+
+    if n_passed:
+        send, recv = refs[6 + 2 * n_passed:]
+
+        @pl.when(first)
+        def _():
+            greet([{"x": 1 - x}])
+            for copy in piece_copies(wholes, passed, send, recv, 0):
+                copy.start()
+
+    offsets = [0] if n_pieces == 1 else [x * (d // 2), (1 - x) * (d // 2)]
+    for t in range(n_weights):
+        @pl.when(first)
+        def _(t=t):
+            copies(w_own)[t].wait()
+
+        for pieces, out in ((own, out_own), (par, out_par)):
+            total = None
+            for piece, at in zip(pieces, offsets):
+                rows = pl.ds(pl.multiple_of(t * d + at, d // 2), piece.shape[1])
+                term = mm(piece[...], held[rows, :])
+                total = term if total is None else total + term
+            out[:, t * cols:(t + 1) * cols] = low(total)
+
+    if n_passed:
+        @pl.when(pl.program_id(0) == pl.num_programs(0) - 1)
+        def _():
+            for copy in piece_copies(wholes, passed, send, recv, 0):
+                copy.wait()
+
+
+def project(own, par, w_own, w_oth, n_weights, passed=()):
+    rows = own[0].shape[0]
+    cols = w_own.shape[1]
+    d = w_own.shape[0] // n_weights
+    n = len(passed)
+    reach = [pltpu.SemaphoreType.DMA((n,))] * 2 if n else []
+    extra = dict(collective_id=2, has_side_effects=True) if n else {}
+    return pl.pallas_call(
+        functools.partial(project_kernel, n_weights, len(own), n),
+        grid=(rows // BT,),
+        in_specs=[rows_spec(piece.shape[1]) for piece in (*own, *par)] + [ANY] * (2 + n),
+        out_specs=[rows_spec(n_weights * cols)] * 2 + [ANY] * n,
+        out_shape=[jax.ShapeDtypeStruct((rows, n_weights * cols), jnp.bfloat16)] * 2 + piece_shapes(passed),
+        scratch_shapes=[pltpu.VMEM(w_own.shape, jnp.bfloat16), pltpu.SemaphoreType.DMA((n_weights,))] + reach,
+        compiler_params=pltpu.CompilerParams(vmem_limit_bytes=58 * MIB, **extra),
+        cost_estimate=pl.CostEstimate(flops=4 * rows * d * cols * n_weights, bytes_accessed=16 * MIB, transcendentals=0),
+        name="project",
+    )(*own, *par, w_own, w_oth, *passed)
+
+
+PREFIX_STEPS = ("zl", "y", "zh", "x")
+
+
+def finish_kernel(dq_own, dq_got, dkv_own, dkv_got, gfirst, w_own, w_oth, pre_ref,
+                  out_ref, pre_out_ref,
+                  lhs, first, held, boxes, land, sums, arrived, local, send, recv):
+    x, core = lax.axis_index("x"), lax.axis_index("c")
+    here = {name: lax.axis_index(name) for name in PREFIX_STEPS}
+    partner, across = {"c": 1 - core}, {"x": 1 - x}
+    stays = x == core
+    blocks = lhs.shape[0]
+    half = blocks * BT
+    cols = out_ref.shape[1]
+    d = held.shape[1] // 3
+
+    def loads(b):
+        rows = pl.ds(b * BT, BT)
+        pairs = [(dq_own.at[rows], lhs.at[b, 0]), (dkv_own.at[0, rows], lhs.at[b, 1]), (dkv_own.at[1, rows], lhs.at[b, 2]),
+                 (dq_got.at[rows], lhs.at[b, 3]), (dkv_got.at[0, rows], lhs.at[b, 4]), (dkv_got.at[1, rows], lhs.at[b, 5]),
+                 (gfirst.at[rows], first.at[b])]
+        return [pltpu.make_async_copy(src, dst, local.at[b, n]) for n, (src, dst) in enumerate(pairs)]
+
+    def weights(agree):
+        pair = (w_own, w_oth) if agree else (w_oth, w_own)
+        return [pltpu.make_async_copy(src, held.at[n], local.at[blocks, n]) for n, src in enumerate(pair)]
+
+    for copy in loads(0):
+        copy.start()
+
+    @pl.when(stays)
+    def _():
+        for copy in weights(True):
+            copy.start()
+
+    @pl.when(jnp.logical_not(stays))
+    def _():
+        for copy in weights(False):
+            copy.start()
+
+    for b in range(1, blocks):
+        for copy in loads(b):
+            copy.start()
+    greet([across, {"x": 1 - x, "c": 1 - core}, partner] + [{name: 1 - here[name]} for name in PREFIX_STEPS[:3]])
+
+    def landing(b):
+        return pl.ds(pl.multiple_of(core * half + b * BT, BT), BT)
+
+    def over(b):
+        return remote(boxes.at[b, 0], land.at[landing(b)], send.at[0, b], recv.at[landing_slot(b)], {"x": 1 - x, "c": x})
+
+    def beside(b):
+        return remote(boxes.at[b, 1], land.at[landing(b)], send.at[1, b], recv.at[landing_slot(b)], partner)
+
+    def landing_slot(b):
+        return core * blocks + b
+
+    def compute(b, which):
+        at = pl.ds(pl.multiple_of(which * cols, cols), cols)
+        total = first[b, :, at]
+        for n in range(6):
+            rows = pl.ds(pl.multiple_of((n % 3) * d + which * cols, cols), cols)
+            total += mm_nt(lhs[b, n], held[n // 3, rows, :])
+        return low(total)
+
+    steps = len(PREFIX_STEPS) + 1
+
+    def prefix_copy(s):
+        target = {PREFIX_STEPS[s]: 1 - here[PREFIX_STEPS[s]]} if s < steps - 1 else partner
+        return remote(sums.at[s], arrived.at[s], send.at[2, s], recv.at[2 * blocks + s], target)
+
+    sums[0] = pre_ref[...]
+    prefix_copy(0).start()
+    for copy in weights(True):
+        copy.wait()
+    for b in range(blocks):
+        for copy in loads(b):
+            copy.wait()
+        boxes[b, 0] = compute(b, 1 - x)
+        over(b).start()
+        kept = compute(b, x)
+
+        @pl.when(stays)
+        def _(b=b, kept=kept):
+            land[landing(b), :] = kept
+
+        @pl.when(jnp.logical_not(stays))
+        def _(b=b, kept=kept):
+            boxes[b, 1] = kept
+            beside(b).start()
+
+        if b < steps - 1:
+            prefix_copy(b).wait()
+            sums[b + 1] = sums[b] + arrived[b]
+            prefix_copy(b + 1).start()
+    for b in range(blocks, steps - 1):
+        prefix_copy(b).wait()
+        sums[b + 1] = sums[b] + arrived[b]
+        prefix_copy(b + 1).start()
+
+    def deliver(t, b):
+        rows = pl.ds(pl.multiple_of(t * half + b * BT, BT), BT)
+        out_ref[rows, :] = land[rows, :].astype(jnp.float32)
+
+    def wait_for(t, b):
+        rows = land.at[pl.ds(pl.multiple_of(t * half + b * BT, BT), BT)]
+        remote(rows, rows, send.at[0, b], recv.at[t * blocks + b], across).wait_recv()
+
+    for b in range(blocks):
+        @pl.when(stays)
+        def _(b=b):
+            deliver(core, b)
+            wait_for(1 - core, b)
+            deliver(1 - core, b)
+
+        @pl.when(jnp.logical_not(stays))
+        def _(b=b):
+            for t in range(2):
+                wait_for(t, b)
+                deliver(t, b)
+
+    prefix_copy(steps - 1).wait()
+    pre_out_ref[...] = jnp.where(stays, sums[steps - 1], arrived[steps - 1])
+    for b in range(blocks):
+        over(b).wait_send()
+
+        @pl.when(jnp.logical_not(stays))
+        def _(b=b):
+            beside(b).wait_send()
+
+
+def finish_tokens(dq_own, dq_got, dkv_own, dkv_got, gfirst, w_own, w_oth, prefix):
+    half, cols = dq_own.shape
+    blocks = half // BT
+    steps = len(PREFIX_STEPS) + 1
+    vmem = pl.BlockSpec(memory_space=pltpu.VMEM)
+    return pl.pallas_call(
+        finish_kernel,
+        in_specs=[ANY] * 7 + [vmem],
+        out_specs=[vmem, vmem],
+        out_shape=[jax.ShapeDtypeStruct((2 * half, cols), jnp.float32), jax.ShapeDtypeStruct(prefix.shape, jnp.float32)],
+        scratch_shapes=[
+            pltpu.VMEM((blocks, 6, BT, cols), jnp.bfloat16),
+            pltpu.VMEM((blocks, BT, 2 * cols), jnp.float32),
+            pltpu.VMEM((2, *w_own.shape), jnp.bfloat16),
+            pltpu.VMEM((blocks, 2, BT, cols), jnp.bfloat16),
+            pltpu.VMEM((2 * half, cols), jnp.bfloat16),
+            pltpu.VMEM((steps, *prefix.shape), jnp.float32),
+            pltpu.VMEM((steps, *prefix.shape), jnp.float32),
+            pltpu.SemaphoreType.DMA((blocks + 1, 7)),
+            pltpu.SemaphoreType.DMA((3, max(blocks, steps))),
+            pltpu.SemaphoreType.DMA((2 * blocks + steps,)),
+        ],
+        compiler_params=pltpu.CompilerParams(collective_id=1, has_side_effects=True, vmem_limit_bytes=58 * MIB),
+        cost_estimate=pl.CostEstimate(flops=12 * half * cols * 2 * cols, bytes_accessed=64 * MIB, transcendentals=0),
+        name="finish_tokens",
+    )(dq_own, dq_got, dkv_own, dkv_got, gfirst, w_own, w_oth, prefix)
+
+
 def swap(value, axis):
     return lax.ppermute(value, axis, SWAP)
 
@@ -628,24 +1138,8 @@
     return lax.optimization_barrier((value, *others))[0]
 
 
-def other_half(weight):
-    group = ("zl", "y", "c")
-    count = math.prod(lax.axis_size(name) for name in group)
-    piece = weight.shape[0] // count
-    mine = lax.dynamic_slice_in_dim(weight, lax.axis_index(group) * piece, piece, 0)
-    return swap(mine, "x")
-
-
 def gather_half(piece):
     return lax.all_gather(piece, ("zl", "y", "c"), axis=0, tiled=True)
-
-
-def bring_in(rows, agree):
-    half = rows.shape[0] // 2
-    core = lax.axis_index("c")
-    keep = lax.dynamic_slice_in_dim(rows, core * half, half, 0)
-    got = swap(lax.dynamic_slice_in_dim(rows, (1 - core) * half, half, 0), "c")
-    return jnp.where(agree, keep, got), jnp.where(agree, got, keep)
 
 
 def in_order(first_here, mine, others, axis):
@@ -665,15 +1159,6 @@
     half = value.shape[1] // 2
     x = lax.axis_index("x")
     return lax.dynamic_slice_in_dim(value, x * half, half, 1), lax.dynamic_slice_in_dim(value, (1 - x) * half, half, 1)
-
-
-def sum_over(value, axes):
-    for name in axes:
-        if lax.axis_size(name) == 2:
-            value = value + swap(value, name)
-        elif lax.axis_size(name) > 2:
-            value = lax.psum(value, name)
-    return value
 
 
 def paired_device(
@@ -686,100 +1171,71 @@
     prefix_count = self_prefix.shape[1]
 
     qkv_flat = self_qkv.reshape(-1, columns)
-    qkv_piece = other_half(qkv_flat)
-    tok_mine, tok_send = bring_in(tokens, agree)
-    mem_mine, mem_send = bring_in(memory, agree)
-    cot_mine, cot_send = bring_in(cotangent, agree)
+    ckv_flat = cross_kv.reshape(-1, columns)
     segs = jnp.concatenate([dec_segments, mem_segments], axis=0)
-    segs = jnp.where(agree, segs, swap(segs, "c"))
+    prefixes = jnp.concatenate([self_prefix, cross_prefix], axis=0)
+    prefixes = jnp.pad(prefixes, ((0, 0), (0, PP - prefix_count), (0, 0)))
+    (
+        rows_own, rows_par, mem_mine, packed, cot_mine, cot_send, qkv_other, prefixes_got, segs_got, *pieces
+    ) = bring_rows(
+        tokens, memory, cotangent, qkv_flat, prefixes, segs, ffn_in, ffn_out, [self_out, cross_q]
+    )
+    segs = jnp.where(agree, segs, segs_got)
     dec_seg, mem_seg = segs[0], segs[1]
-    prefixes = jnp.concatenate([self_prefix, cross_prefix], axis=0)
-    prefixes = jnp.where(agree, prefixes, swap(prefixes, "x"))
-    prefixes = jnp.pad(prefixes, ((0, 0), (0, PP - prefix_count), (0, 0)))
+    prefixes = jnp.where(agree, prefixes, prefixes_got)
     self_pre, cross_pre = prefixes[:2], prefixes[2:]
-
-    tok_got = swap(tok_send, "x")
-    rows_own = in_order(x == 0, tok_mine, tok_got, 1)
-    rows_par = swap(rows_own, "c")
-    qkv_other = gather_half(qkv_piece)
-
-    gate = tok_got
-    mem_got = swap(after(mem_send, gate), "x")
-    ckv_flat = cross_kv.reshape(-1, columns)
-    ckv_other = gather_half(other_half(after(ckv_flat, gate)))
-    so_other = gather_half(other_half(after(self_out, gate)))
-    cq_other = gather_half(other_half(after(cross_q, gate)))
-    co_other = gather_half(other_half(after(cross_out, gate)))
-
     self_masks = mask_columns(dec_seg, dec_seg, prefix_count)
     self_lo, self_hi = ranges(dec_seg, dec_seg, True)
     cross_masks = mask_columns(dec_seg, mem_seg, prefix_count)
     cross_lo, cross_hi = ranges(dec_seg, mem_seg, False)
 
-    qkv_here = jnp.where(agree, qkv_flat, qkv_other).reshape(self_qkv.shape)
-    qkv_there = jnp.where(agree, qkv_other, qkv_flat).reshape(self_qkv.shape)
-
-    def project(rows, weights):
-        return [low(mm(rows, weights[t])) for t in range(weights.shape[0])]
-
-    own = project(rows_own, qkv_here)
-    par = project(rows_par, qkv_here)
-    self_q, self_k, self_v = ([(own[t], 0), (par[t], 0)] for t in range(3))
+    so_other, cq_other = (gather_half(piece) for piece in pieces)
+    own, par, *pieces = project([rows_own], [rows_par], qkv_flat, qkv_other, 3, [ckv_flat, cross_out])
+    ckv_other, co_other = (gather_half(piece) for piece in pieces)
+    got = swap(after(packed, own), "x")
+    self_q, self_k, self_v = ([(own, t), (par, t)] for t in range(3))
     self_o, self_ot, self_lt = attend_fwd(
         self_q, self_k, self_v, columns, self_masks, self_pre, self_lo, self_hi, True
     )
     heads_got = swap(self_o[1], "c")
 
-    gate = (mem_got, heads_got)
-    in_other = gather_half(other_half(after(ffn_in, *gate)))
-    out_other = gather_half(other_half(after(ffn_out, *gate)))
-    cot_got = swap(after(cot_send, *gate), "x")
+    mem_got = got[:mem_mine.shape[0]]
+    ffn_other = gather_half(after(got, heads_got)[mem_mine.shape[0]:])
+    ffn_other = ffn_other.reshape(8, -1, columns)
     down_full = lax.all_gather(adapter_down.T, ("y", "c"), axis=0, tiled=True).T
     up_full = lax.all_gather(adapter_up, ("y", "c"), axis=0, tiled=True)
 
-    mem_own = in_order(x == 0, mem_mine, mem_got, 1)
-    mem_par = swap(mem_own, "c")
-    ckv_here = jnp.where(agree, ckv_flat, ckv_other).reshape(cross_kv.shape)
-    ckv_there = jnp.where(agree, ckv_other, ckv_flat).reshape(cross_kv.shape)
+    cot_got = swap(after(cot_send, got), "x")
+    mem_par, mem_par_got = swap(mem_mine, "c"), swap(mem_got, "c")
     first_sum, cq_own, cq_send = after_self(
         self_o[0], heads_got, rows_own, gains, self_out, so_other, cross_q, cq_other
     )
     cq_par = swap(cq_send, "c")
-    own = project(mem_own, ckv_here)
-    par = project(mem_par, ckv_here)
+    own, par = project([mem_mine, mem_got], [mem_par, mem_par_got], ckv_flat, ckv_other, 2)
     cross_qp = [(cq_own, 0), (cq_par, 0)]
-    cross_k, cross_v = ([(own[t], 0), (par[t], 0)] for t in range(2))
+    cross_k, cross_v = ([(own, t), (par, t)] for t in range(2))
     cross_o, cross_ot, cross_lt = attend_fwd(
         cross_qp, cross_k, cross_v, columns, cross_masks, cross_pre, cross_lo, cross_hi, False
     )
     cross_got = swap(cross_o[1], "c")
-    cot_own = in_order(x == 0, cot_mine, cot_got, 1)
     out_keep, out_send, grad_second, g_own, g_send, grad_adapt = ffn_both_ways(
-        cross_o[0], cross_got, first_sum, cot_own, gains, down_full, up_full,
-        cross_out, co_other, ffn_in, in_other, ffn_out, out_other,
+        cross_o[0], cross_got, first_sum, cot_mine, cot_got, gains, down_full, up_full,
+        cross_out, co_other, ffn_in, ffn_out, ffn_other,
     )
     g_par = swap(g_send, "c")
     output = send_out(out_keep, out_send, agree)
 
-    n_y = lax.axis_size("y")
-    block = grad_adapt.shape[1] // (2 * n_y)
-    blocks = grad_adapt.reshape(2, n_y, 2, block, -1)
+    blocks = grad_adapt.reshape(2, 2, 2, grad_adapt.shape[1] // 4, -1)
     part = lax.dynamic_index_in_dim(blocks, core, 2, False) + swap(
         lax.dynamic_index_in_dim(blocks, 1 - core, 2, False), "c"
     )
-    if n_y == 2:
-        y = lax.axis_index("y")
-        part = lax.dynamic_index_in_dim(part, y, 1, False) + swap(
-            low(lax.dynamic_index_in_dim(part, 1 - y, 1, False)), "y"
-        ).astype(jnp.float32)
-    else:
-        part = lax.psum_scatter(part, "y", scatter_dimension=1, tiled=False)
+    y = lax.axis_index("y")
+    part = lax.dynamic_index_in_dim(part, y, 1, False) + swap(
+        low(lax.dynamic_index_in_dim(part, 1 - y, 1, False)), "y"
+    ).astype(jnp.float32)
     for name in ("zl", "zh", "x"):
-        if lax.axis_size(name) == 2:
-            part = low(part)
-            part = part.astype(jnp.float32) + swap(part, name).astype(jnp.float32)
-        elif lax.axis_size(name) > 2:
-            part = lax.psum(part, name)
+        part = low(part)
+        part = part.astype(jnp.float32) + swap(part, name).astype(jnp.float32)
     grad_down, grad_up = part[0].T, part[1]
 
     cdq, cdkv, cross_dp = attend_bwd(
@@ -801,6 +1257,8 @@
                 total = term if total is None else total + term
         return total
 
+    ckv_here = jnp.where(agree, ckv_flat, ckv_other).reshape(cross_kv.shape)
+    ckv_there = jnp.where(agree, ckv_other, ckv_flat).reshape(cross_kv.shape)
     grad_mem = low(back(cdkv[0], cdkv_got, ckv_here, ckv_there))
     mem_keep, mem_out = feature_halves(grad_mem)
     grad_memory = send_out(mem_keep, mem_out, agree).astype(jnp.float32)
@@ -811,22 +1269,13 @@
     )
     sdq_got = swap(sdq[1], "c")
     sdkv_got = swap(sdkv[1], "c")
-    grad_rows = low(
-        grad_first
-        + back(
-            [sdq[0], sdkv[0][0], sdkv[0][1]], [sdq_got, sdkv_got[0], sdkv_got[1]], qkv_here, qkv_there
-        )
-    )
-    tok_keep, tok_out = feature_halves(grad_rows)
-    grad_tokens = send_out(tok_keep, tok_out, agree).astype(jnp.float32)
-
-    def prefix_total(value):
-        value = sum_over(value, ("zl", "y", "zh", "x"))
-        return jnp.where(agree, value, swap(value, "c"))[:, :prefix_count]
-
-    return (
-        output, grad_tokens, grad_memory, prefix_total(self_dp), prefix_total(cross_dp), grad_down, grad_up,
-    )
+    grad_tokens, prefix_sums = finish_tokens(
+        sdq[0], sdq_got, sdkv[0], sdkv_got, grad_first, qkv_flat, qkv_other,
+        jnp.concatenate([self_dp, cross_dp], axis=0),
+    )
+    prefix_sums = prefix_sums[:, :prefix_count]
+
+    return (output, grad_tokens, grad_memory, prefix_sums[:2], prefix_sums[2:], grad_down, grad_up)
 
 
 def norm_grad(gathered, gain, upstream):
@@ -931,9 +1380,8 @@
 
 def solution(mesh):
     dp, wide, narrow = (mesh.shape[name] for name in ("dp", "wide", "narrow"))
-    if wide == 2 and narrow % 2 == 0:
-        zl = 2 if dp % 2 == 0 else 1
-        parts = Mesh(mesh.devices.reshape(dp // zl, zl, wide, narrow // 2, 2), ("zh", "zl", "x", "y", "c"))
+    if (dp, wide, narrow) == (4, 2, 4):
+        parts = Mesh(mesh.devices.reshape(2, 2, 2, 2, 2), ("zh", "zl", "x", "y", "c"))
         device, used = paired_device, parts
         rows, split, thin = ("zh", "zl", "y", "c"), "x", ("y", "c")
     else:

time: 683 us -> 602 us (0.88)
  Pallas kernels: 298 us -> 421 us
  waiting for transfers between devices: 132 us -> 68.1 us
  starting transfers between devices: 68.3 us -> 20.4 us
  matrix products: 63.7 us -> 18.8 us
  other arithmetic: 56.8 us -> 29.9 us
  local copies, waits for them, and re-layouts: 44.5 us -> 21 us
    pallas_call x0 -> x4, Pallas kernels: none -> 111 us  [the longest x1 45.3 us: bring_rows(): pl.pallas_call(bring_kernel, in_specs=[ANY] * 10, out_specs=[ANY] * 11, o...]
    ppermute x47 -> x22, waiting for transfers between devices: 131 us -> 36.8 us  [swap(): return lax.ppermute(value, axis, SWAP)]
    ppermute x47 -> x22, starting transfers between devices: 67.5 us -> 19.9 us  [swap(): return lax.ppermute(value, axis, SWAP)]
    dot_general x10 -> x0, matrix products: 30.6 us -> none  [mm(): return jnp.dot(a, b, preferred_element_type=jnp.float32)]
    all_gather x7 -> x5, waiting for transfers between devices: 0.03 us -> 29.5 us  [gather_half(): return lax.all_gather(piece, ('zl', 'y', 'c'), axis=0, tiled=True)]
    dot_general x10 -> x4, matrix products: 33.1 us -> 18.8 us  [mm_nt(): lax.dot_general(a, b, (((1,), (1,)), ((), ())), preferred_element_type=jn...]
    unnamed x138 -> x44, local copies, waits for them, and re-layouts: 23.2 us -> 10.8 us
    dynamic_slice x10 -> x0, local copies, waits for them, and re-layouts: 12.1 us -> none  [the longest x7 6.14 us: other_half(): lax.dynamic_slice_in_dim(weight, lax.axis_index(group) * piece, piece, 0)]
  transfers between devices with their start and end apart: 56 -> 29, of which waited for: 18 -> 6; matrix products, arithmetic and copies ran while one was open for 21% -> 9% of each run, Pallas kernels for 32% -> 50%
where the time goes in v2:
time: 602 us; the launch traced here: 594 us
  Pallas kernels  421 us (70%)
  waiting for transfers between devices  68.1 us (11%)
  other arithmetic  29.9 us (5%)
  local copies, waits for them, and re-layouts  21 us (3%)
  starting transfers between devices  20.4 us (3%)
  matrix products  18.8 us (3%)
  between operations  14.8 us (2%)
    pallas_call x2, Pallas kernels, attend_bwd(): pl.pallas_call(functools.partial(bwd_kernel, causal, n), grid_spec=grid_s...  119 us
    pallas_call x2, Pallas kernels, attend_fwd(): pl.pallas_call(functools.partial(fwd_kernel, causal, n), grid_spec=grid_s...  87.2 us
    pallas_call x1, Pallas kernels, ffn_both_ways(): pl.pallas_call(ffn_kernel, grid=(rows // BT,), in_specs=[rows_spec(half),...  81.5 us
    pallas_call x1, Pallas kernels, bring_rows(): pl.pallas_call(bring_kernel, in_specs=[ANY] * 10, out_specs=[ANY] * 11, o...  45.3 us
    pallas_call x1, Pallas kernels, finish_tokens(): pl.pallas_call(finish_kernel, in_specs=[ANY] * 7 + [vmem], out_specs=[vme...  43.8 us
    ppermute x22, waiting for transfers between devices, swap(): return lax.ppermute(value, axis, SWAP)  36.8 us
    all_gather x5, waiting for transfers between devices, gather_half(): return lax.all_gather(piece, ('zl', 'y', 'c'), axis=0, tiled=True)  29.5 us
    pallas_call x2, Pallas kernels, project(): pl.pallas_call(functools.partial(project_kernel, n_weights, len(own), n),...  22.1 us
  transfers between devices with their start and end apart: 29, of which 6 were waited for; matrix products, arithmetic and copies ran while one was open for 9% of the time, Pallas kernels for 50%

profile of v2, /device:TPU:0, one launch (start us, length us, event | category | flops | bytes accessed | tf_op | source)
XLA Modules:
  0.0 593.9 jit_solution(9668969769919763554)
XLA Ops:
  7.2 0.8 copy.33
  8.1 0.8 copy.34
  8.9 0.7 fusion.19.prefix
  9.6 1.3 pad_add_fusion.segs
  10.9 45.3 %bring_rows.1 = (bf16[1024,1024]{1,0:T(8,128)(2,1)}, bf16[1024,1024]{1,0:T(8,128)(2,1)}, bf16[1024,512]{1,0:T(8,128)(2,1)}, bf16[2048,512]{1,0:T(8,128)(2,1)}, b...) custom-call(bf16[2048,512]{1,0:T(8,128)(2,1)} %tok.1, ...), custom_call_target="tpu_custom_call" | custom-call | bytes 67108864 | tf_op jit(solution)/shard_map/bring_rows/pallas_call | solution.py:877
  56.3 0.7 all-gather.8.cloned.1.call-update
  57.1 12.9 %project.2 = (bf16[1024,1536]{1,0:T(8,128)(2,1)}, bf16[1024,1536]{1,0:T(8,128)(2,1)}, bf16[256,512]{1,0:T(8,128)(2,1)}, bf16[64,1024]{1,0:T(8,128)(2,1)}) custom-call(bf16[1024,1024]{1,0:T(8,128)(2,1)} %get-tuple-element.60.refs_0_.tok_ref, bf16[1024,1024]{1,0:T(8,128)(2,1)} %get-tuple-element.61.refs_1_, bf16[3072,512]{1,0:T(8,128)(2,1)} %bitcast.47, ...), custom_call_target="tpu_custom_call" | custom-call | flops 6442450944 | bytes 16777216 | tf_op jit(solution)/shard_map/project/pallas_call | solution.py:962
  71.3 1.8 collective-permute-start.2
  73.7 1.1 fusion.12.refs_6_.refs_10_
  75.1 0.6 and_select_fusion.lo_ref
  75.7 0.7 fusion.21
  76.3 1.1 select_convert_fusion.refs_7_.refs_11_
  77.5 0.7 and_convert_fusion.refs_9_.refs_13_
  78.7 40.6 %attend_fwd_self.1 = (bf16[1024,512]{1,0:T(8,128)(2,1)}, bf16[1024,512]{1,0:T(8,128)(2,1)}, bf16[512,2048]{1,0:T(8,128)(2,1)}, f32[4,2,2048]{2,1,0:T(2,128)}) custom-call(s32[8]{0:T(128)} %and_select_fusion.lo_ref, s32[8]{0:T(128)} %iota.40.hi_ref, bf16[1024,1536]{1,0:T(8,128)(2,1)} %get-tuple-element.63.refs_0_.refs_2_.refs_4_, ...), custom_call_target="tpu_custom_call" | custom-call | flops 17179869184 | bytes 12582912 | tf_op jit(solution)/shard_map/attend_fwd_self/pallas_call | solution.py:178
  119.3 2.9 collective-permute-done.par_ref
  122.1 1.2 slice.75
  124.1 10.7 %after_self.1 = (bf16[1024,1024]{1,0:T(8,128)(2,1)}, bf16[1024,512]{1,0:T(8,128)(2,1)}, bf16[1024,512]{1,0:T(8,128)(2,1)}) custom-call(bf16[1024,512]{1,0:T(8,128)(2,1)} %get-tuple-element.66.own_ref, bf16[1024,512]{1,0:T(8,128)(2,1)} %copy-done.15, bf16[1024,1024]{1,0:T(8,128)(2,1)} %get-tuple-element.60.refs_0_.tok_ref, f32[3,1024]{1,0:T(4,128)} %gains_ref.5, ...), custom_call_target="tpu_custom_call" | custom-call | flops 4294967296 | bytes 12582912 | tf_op jit(solution)/shard_map/after_self/pallas_call | solution.py:440
  135.1 0.6 and_select_fusion.1
  135.6 1.1 fusion.15.refs_6_.refs_10_
  137.2 9.1 %project.3 = (bf16[1024,1024]{1,0:T(8,128)(2,1)}, bf16[1024,1024]{1,0:T(8,128)(2,1)}) custom-call(bf16[1024,512]{1,0:T(8,128)(2,1)} %get-tuple-element.72.refs_0_, bf16[1024,512]{1,0:T(8,128)(2,1)} %copy-done.5, bf16[1024,512]{1,0:T(8,128)(2,1)} %collective-permute-done.3.refs_2_, bf16[1024,512]{1,0:T(8,128)(2,1)} %collective-permute-done.4.refs_3_, ...), custom_call_target="tpu_custom_call" | custom-call | flops 4294967296 | bytes 16777216 | tf_op jit(solution)/shard_map/project/pallas_call | solution.py:962
  146.4 0.9 copy-done.13
  147.3 46.6 %attend_fwd_cross.1 = (bf16[1024,512]{1,0:T(8,128)(2,1)}, bf16[1024,512]{1,0:T(8,128)(2,1)}, bf16[512,2048]{1,0:T(8,128)(2,1)}, f32[4,2,2048]{2,1,0:T(2,128)}) custom-call(s32[8]{0:T(128)} %get-tuple-element.148.lo_ref, s32[8]{0:T(128)} %get-tuple-element.147.hi_ref, bf16[1024,512]{1,0:T(8,128)(2,1)} %get-tuple-element.70.refs_0_, ...), custom_call_target="tpu_custom_call" | custom-call | flops 17179869184 | bytes 12582912 | tf_op jit(solution)/shard_map/attend_fwd_cross/pallas_call | solution.py:178
  194.0 2.8 collective-permute-done.5.par_ref
  196.8 29.4 %all-gather.20.cloned.1.call-done = bf16[8192,512]{1,0:T(8,128)(2,1)} async-done(((bf16[1024,512]{1,0:T(8,128)(2,1)}), bf16[8192,512]{1,0:T(8,128)(2,1)}) %all-gather.20.cloned.1.call-update) | async-done | bytes 8388624 | tf_op jit(solution)/shard_map/all_gather | solution.py:1142
  226.3 81.5 %ffn_both_ways.1 = (bf16[1024,512]{1,0:T(8,128)(2,1)}, bf16[1024,512]{1,0:T(8,128)(2,1)}, f32[1024,1024]{1,0:T(8,128)}, bf16[1024,512]{1,0:T(8,128)(2,1)}, bf16[...) custom-call(bf16[1024,512]{1,0:T(8,128)(2,1)} %get-tuple-element.78.own_ref, bf16[1024,512]{1,0:T(8,128)(2,1)} %copy-done.16, ...), custom_call_target="tpu_custom_call" | custom-call | flops 45097156608 | bytes 50331648 | tf_op jit(solution)/shard_map/ffn_both_ways/pallas_call | solution.py:564
  308.1 2.7 constant_dynamic-slice_fusion.1
  310.7 1.5 copy.46
  312.4 1.5 collective-permute-start.7
  314.0 1.0 copy-done.14
  315.0 63.0 %attend_bwd_cross.1 = (bf16[1024,512]{1,0:T(8,128)(2,1)}, bf16[1024,512]{1,0:T(8,128)(2,1)}, bf16[2,1024,512]{2,1,0:T(8,128)(2,1)}, bf16[2,1024,512]{2,1,0:T(8,128)(2,1)}, f32[2,32,512]{2,1,0:T(8,128)}) custom-call(s32[8]{0:T(128)} %get-tuple-element.148.lo_ref, s32[8]{0:T(128)} %get-tuple-element.147.hi_ref, bf16[1024,512]{1,0:T(8,128)(2,1)} %get-tuple-element.70.refs_0_, ...), custom_call_target="tpu_custom_call" | custom-call | flops 25769803776 | bytes 20971520 | tf_op jit(solution)/shard_map/attend_bwd_cross/pallas_call | solution.py:339
  378.1 4.5 broadcast_select_fusion
  383.1 1.3 copy-done.3
  384.4 2.2 bitcast_add_fusion
  386.8 2.3 broadcast_select_fusion.4
  389.1 11.8 %before_self.1 = (f32[1024,1024]{1,0:T(8,128)}, bf16[1024,512]{1,0:T(8,128)(2,1)}, bf16[1024,512]{1,0:T(8,128)(2,1)}) custom-call(f32[1024,1024]{1,0:T(8,128)} %get-tuple-element.88.gsec_ref, bf16[1024,512]{1,0:T(8,128)(2,1)} %get-tuple-element.93.own_ref, bf16[1024,512]{1,0:T(8,128)(2,1)} %collective-permute-done.10.par_ref, ...), custom_call_target="tpu_custom_call" | custom-call | flops 4294967296 | bytes 16777216 | tf_op jit(solution)/shard_map/before_self/pallas_call | solution.py:619
  401.7 5.1 collective-permute-start.19
  406.8 4.7 fusion.1
  411.5 3.3 fusion.5
  414.7 4.2 collective-permute-done.19
  418.9 1.0 add_convert_fusion.2
  419.9 3.6 collective-permute-start.20
  423.5 4.5 fusion.3
  428.5 55.6 %attend_bwd_self.1 = (bf16[1024,512]{1,0:T(8,128)(2,1)}, bf16[1024,512]{1,0:T(8,128)(2,1)}, bf16[2,1024,512]{2,1,0:T(8,128)(2,1)}, bf16[2,1024,512]{2,1,0:T(8,128)(2,1)}, f32[2,32,512]{2,1,0:T(8,128)}) custom-call(s32[8]{0:T(128)} %and_select_fusion.lo_ref, s32[8]{0:T(128)} %iota.44.hi_ref, bf16[1024,1536]{1,0:T(8,128)(2,1)} %get-tuple-element.63.refs_0_.refs_2_.refs_4_, ...), custom_call_target="tpu_custom_call" | custom-call | flops 25769803776 | bytes 20971520 | tf_op jit(solution)/shard_map/attend_bwd_self/pallas_call | solution.py:339
  484.2 6.3 %add_convert_fusion = bf16[1024,1024]{1,0:T(8,128)(2,1)S(1)} fusion(f32[1024,1024]{1,0:T(8,128)} %fusion.1, f32[1024,1024]{1,0:T(8,128)} %fusion.5, f32[1024,1024]{1,0:T(8,128)} %fusion.3, bf16[2048,512]{1,0:T(8,128)(2,1)S(1)} %copy-done, bf16[2,1024,512]{2,1,0:T(8,128)(2,1)} %collective-permute-done.14), kind=kOutput, calls=%fused_computation | convolution fusion | flops 1077936128 | bytes 16777216 | tf_op jit(solution)/shard_map/dot_general | solution.py:31
  490.5 1.1 constant_dynamic-slice_fusion.2
  491.6 4.1 collective-permute-start.15
  495.7 1.4 broadcast_select_fusion.9
  497.1 0.6 collective-permute-start.12
  497.7 1.4 add_convert_fusion.1
  499.2 1.5 pad_maximum_fusion
  500.7 0.7 pad_maximum_fusion.1.pre_ref
  501.4 18.6 %collective-permute-done.15 = bf16[1024,512]{1,0:T(8,128)(2,1)} collective-permute-done((bf16[1024,512]{1,0:T(8,128)(2,1)}, bf16[1024,512]{1,0:T(8,128)(2,1)}, u32[]{:S(2)}, u32[]{:S(2)}) %collective-permute-start.15) | collective-permute-done | bytes 1048608 | tf_op jit(solution)/shard_map/ppermute | solution.py:1134
  520.0 2.6 broadcast_select_fusion.2
  522.6 8.4 %collective-permute-done.21 = bf16[2,128,1024]{2,1,0:T(8,128)(2,1)S(1)} collective-permute-done((bf16[2,128,1024]{2,1,0:T(8,128)(2,1)S(1)}, bf16[2,128,1024]{2,1,0:T(8,128)(2,1)S(1)}, u32[]{:S(2)}, u32[]{:S(2)}) %collective-permute-start.21) | collective-permute-done | bytes 524320 | tf_op jit(solution)/shard_map/ppermute | solution.py:1134
  531.2 0.9 slice_bitcast_fusion.4
  532.1 1.0 copy.41
  533.1 43.8 %finish_tokens.1 = (f32[2048,512]{1,0:T(8,128)}, f32[4,32,512]{2,1,0:T(8,128)}) custom-call(bf16[1024,512]{1,0:T(8,128)(2,1)} %get-tuple-element.99.dq_own, bf16[1024,512]{1,0:T(8,128)(2,1)} %collective-permute-done.12.dq_got, bf16[2,1024,512]{2,1,0:T(8,128)(2,1)} %get-tuple-element.101.dkv_own, bf16[2,1024,512]{2,1,0:T(8,128)(2,1)} %collective-permute-done.13.dkv_got, ...), custom_call_target="tpu_custom_call" | custom-call | flops 6442450944 | bytes 67108864 | tf_op jit(solution)/shard_map/finish_tokens/pallas_call | solution.py:1110
  576.9 1.0 fusion.20
  577.8 0.7 copy.39
  578.6 0.7 copy.40
  579.3 1.8 broadcast_select_fusion.7
  581.1 2.7 maximum_convert_fusion
  583.9 1.0 copy-done.1
  584.8 2.0 copy.48
  (100 shorter events, 7.2 us)
Async XLA Ops:
  7.2 116.9 %all-gather.10.cloned.1.call-start = ((), (), s32[]{:S(2)}) async-start(), calls=%async_computation.1 | async-start | bytes 1179648 | tf_op jit(solution)/shard_map/all_gather | solution.py:1142
  56.2 67.9 %all-gather.8.cloned.1.call-start = ((), (), s32[]{:S(2)}) async-start(), calls=%async_computation | async-start | bytes 1179648 | tf_op jit(solution)/shard_map/all_gather | solution.py:1142
  57.0 80.2 %all-gather.12.cloned.1.call-start = ((), (), s32[]{:S(2)}) async-start(), calls=%async_computation.2 | async-start | bytes 2359296 | tf_op jit(solution)/shard_map/all_gather | solution.py:1142
  57.0 16.3 %copy-start.9 = (s32[1,2048]{1,0:T(1,128)S(1)}, s32[1,2048]{1,0:T(1,128)}, u32[]{:S(2)}) copy-start(s32[1,2048]{1,0:T(1,128)} %param.20) | copy-start | bytes 24580
  57.0 16.3 %copy-start.10 = (s32[1,2048]{1,0:T(1,128)S(1)}, s32[1,2048]{1,0:T(1,128)}, u32[]{:S(2)}) copy-start(s32[1,2048]{1,0:T(1,128)} %param.19) | copy-start | bytes 24580
  57.1 16.3 %copy-start.11 = (s32[2,2048]{1,0:T(2,128)S(1)}, s32[2,2048]{1,0:T(2,128)}, u32[]{:S(2)}) copy-start(s32[2,2048]{1,0:T(2,128)} %get-tuple-element.59) | copy-start | bytes 49156
  57.1 18.6 %copy-start.6 = (bf16[4,32,512]{2,1,0:T(8,128)(2,1)S(1)}, bf16[4,32,512]{2,1,0:T(8,128)(2,1)}, u32[]{:S(2)}) copy-start(bf16[4,32,512]{2,1,0:T(8,128)(2,1)} %get-tuple-element.65) | copy-start | bytes 393220
  70.0 123.9 %all-gather.16.cloned.1.call-start = ((), (), s32[]{:S(2)}) async-start(), calls=%async_computation.4 | async-start | bytes 1310720 | tf_op jit(solution)/shard_map/all_gather | solution.py:1206
  70.6 123.4 %all-gather.14.cloned.1.call-start = ((), (), s32[]{:S(2)}) async-start(), calls=%async_computation.3 | async-start | bytes 1310720 | tf_op jit(solution)/shard_map/all_gather | solution.py:1205
  71.2 122.8 %all-gather.18.cloned.1.call-start = ((), (), s32[]{:S(2)}) async-start(), calls=%async_computation.5 | async-start | bytes 1179648 | tf_op jit(solution)/shard_map/all_gather | solution.py:1142
  71.3 50.9 %collective-permute-start.2 = (bf16[2048,512]{1,0:T(8,128)(2,1)}, bf16[2048,512]{1,0:T(8,128)(2,1)S(1)}, u32[]{:S(2)}, u32[]{:S(2)}) collective-permute-start(bf16[2048,512]{1,0:T(8,128)(2,1)} %get-tuple-element.74), channel_id=1, source_target_pairs={{0,4},{4,0},{1,5},{5,1},{2,6},{6,2},{3,7},{7,3},{8,12},{12,8},{9,1... | collective-permute-start | bytes 6291464 | tf_op jit(solution)/shard_map/ppermute | solution.py:1134
  73.1 153.2 %all-gather.20.cloned.1.call-start = ((), (), s32[]{:S(2)}) async-start(), calls=%async_computation.6 | async-start | bytes 9437184 | tf_op jit(solution)/shard_map/all_gather | solution.py:1142
  119.2 2.9 collective-permute-start
  122.1 1.3 copy-start.15
  123.4 13.8 %collective-permute-start.3 = (bf16[1024,512]{1,0:T(8,128)(2,1)}, bf16[1024,512]{1,0:T(8,128)(2,1)}, u32[]{:S(2)}, u32[]{:S(2)}) collective-permute-start(bf16[1024,512]{1,0:T(8,128)(2,1)} %get-tuple-element.72.refs_0_), channel_id=1, source_target_pairs={{0,1},{1,0},{2,3},{3,2},{4,5},{5,4},{6,7},{7,6},{8,9},{9,8},{10,11... | collective-permute-start | bytes 3145736 | tf_op jit(solution)/shard_map/ppermute | solution.py:1134
  123.6 11.1 %copy-start.5 = (bf16[1024,512]{1,0:T(8,128)(2,1)}, bf16[1024,512]{1,0:T(8,128)(2,1)S(1)}, u32[]{:S(2)}) copy-start(bf16[1024,512]{1,0:T(8,128)(2,1)S(1)} %slice.93.refs_1_) | copy-start | bytes 3145732
  123.7 13.6 %collective-permute-start.4 = (bf16[1024,512]{1,0:T(8,128)(2,1)S(1)}, bf16[1024,512]{1,0:T(8,128)(2,1)}, u32[]{:S(2)}, u32[]{:S(2)}) collective-permute-start(bf16[1024,512]{1,0:T(8,128)(2,1)S(1)} %slice.93.refs_1_), channel_id=1, source_target_pairs={{0,1},{1,0},{2,3},{3,2},{4,5},{5,4},{6,7},{7,6},{8,9},{9,8},{10,11... | collective-permute-start | bytes 3145736 | tf_op jit(solution)/shard_map/ppermute | solution.py:1134
  124.1 12.7 %copy-start.12 = (bf16[1024,512]{1,0:T(8,128)(2,1)S(1)}, bf16[1024,512]{1,0:T(8,128)(2,1)}, u32[]{:S(2)}) copy-start(bf16[1024,512]{1,0:T(8,128)(2,1)} %get-tuple-element.83) | copy-start | bytes 3145732
  134.8 11.6 %collective-permute-start.1 = (bf16[1024,512]{1,0:T(8,128)(2,1)}, bf16[1024,512]{1,0:T(8,128)(2,1)S(1)}, u32[]{:S(2)}, u32[]{:S(2)}) collective-permute-start(bf16[1024,512]{1,0:T(8,128)(2,1)} %get-tuple-element.71), channel_id=1, source_target_pairs={{0,1},{1,0},{2,3},{3,2},{4,5},{5,4},{6,7},{7,6},{8,9},{9,8},{10,11... | collective-permute-start | bytes 3145736 | tf_op jit(solution)/shard_map/ppermute | solution.py:1134
  136.8 57.3 %collective-permute-start.6 = (bf16[1024,512]{1,0:T(8,128)(2,1)S(1)}, bf16[1024,512]{1,0:T(8,128)(2,1)}, u32[]{:S(2)}, u32[]{:S(2)}) collective-permute-start(bf16[1024,512]{1,0:T(8,128)(2,1)S(1)} %copy-done.12), channel_id=1, source_target_pairs={{0,4},{4,0},{1,5},{5,1},{2,6},{6,2},{3,7},{7,3},{8,12},{12,8},{9,1... | collective-permute-start | bytes 3145736 | tf_op jit(solution)/shard_map/ppermute | solution.py:1134
  146.4 1.0 copy-start.13
  193.9 2.9 collective-permute-start.5
  196.8 29.5 %copy-start.16 = (bf16[1024,512]{1,0:T(8,128)(2,1)}, bf16[1024,512]{1,0:T(8,128)(2,1)S(1)}, u32[]{:S(2)}) copy-start(bf16[1024,512]{1,0:T(8,128)(2,1)S(1)} %collective-permute-done.5.par_ref) | copy-start | bytes 3145732
  307.7 6.2 %collective-permute-start.9 = (bf16[1024,512]{1,0:T(8,128)(2,1)}, bf16[1024,512]{1,0:T(8,128)(2,1)S(1)}, u32[]{:S(2)}, u32[]{:S(2)}) collective-permute-start(bf16[1024,512]{1,0:T(8,128)(2,1)} %get-tuple-element.90), channel_id=1, source_target_pairs={{0,1},{1,0},{2,3},{3,2},{4,5},{5,4},{6,7},{7,6},{8,9},{9,8},{10,11... | collective-permute-start | bytes 3145736 | tf_op jit(solution)/shard_map/ppermute | solution.py:1134
  312.2 70.9 %collective-permute-start.17 = (f32[2,2,128,1024]{3,2,0,1:T(8,128)}, f32[2,2,128,1024]{3,2,0,1:T(8,128)S(1)}, u32[]{:S(2)}, u32[]{:S(2)}) collective-permute-start(f32[2,2,128,1024]{3,2,0,1:T(8,128)} %bitcast.42), channel_id=1, source_target_pairs={{0,1},{1,0},{2,3},{3,2},{4,5},{5,4},{6,7},{7,6},{8,9},{9,8},{10,11... | collective-permute-start | bytes 6291464 | tf_op jit(solution)/shard_map/ppermute | solution.py:1134
  312.4 74.4 %collective-permute-start.7 = (bf16[1024,512]{1,0:T(8,128)(2,1)}, bf16[1024,512]{1,0:T(8,128)(2,1)}, u32[]{:S(2)}, u32[]{:S(2)}) collective-permute-start(bf16[1024,512]{1,0:T(8,128)(2,1)} %get-tuple-element.87), channel_id=1, source_target_pairs={{0,4},{4,0},{1,5},{5,1},{2,6},{6,2},{3,7},{7,3},{8,12},{12,8},{9,1... | collective-permute-start | bytes 3145736 | tf_op jit(solution)/shard_map/ppermute | solution.py:1134
  314.0 1.0 copy-start.14
  378.0 11.1 %collective-permute-start.10 = (bf16[1024,512]{1,0:T(8,128)(2,1)}, bf16[1024,512]{1,0:T(8,128)(2,1)}, u32[]{:S(2)}, u32[]{:S(2)}) collective-permute-start(bf16[1024,512]{1,0:T(8,128)(2,1)} %get-tuple-element.94), channel_id=1, source_target_pairs={{0,1},{1,0},{2,3},{3,2},{4,5},{5,4},{6,7},{7,6},{8,9},{9,8},{10,11... | collective-permute-start | bytes 3145736 | tf_op jit(solution)/shard_map/ppermute | solution.py:1134
  382.6 40.9 %collective-permute-start.14 = (bf16[2,1024,512]{2,1,0:T(8,128)(2,1)}, bf16[2,1024,512]{2,1,0:T(8,128)(2,1)}, u32[]{:S(2)}, u32[]{:S(2)}) collective-permute-start(bf16[2,1024,512]{2,1,0:T(8,128)(2,1)} %get-tuple-element.108), channel_id=1, source_target_pairs={{0,1},{1,0},{2,3},{3,2},{4,5},{5,4},{6,7},{7,6},{8,9},{9,8},{10,11... | collective-permute-start | bytes 6291464 | tf_op jit(solution)/shard_map/ppermute | solution.py:1134
  383.1 1.3 copy-start.3
  384.4 2.4 copy-start.2
  386.7 14.8 %collective-permute-start.18 = (bf16[2,128,1024]{2,1,0:T(8,128)(2,1)S(1)}, bf16[2,128,1024]{2,1,0:T(8,128)(2,1)S(1)}, u32[]{:S(2)}, u32[]{:S(2)}) collective-permute-start(bf16[2,128,1024]{2,1,0:T(8,128)(2,1)S(1)} %fusion.16), channel_id=1, source_target_pairs={{0,2},{2,0},{1,3},{3,1},{4,6},{6,4},{5,7},{7,5},{8,10},{10,8},{9,1... | collective-permute-start | bytes 1572872 | tf_op jit(solution)/shard_map/ppermute | solution.py:1134
  389.1 106.6 %collective-permute-start.8 = (bf16[1024,512]{1,0:T(8,128)(2,1)}, bf16[1024,512]{1,0:T(8,128)(2,1)}, u32[]{:S(2)}, u32[]{:S(2)}) collective-permute-start(bf16[1024,512]{1,0:T(8,128)(2,1)} %broadcast_select_fusion.4), channel_id=1, source_target_pairs={{0,1},{1,0},{2,3},{3,2},{4,5},{5,4},{6,7},{7,6},{8,9},{9,8},{10,11... | collective-permute-start | bytes 3145736 | tf_op jit(solution)/shard_map/ppermute | solution.py:1134
  401.0 5.8 copy-start.4
  401.0 27.0 %collective-permute-start.11 = (bf16[1024,512]{1,0:T(8,128)(2,1)}, bf16[1024,512]{1,0:T(8,128)(2,1)}, u32[]{:S(2)}, u32[]{:S(2)}) collective-permute-start(bf16[1024,512]{1,0:T(8,128)(2,1)} %get-tuple-element.96), channel_id=1, source_target_pairs={{0,1},{1,0},{2,3},{3,2},{4,5},{5,4},{6,7},{7,6},{8,9},{9,8},{10,11... | collective-permute-start | bytes 3145736 | tf_op jit(solution)/shard_map/ppermute | solution.py:1134
  401.7 17.2 %collective-permute-start.19 = (bf16[2,128,1024]{2,1,0:T(8,128)(2,1)S(1)}, bf16[2,128,1024]{2,1,0:T(8,128)(2,1)S(1)}, u32[]{:S(2)}, u32[]{:S(2)}) collective-permute-start(bf16[2,128,1024]{2,1,0:T(8,128)(2,1)S(1)} %fusion.7), channel_id=1, source_target_pairs={{0,8},{8,0},{1,9},{9,1},{2,10},{10,2},{3,11},{11,3},{4,12},{12,4},... | collective-permute-start | bytes 1572872 | tf_op jit(solution)/shard_map/ppermute | solution.py:1134
  406.8 4.7 copy-start.17
  411.5 12.0 %copy-start = (bf16[2048,512]{1,0:T(8,128)(2,1)S(1)}, bf16[2048,512]{1,0:T(8,128)(2,1)}, u32[]{:S(2)}) copy-start(bf16[2048,512]{1,0:T(8,128)(2,1)} %get-tuple-element.132) | copy-start | bytes 6291460
  419.9 77.8 %collective-permute-start.20 = (bf16[2,128,1024]{2,1,0:T(8,128)(2,1)}, bf16[2,128,1024]{2,1,0:T(8,128)(2,1)}, u32[]{:S(2)}, u32[]{:S(2)}) collective-permute-start(bf16[2,128,1024]{2,1,0:T(8,128)(2,1)} %add_convert_fusion.2), channel_id=1, source_target_pairs={{0,16},{16,0},{1,17},{17,1},{2,18},{18,2},{3,19},{19,3},{4,20},{20... | collective-permute-start | bytes 1572872 | tf_op jit(solution)/shard_map/ppermute | solution.py:1134
  484.1 48.9 %collective-permute-start.13 = (bf16[2,1024,512]{2,1,0:T(8,128)(2,1)}, bf16[2,1024,512]{2,1,0:T(8,128)(2,1)}, u32[]{:S(2)}, u32[]{:S(2)}) collective-permute-start(bf16[2,1024,512]{2,1,0:T(8,128)(2,1)} %get-tuple-element.102), channel_id=1, source_target_pairs={{0,1},{1,0},{2,3},{3,2},{4,5},{5,4},{6,7},{7,6},{8,9},{9,8},{10,11... | collective-permute-start | bytes 6291464 | tf_op jit(solution)/shard_map/ppermute | solution.py:1134
  491.6 28.4 %collective-permute-start.15 = (bf16[1024,512]{1,0:T(8,128)(2,1)}, bf16[1024,512]{1,0:T(8,128)(2,1)}, u32[]{:S(2)}, u32[]{:S(2)}) collective-permute-start(bf16[1024,512]{1,0:T(8,128)(2,1)} %constant_dynamic-slice_fusion.2), channel_id=1, source_target_pairs={{0,4},{4,0},{1,5},{5,1},{2,6},{6,2},{3,7},{7,3},{8,12},{12,8},{9,1... | collective-permute-start | bytes 3145736 | tf_op jit(solution)/shard_map/ppermute | solution.py:1134
  497.1 35.9 %collective-permute-start.12 = (bf16[1024,512]{1,0:T(8,128)(2,1)}, bf16[1024,512]{1,0:T(8,128)(2,1)}, u32[]{:S(2)}, u32[]{:S(2)}) collective-permute-start(bf16[1024,512]{1,0:T(8,128)(2,1)} %get-tuple-element.100), channel_id=1, source_target_pairs={{0,1},{1,0},{2,3},{3,2},{4,5},{5,4},{6,7},{7,6},{8,9},{9,8},{10,11... | collective-permute-start | bytes 3145736 | tf_op jit(solution)/shard_map/ppermute | solution.py:1134
  499.1 31.8 %collective-permute-start.21 = (bf16[2,128,1024]{2,1,0:T(8,128)(2,1)S(1)}, bf16[2,128,1024]{2,1,0:T(8,128)(2,1)S(1)}, u32[]{:S(2)}, u32[]{:S(2)}) collective-permute-start(bf16[2,128,1024]{2,1,0:T(8,128)(2,1)S(1)} %add_convert_fusion.1), channel_id=1, source_target_pairs={{0,4},{4,0},{1,5},{5,1},{2,6},{6,2},{3,7},{7,3},{8,12},{12,8},{9,1... | collective-permute-start | bytes 1572872 | tf_op jit(solution)/shard_map/ppermute | solution.py:1134
  499.2 1.5 copy-start.7
  499.2 1.5 copy-start.8
  522.6 56.7 %collective-permute-start.16 = (bf16[1024,512]{1,0:T(8,128)(2,1)}, bf16[1024,512]{1,0:T(8,128)(2,1)}, u32[]{:S(2)}, u32[]{:S(2)}) collective-permute-start(bf16[1024,512]{1,0:T(8,128)(2,1)} %broadcast_select_fusion.2), channel_id=1, source_target_pairs={{0,1},{1,0},{2,3},{3,2},{4,5},{5,4},{6,7},{7,6},{8,9},{9,8},{10,11... | collective-permute-start | bytes 3145736 | tf_op jit(solution)/shard_map/ppermute | solution.py:1134
  581.1 3.7 copy-start.1
Sparse Core Ops, SparseCore 0:
  56.4 19.6 all-gather.9
  77.6 19.1 all-gather.7
  98.4 21.6 all-gather.11
  121.5 16.8 all-gather.15
  139.8 16.8 all-gather.13
  158.1 19.4 all-gather.17
  179.2 47.0 all-gather.19
